TPU v7x, 32 devices: a whole 2x2x4 slice. The times are simulated.
32 devices in a mesh: rows: 8 (over y, x, core), section: 4 (over z).
Axes of the slice: x: 2, y: 2, z: 4, core: 2. Of those that a mesh axis runs over, the one named last changes fastest.
Arguments:
- x_blocks: bfloat16 [96, 4, 2, 128, 128], P('rows', 'section'), may hold values from -2 to 2
- x_cols: int32 [96, 4], P('rows', 'section'), may hold values from -1 to 23, as said below
- c_cols: int32 [96, 12], P('rows', 'section'), may hold values from 0 to 23, as said below
- c_keep: int32 [96, 12], P('rows', 'section'), may hold values 0 or 1
Outputs:
- squared: bfloat16 [96, 12, 2, 128, 128], P('rows', 'section')
Inputs may be any that keep to these rules, and one draw needn't show every extreme that they name: `x_cols`: for each block row and panel, the non-empty entries among its 1 slots name distinct columns of the panel; the share of empty slots differs from block row to block row. `c_cols`: for each block row and panel, its 3 entries name distinct columns of the panel.
All inputs are finite; a program needn't handle non-finite values. No bound on the sum of `c_keep` on one device may be relied on, other than what follows from the above.
Results may differ from a plain program's by a relative error of at most 0.001.
Values may be sent and summed in bfloat16 or wider, within the bound.
No kernel may reach another device: no remote copies, remote signals or barrier semaphores. Data moves between devices by JAX's collectives and lax.ppermute only.
A program may use at most 128 MiB of HBM per device.

v0:
```python
import jax
import jax.numpy as jnp
from jax import lax
from jax.sharding import PartitionSpec as P


def column_of(cols, per_panel, panel_width):
    slot_ids = jnp.arange(cols.shape[1], dtype=jnp.int32)
    return jnp.where(cols >= 0, (slot_ids // per_panel)[None, :] * panel_width + cols, -1)


def contribute(a_blocks, a_rows, b_blocks, b_cols, b_start, c_cols):
    row_count = b_blocks.shape[0]
    offset_rows = a_rows - b_start
    usable_row = (offset_rows >= 0) & (offset_rows < row_count)
    row_index = jnp.clip(offset_rows, 0, row_count - 1).astype(jnp.int32)
    chosen = jnp.where(
        usable_row[:, :, None, None, None, None], b_blocks[row_index], jnp.zeros((), jnp.bfloat16)
    )
    real_side = jnp.stack([chosen[:, :, :, 0], -chosen[:, :, :, 1]], axis=3)
    imag_side = jnp.stack([chosen[:, :, :, 1], chosen[:, :, :, 0]], axis=3)
    real_part = jnp.einsum(
        "iapxy,ialpyz->ialxz", a_blocks, real_side, preferred_element_type=jnp.float32
    )
    imag_part = jnp.einsum(
        "iapxy,ialpyz->ialxz", a_blocks, imag_side, preferred_element_type=jnp.float32
    )
    terms = jnp.stack([real_part, imag_part], axis=3)
    sel_cols = b_cols[row_index]
    matched = usable_row[:, :, None, None] & (sel_cols[:, :, :, None] == c_cols[:, None, None, :])
    return jnp.einsum(
        "ialc,ialrxz->icrxz", matched.astype(jnp.float32), terms, precision=lax.Precision.HIGHEST
    )


def on_device(x_blocks, x_cols, c_cols, c_keep):
    n_rows = lax.axis_size("rows")
    n_section = lax.axis_size("section")
    row_count = x_blocks.shape[0]
    per_panel = x_blocks.shape[1]
    panel_width = row_count * n_rows // n_section
    strip_blocks, strip_cols = (
        lax.all_gather(x_blocks, "section", axis=1, tiled=True),
        lax.all_gather(x_cols, "section", axis=1, tiled=True),
    )
    strip_rows = column_of(strip_cols, per_panel, panel_width)
    piece_blocks = lax.all_gather(x_blocks, "rows", axis=0, tiled=True)
    piece_cols = lax.all_gather(x_cols, "rows", axis=0, tiled=True)
    squared_sum = contribute(
        strip_blocks, strip_rows, piece_blocks, piece_cols, jnp.int32(0), c_cols
    )
    kept = c_keep.astype(jnp.float32)[:, :, None, None, None]
    return (squared_sum * kept).astype(jnp.bfloat16)


def solution(mesh):
    in_specs = (
        P("rows", "section", None, None, None),
        P("rows", "section"),
        P("rows", "section"),
        P("rows", "section"),
    )
    out_specs = P("rows", "section", None, None, None)
    return jax.shard_map(
        on_device, mesh=mesh, in_specs=in_specs, out_specs=out_specs, check_vma=False
    )
```

profile of v0, /device:TPU:0, one launch (start us, length us, event | category | flops | bytes accessed | tf_op | source)
XLA Modules:
  0.0 155.6 jit_solution(3955792724583778904)
XLA Ops:
  6.5 0.0 all-gather.4.cloned.1.call-start
  6.5 0.7 all-gather.4.cloned.1.call-update
  7.3 0.0 all-gather.6.cloned.1.call-start
  7.3 0.7 all-gather.6.cloned.1.call-update
  8.0 12.7 %all-gather = s32[4,1,12]{2,1,0:T(1,128)S(1)} all-gather(s32[1,1,12]{2,1,0:T(1,128)} %bitcast.51), channel_id=1, replica_groups=mesh['rows'=8,'section'=4] {'section'}, dimensions={0}, use_global_device_ids=true | all-gather | bytes 240 | tf_op jit(solution)/shard_map/all_gather | solution.py:44
  20.7 0.1 compare_select_fusion
  20.8 0.1 copy.22
  20.9 0.1 reshape.50
  21.0 0.1 and_bitcast_fusion
  21.1 0.1 copy.21
  21.2 1.2 dynamic-slice
  23.1 0.8 bitcast_dynamic-update-slice_fusion
  23.8 8.1 %all-reduce = s32[96]{0:T(128)S(1)} all-reduce(s32[96]{0:T(128)S(1)} %bitcast_dynamic-update-slice_fusion), channel_id=1, replica_groups=mesh['rows'=8,'section'=4] {'rows'}, use_global_device_ids=true, to_apply=%add | all-reduce | flops 96 | bytes 768 | tf_op jit(solution)/shard_map/all_gather | solution.py:48
  31.9 0.0 copy-start.2
  31.9 0.0 copy-start.1
  31.9 0.8 gather_fusion
  32.7 0.1 eq.18
  32.8 0.0 copy-done.2
  32.8 0.1 copy.27
  32.9 0.1 copy.23
  33.0 24.6 %all-gather.4.cloned.1.call-done = bf16[96,1,2,128,128]{4,3,2,1,0:T(8,128)(2,1)} async-done(((bf16[12,1,2,128,128]{4,3,2,1,0:T(8,128)(2,1)}), bf16[96,1,2,128,128]{4,3,2,1,0:T(8,128)(2,1)}) %all-gather.4.cloned.1.call-update) | async-done | bytes 6291472 | tf_op jit(solution)/shard_map/all_gather | solution.py:47
  57.6 3.9 %gather_fusion.1 = bf16[48,2,128,128]{3,2,1,0:T(8,128)(2,1)S(1)} fusion(bf16[96,2,128,128]{3,2,1,0:T(8,128)(2,1)} %bitcast.48, s32[1024]{0:T(1024)S(1)} %pad_clamp_fusion), kind=kCustom, calls=%fused_computation.1 | custom fusion | bytes 6291648 | tf_op jit(solution)/shard_map/gather | solution.py:18
  61.5 2.8 %copy.25 = bf16[48,2,128,128]{2,3,1,0:T(8,128)(2,1)} copy(bf16[48,2,128,128]{3,2,1,0:T(8,128)(2,1)S(1)} %gather_fusion.1) | data formatting | bytes 6291456 | tf_op jit(solution)/shard_map/gather | solution.py:18
  64.3 2.3 %broadcast_select_fusion = bf16[12,4,1,2,128,128]{4,5,3,1,0,2:T(8,128)(2,1)S(1)} fusion(bf16[12,4,1,2,128,128]{4,5,3,1,0,2:T(8,128)(2,1)} %bitcast.47, pred[12,4]{1,0:T(8,128)(4,1)S(1)} %copy.21), kind=kLoop, calls=%fused_computation.12 | loop fusion | flops 1572864 | bytes 6291504 | tf_op jit(solution)/shard_map/jit(_where)/select_n | solution.py:17
  66.7 1.5 slice_negate_fusion
  68.2 54.4 %all-gather.6.cloned.1.call-done = bf16[12,4,2,128,128]{4,3,2,1,0:T(8,128)(2,1)} async-done(((bf16[12,1,2,128,128]{4,3,2,1,0:T(8,128)(2,1)}), bf16[12,4,2,128,128]{4,3,2,1,0:T(8,128)(2,1)}) %all-gather.6.cloned.1.call-update) | async-done | bytes 3145744 | tf_op jit(solution)/shard_map/all_gather | solution.py:43
  122.7 3.5 %fusion.7 = f32[12,4,1,1,128,128]{4,5,1,0,3,2:T(8,128)S(1)} fusion(bf16[12,4,2,128,128]{4,3,2,1,0:T(8,128)(2,1)} %all-gather.6.cloned.1.call-done, bf16[12,4,1,1,128,128]{4,5,3,1,0,2:T(8,128)(2,1)} %get-tuple-element.5, bf16[12,4,1,1,128,128]{4,5,3,1,0,2:T(8,128)(2,1)S(1)} %get-tuple-element.7), kind=kOutput, calls=%fused_computation.14 | convolution fusion | flops 404226048 | bytes 9437184 | tf_op jit(solution)/shard_map/iapxy,ialpyz->ialxz/dot_general | solution.py:22
  126.2 1.0 fusion.6
  127.1 3.1 %maximum_bitcast_fusion = f32[12,4,2,128,128]{3,4,1,0,2:T(8,128)} fusion(f32[12,4,1,1,128,128]{4,5,1,0,3,2:T(8,128)S(1)} %fusion.6, f32[12,4,1,1,128,128]{4,5,1,0,3,2:T(8,128)S(1)} %fusion.7), kind=kLoop, calls=%fused_computation.2 | loop fusion | flops 1572864 | bytes 12582912 | tf_op jit(solution)/shard_map/reshape.9
  130.2 7.6 %copy.26 = f32[12,4,2,128,128]{4,1,3,2,0:T(4,128)} copy(f32[12,4,2,128,128]{3,4,1,0,2:T(8,128)} %maximum_bitcast_fusion) | data formatting | bytes 12582912 | tf_op jit(solution)/shard_map/reshape.9
  137.8 8.8 %multiply_convert_fusion = bf16[12,3,2,128,128]{4,1,3,2,0:T(4,128)(2,1)S(1)} fusion(f32[12,3]{1,0:T(8,128)S(1)} %copy.27, f32[12,4,2,128,128]{4,1,3,2,0:T(4,128)} %copy.26, s32[12,3]{1,0:T(8,128)S(1)} %copy.23, s32[12,4]{1,0:T(8,128)S(1)} %eq.18, pred[12,4]{1,0:T(8,128)(4,1)S(1)} %copy.21), kind=kOutput, calls=%fused_computation.3 | convolution fusion | flops 58982688 | bytes 8651280 | tf_op jit(solution)/shard_map/ialc,ialrxz->icrxz/dot_general | solution.py:31
  146.7 2.1 %copy.28 = bf16[12,3,2,128,128]{4,3,2,1,0:T(8,128)(2,1)} copy(bf16[12,3,2,128,128]{4,1,3,2,0:T(4,128)(2,1)S(1)} %multiply_convert_fusion) | data formatting | bytes 4718592 | tf_op jit(solution)/shard_map/convert_element_type | solution.py:53
  (7 shorter events, 0.0 us)
Async XLA Ops:
  6.5 51.0 %all-gather.4.cloned.1.call-start = ((), (), s32[]{:S(2)}) async-start(), calls=%async_computation | async-start | bytes 7077888 | tf_op jit(solution)/shard_map/all_gather | solution.py:47
  7.3 115.4 %all-gather.6.cloned.1.call-start = ((), (), s32[]{:S(2)}) async-start(), calls=%async_computation.1 | async-start | bytes 3932160 | tf_op jit(solution)/shard_map/all_gather | solution.py:43
  31.9 0.9 copy-start.2
  31.9 1.0 copy-start.1
  122.6 3.5 %copy-start = (bf16[12,4,2,128,128]{4,3,2,1,0:T(8,128)(2,1)S(1)}, bf16[12,4,2,128,128]{4,3,2,1,0:T(8,128)(2,1)}, u32[]{:S(2)}) copy-start(bf16[12,4,2,128,128]{4,3,2,1,0:T(8,128)(2,1)} %all-gather.6.cloned.1.call-done) | copy-start | bytes 9437188
Sparse Core Ops, SparseCore 0:
  9.2 48.2 all-gather.3
  59.2 63.4 all-gather.5
where the time goes:
time: 156 us
  waiting for transfers between devices  80.4 us (52%)
  blocking collectives  20.8 us (13%)
  local copies, waits for them, and re-layouts  19.8 us (13%)
  between operations  14.1 us (9%)
  matrix products  13.3 us (9%)
  other arithmetic  7.15 us (5%)
    all_gather x1, waiting for transfers between devices, on_device(): lax.all_gather(x_blocks, 'section', axis=1, tiled=True)  54.4 us
    all_gather x1, waiting for transfers between devices, on_device(): piece_blocks = lax.all_gather(x_blocks, 'rows', axis=0, tiled=True)  24.6 us
    all_gather x1, blocking collectives, on_device(): lax.all_gather(x_cols, 'section', axis=1, tiled=True)  12.7 us
    dot_general x1, matrix products, contribute(): jnp.einsum('ialc,ialrxz->icrxz', matched.astype(jnp.float32), terms, prec...  8.85 us
    all_gather x1, blocking collectives, on_device(): piece_cols = lax.all_gather(x_cols, 'rows', axis=0, tiled=True)  8.07 us
    another operation x1, local copies, waits for them, and re-layouts  7.6 us
    gather x2, local copies, waits for them, and re-layouts, contribute(): b_blocks[row_index]  6.73 us
    dot_general x1, matrix products, contribute(): jnp.einsum('iapxy,ialpyz->ialxz', a_blocks, real_side, preferred_element_...  3.49 us
  transfers between devices with their start and end apart: 2, of which 2 were waited for; matrix products, arithmetic and copies ran while one was open for 9% of the time, Pallas kernels for 0%

commit v1 on v0

v1 whole, which is shorter than its diff:
```python
import functools

import jax
import jax.numpy as jnp
from jax import lax
from jax.experimental import pallas as pl
from jax.experimental.pallas import tpu as pltpu
from jax.sharding import PartitionSpec as P

FIRST = ((0, 2), (2, 3), (3, 1), (1, 0))
SECOND = ((1, 3), (2, 0), (0, 1), (3, 2))
RELAY = ((2, 3), (1, 0))
MIDDLE = ((2, 1), (1, 2))
THIRD = ((0, 3), (3, 0), (1, 2), (2, 1))


def origin_of(section, *permutations):
    size = max(max(pair) for p in permutations for pair in p) + 1
    tables = [jnp.arange(size, dtype=jnp.int32)]
    for p in permutations:
        source = dict((dst, src) for src, dst in p)
        tables.append(jnp.array([source[d] for d in range(size)], jnp.int32))
    return jnp.stack(tables)[:, section]


def multiply_kernel(
    n_a, n_b, n_panels, per_panel, table, which, *refs
):
    a_bufs, b_bufs = refs[:n_a], refs[n_a : n_a + n_b]
    out, left, right, total, result, load_sem, store_sem = refs[n_a + n_b :]
    rows = out.shape[0]
    slots = n_panels * per_panel

    def fetch(index, carry):
        row, a = index // slots, index % slots

        @pl.when(table[0, row, a] >= 0)
        def _():
            for b in range(n_a):
                @pl.when(which[a // per_panel] == b)
                def _():
                    pltpu.make_async_copy(
                        a_bufs[b].at[row, a % per_panel], left.at[index], load_sem.at[index, 0]
                    ).start()
            for b in range(n_b):
                @pl.when(table[1, row, a] == b)
                def _():
                    pltpu.make_async_copy(
                        b_bufs[b].at[table[2, row, a], 0], right.at[index], load_sem.at[index, 1]
                    ).start()

        return carry

    lax.fori_loop(0, rows * slots, fetch, 0)

    def one_row(row, carry):
        total[...] = jnp.zeros_like(total)

        def one_term(a, inner):
            c = table[0, row, a]

            @pl.when(c >= 0)
            def _():
                index = row * slots + a
                for side, dst in ((0, left), (1, right)):
                    pltpu.make_async_copy(
                        dst.at[index], dst.at[index], load_sem.at[index, side]
                    ).wait()
                b_re, b_im = right[index, 0], right[index, 1]
                lhs = jnp.concatenate([left[index, 0], left[index, 1]], axis=1)
                rhs = jnp.concatenate(
                    [
                        jnp.concatenate([b_re, b_im], axis=1),
                        jnp.concatenate([-b_im, b_re], axis=1),
                    ],
                    axis=0,
                )
                total[c] += jnp.dot(lhs, rhs, preferred_element_type=jnp.float32)

            return inner

        lax.fori_loop(0, slots, one_term, 0)
        bs = result.shape[-1]
        for c in range(result.shape[1]):
            for part in range(2):
                result[row, c, part] = total[c, :, part * bs : (part + 1) * bs].astype(result.dtype)
        pltpu.make_async_copy(result.at[row], out.at[row], store_sem.at[row]).start()
        return carry

    lax.fori_loop(0, rows, one_row, 0)

    def drain(row, carry):
        pltpu.make_async_copy(result.at[row], out.at[row], store_sem.at[row]).wait()
        return carry

    lax.fori_loop(0, rows, drain, 0)


def multiply(table, which, a_bufs, b_bufs, out_shape, per_panel):
    rows, slots = table.shape[1:]
    results, bs = out_shape[1], out_shape[-1]
    n_panels = slots // per_panel
    smem = pl.BlockSpec(memory_space=pltpu.SMEM)
    hbm = pl.BlockSpec(memory_space=pl.ANY)
    return pl.pallas_call(
        functools.partial(
            multiply_kernel, len(a_bufs), len(b_bufs), n_panels, per_panel
        ),
        out_shape=jax.ShapeDtypeStruct(out_shape, jnp.bfloat16),
        in_specs=[smem, smem] + [hbm] * (len(a_bufs) + len(b_bufs)),
        out_specs=hbm,
        scratch_shapes=[
            pltpu.VMEM((rows * slots, 2, bs, bs), jnp.bfloat16),
            pltpu.VMEM((rows * slots, 2, bs, bs), jnp.bfloat16),
            pltpu.VMEM((results, bs, 2 * bs), jnp.float32),
            pltpu.VMEM((rows, results, 2, bs, bs), jnp.bfloat16),
            pltpu.SemaphoreType.DMA((rows * slots, 2)),
            pltpu.SemaphoreType.DMA((rows,)),
        ],
        compiler_params=pltpu.CompilerParams(vmem_limit_bytes=40 * 1024 * 1024),
        cost_estimate=pl.CostEstimate(
            flops=rows * slots * 16 * bs**3, bytes_accessed=16 * rows * slots * bs**2, transcendentals=0
        ),
    )(table, which, *a_bufs, *b_bufs)


def on_device(x_blocks, x_cols, c_cols, c_keep):
    n_rows = lax.axis_size("rows")
    n_section = lax.axis_size("section")
    me_row, me_section = lax.axis_index("rows"), lax.axis_index("section")
    row_count, per_panel, _, bs, _ = x_blocks.shape
    panel_width = row_count * n_rows // n_section
    send = lax.ppermute

    if (n_rows, n_section) == (8, 4):
        swap = lambda x, m: send(x, "rows", [(r, r ^ m) for r in range(n_rows)])
        first = send(x_blocks, "section", FIRST)
        second = send(x_blocks, "section", SECOND)
        along_x, along_y, across = (swap(x_blocks, m) for m in (2, 4, 6))
        middle = send(x_blocks, "section", MIDDLE)
        relayed = send(first, "section", RELAY)
        a_bufs = [x_blocks, first, second, relayed, middle]
        b_bufs = [
            x_blocks, swap(x_blocks, 1), along_x, swap(along_x, 1),
            along_y, swap(along_y, 1), across, swap(across, 1),
        ]
        origin = origin_of(me_section, FIRST, SECOND, THIRD)
        held = jnp.array([0, 1, 2, 3], jnp.int32)
        in_middle = (me_section == 1) | (me_section == 2)
        held = held + ((held == 3) & in_middle)
        which = jnp.sum(
            (origin[None, :] == jnp.arange(4)[:, None]) * held[None, :], axis=1, dtype=jnp.int32
        )
        strips = [x_cols] + [send(x_cols, "section", p) for p in (FIRST, SECOND, THIRD)]
        strip = jnp.stack(strips, axis=1)[:, :, :]
        order = (origin[None, :] == jnp.arange(4)[:, None]).astype(jnp.int32)
        strip = jnp.sum(order[None, :, :, None] * strip[:, None], axis=2).reshape(row_count, -1)
        pieces = x_cols[None]
        for m in (1, 2, 4):
            pieces = jnp.concatenate([pieces, swap(pieces, m)], axis=0)
        mine = lambda group: group ^ me_row
    else:
        shift = lambda x, axis, n, d: send(x, axis, [(p, (p + d) % n) for p in range(n)])
        a_bufs = [x_blocks] + [shift(x_blocks, "section", n_section, d) for d in range(1, n_section)]
        b_bufs = [x_blocks] + [shift(x_blocks, "rows", n_rows, d) for d in range(1, n_rows)]
        which = (me_section - jnp.arange(n_section, dtype=jnp.int32)) % n_section
        strip = lax.all_gather(x_cols, "section", axis=1, tiled=True)
        pieces = jnp.stack([x_cols] + [shift(x_cols, "rows", n_rows, d) for d in range(1, n_rows)])
        mine = lambda group: (me_row - group) % n_rows

    panels = jnp.arange(strip.shape[1], dtype=jnp.int32) // per_panel
    far = jnp.where(strip >= 0, panels[None, :] * panel_width + strip, -1)
    buffer = mine(far // row_count)
    inside = far % row_count
    place = jnp.where(far >= 0, buffer * row_count + inside, -1)
    listed = pieces.reshape(-1)
    hit = place[:, :, None] == jnp.arange(listed.shape[0], dtype=jnp.int32)
    column = jnp.sum(jnp.where(hit, listed + 1, 0), axis=2) - 1
    wanted = jnp.where(c_keep > 0, c_cols, -2)
    match = column[:, :, None] == wanted[:, None, :]
    slot_ids = jnp.arange(wanted.shape[1], dtype=jnp.int32)
    target = jnp.sum(jnp.where(match, slot_ids + 1, 0), axis=2) - 1
    table = jnp.stack([target, buffer, inside]).astype(jnp.int32)
    out_shape = (row_count, c_cols.shape[1], 2, bs, bs)
    return multiply(table, which.astype(jnp.int32), a_bufs, b_bufs, out_shape, per_panel)


def solution(mesh):
    in_specs = (
        P("rows", "section", None, None, None),
        P("rows", "section"),
        P("rows", "section"),
        P("rows", "section"),
    )
    out_specs = P("rows", "section", None, None, None)
    return jax.shard_map(
        on_device, mesh=mesh, in_specs=in_specs, out_specs=out_specs, check_vma=False
    )
```

time: 156 us -> 101 us (0.65)
  blocking collectives: 20.8 us -> 0 us
  starting transfers between devices: 0.04 us -> 17.9 us
  local copies, waits for them, and re-layouts: 19.8 us -> 2.2 us
  waiting for transfers between devices: 80.4 us -> 65.5 us
  between operations: 14.1 us -> 0.07 us
  matrix products: 13.3 us -> 0 us
  Pallas kernels: 0 us -> 10.5 us
  other arithmetic: 7.15 us -> 4.2 us
    all_gather x2 -> x0, waiting for transfers between devices: 79 us -> none  [the longest x1 54.4 us: on_device(): lax.all_gather(x_blocks, 'section', axis=1, tiled=True)]
    ppermute x0 -> x17, waiting for transfers between devices: none -> 65.5 us  [the longest x1 20.1 us: on_device(): second = send(x_blocks, 'section', SECOND)]
    all_gather x2 -> x0, blocking collectives: 20.8 us -> none  [the longest x1 12.7 us: on_device(): lax.all_gather(x_cols, 'section', axis=1, tiled=True)]
    ppermute x0 -> x17, starting transfers between devices: none -> 17.9 us  [the longest x3 7.97 us: on_device(): send(x_cols, 'section', p)]
    dot_general x3 -> x0, matrix products: 13.3 us -> none  [the longest x1 8.85 us: contribute(): jnp.einsum('ialc,ialrxz->icrxz', matched.astype(jnp.float32), terms, prec...]
    pallas_call x0 -> x1, Pallas kernels: none -> 10.5 us  [multiply(): pl.pallas_call(functools.partial(multiply_kernel, len(a_bufs), len(b_bufs...]
    gather x3 -> x0, local copies, waits for them, and re-layouts: 7.51 us -> none  [the longest x2 6.73 us: contribute(): b_blocks[row_index]]
    another operation x1, local copies, waits for them, and re-layouts: 7.6 us -> 0.11 us  [on_device(): table = jnp.stack([target, buffer, inside]).astype(jnp.int32)]
  transfers between devices with their start and end apart: 2 -> 17, of which waited for: 2 -> 7; matrix products, arithmetic and copies ran while one was open for 9% -> 5% of each run, Pallas kernels for 0% -> 0%
where the time goes in v1:
time: 101 us; the launch traced here: 100 us
  waiting for transfers between devices  65.5 us (65%)
  starting transfers between devices  17.9 us (18%)
  Pallas kernels  10.5 us (10%)
  other arithmetic  4.2 us (4%)
  local copies, waits for them, and re-layouts  2.2 us (2%)
    ppermute x1, waiting for transfers between devices, on_device(): second = send(x_blocks, 'section', SECOND)  20.1 us
    ppermute x10, waiting for transfers between devices, on_device(): swap = lambda x, m: send(x, 'rows', [(r, r ^ m) for r in range(n_rows)])  17.4 us
    ppermute x1, waiting for transfers between devices, on_device(): relayed = send(first, 'section', RELAY)  16.7 us
    ppermute x1, waiting for transfers between devices, on_device(): first = send(x_blocks, 'section', FIRST)  11.2 us
    pallas_call x1, Pallas kernels, multiply(): pl.pallas_call(functools.partial(multiply_kernel, len(a_bufs), len(b_bufs...  10.5 us
    ppermute x3, starting transfers between devices, on_device(): send(x_cols, 'section', p)  7.97 us
    ppermute x10, starting transfers between devices, on_device(): swap = lambda x, m: send(x, 'rows', [(r, r ^ m) for r in range(n_rows)])  7.96 us
  transfers between devices with their start and end apart: 17, of which 7 were waited for; matrix products, arithmetic and copies ran while one was open for 5% of the time, Pallas kernels for 0%

profile of v1, /device:TPU:0, one launch (start us, length us, event | category | flops | bytes accessed | tf_op | source)
XLA Modules:
  0.0 100.4 jit_solution(258851731795644723)
XLA Ops:
  0.0 3.0 %collective-permute-start.1 = (s32[12,1]{0,1:T(1,128)}, s32[12,1]{0,1:T(1,128)S(1)}, u32[]{:S(2)}, u32[]{:S(2)}) collective-permute-start(s32[12,1]{0,1:T(1,128)} %param.9), channel_id=1, source_target_pairs={{1,3},{2,0},{0,1},{3,2},{5,7},{6,4},{4,5},{7,6},{9,11},{10,8},{8,9... | collective-permute-start | bytes 152 | tf_op jit(solution)/shard_map/ppermute | solution.py:154
  3.0 1.0 %collective-permute-start = (s32[12,1]{0,1:T(1,128)}, s32[12,1]{0,1:T(1,128)S(1)}, u32[]{:S(2)}, u32[]{:S(2)}) collective-permute-start(s32[12,1]{0,1:T(1,128)} %param.9), channel_id=1, source_target_pairs={{0,2},{2,3},{3,1},{1,0},{4,6},{6,7},{7,5},{5,4},{8,10},{10,11},{11... | collective-permute-start | bytes 152 | tf_op jit(solution)/shard_map/ppermute | solution.py:154
  4.0 3.9 %collective-permute-start.2 = (s32[12,1]{0,1:T(1,128)}, s32[12,1]{0,1:T(1,128)S(1)}, u32[]{:S(2)}, u32[]{:S(2)}) collective-permute-start(s32[12,1]{0,1:T(1,128)} %param.9), channel_id=1, source_target_pairs={{0,3},{3,0},{1,2},{2,1},{4,7},{7,4},{5,6},{6,5},{8,11},{11,8},{9,1... | collective-permute-start | bytes 152 | tf_op jit(solution)/shard_map/ppermute | solution.py:154
  8.0 1.5 %collective-permute-start.13 = (bf16[12,1,2,128,128]{4,3,2,1,0:T(8,128)(2,1)}, bf16[12,1,2,128,128]{4,3,2,1,0:T(8,128)(2,1)S(1)}, u32[]{:S(2)}, u32[]{:S(2)}) collective-permute-start(bf16[12,1,2,128,128]{4,3,2,1,0:T(8,128)(2,1)} %refs_5_.1), channel_id=1, source_target_pairs={{0,16},{4,20},{8,24},{12,28},{16,0},{20,4},{24,8},{28,12},{1,17},{... | collective-permute-start | bytes 2359304 | tf_op jit(solution)/shard_map/ppermute | solution.py:136
  9.5 0.7 dynamic-slice_bitcast_fusion
  10.2 0.1 select_reduce_fusion.2.which
  10.3 0.7 compare_select_fusion
  11.0 0.7 pad_add_fusion.3
  11.7 1.5 %collective-permute-start.4 = (s32[2,12,1]{1,2,0:T(1,128)S(1)}, s32[2,12,1]{1,2,0:T(1,128)S(1)}, u32[]{:S(2)}, u32[]{:S(2)}) collective-permute-start(s32[2,12,1]{1,2,0:T(1,128)S(1)} %pad_add_fusion.3), channel_id=1, source_target_pairs={{0,8},{4,12},{8,0},{12,4},{16,24},{20,28},{24,16},{28,20},{1,9},{5... | collective-permute-start | bytes 296 | tf_op jit(solution)/shard_map/ppermute | solution.py:136
  13.2 2.1 %collective-permute-done.4 = s32[2,12,1]{1,2,0:T(1,128)S(1)} collective-permute-done((s32[2,12,1]{1,2,0:T(1,128)S(1)}, s32[2,12,1]{1,2,0:T(1,128)S(1)}, u32[]{:S(2)}, u32[]{:S(2)}) %collective-permute-start.4) | collective-permute-done | bytes 128 | tf_op jit(solution)/shard_map/ppermute | solution.py:136
  15.3 1.5 %collective-permute-start.11 = (bf16[12,1,2,128,128]{4,3,2,1,0:T(8,128)(2,1)}, bf16[12,1,2,128,128]{4,3,2,1,0:T(8,128)(2,1)S(1)}, u32[]{:S(2)}, u32[]{:S(2)}) collective-permute-start(bf16[12,1,2,128,128]{4,3,2,1,0:T(8,128)(2,1)} %refs_5_.1), channel_id=1, source_target_pairs={{0,8},{4,12},{8,0},{12,4},{16,24},{20,28},{24,16},{28,20},{1,9},{5... | collective-permute-start | bytes 2359304 | tf_op jit(solution)/shard_map/ppermute | solution.py:136
  16.7 0.7 pad_add_fusion.2
  17.4 0.5 collective-permute-start.5
  17.9 0.7 collective-permute-start.9
  18.6 9.5 %collective-permute-done.5 = s32[4,12,1]{1,2,0:T(1,128)S(1)} collective-permute-done((s32[4,12,1]{1,2,0:T(1,128)S(1)}, s32[4,12,1]{1,2,0:T(1,128)S(1)}, u32[]{:S(2)}, u32[]{:S(2)}) %collective-permute-start.5) | collective-permute-done | bytes 224 | tf_op jit(solution)/shard_map/ppermute | solution.py:136
  28.2 2.4 %collective-permute-start.15 = (bf16[12,1,2,128,128]{4,3,2,1,0:T(8,128)(2,1)}, bf16[12,1,2,128,128]{4,3,2,1,0:T(8,128)(2,1)}, u32[]{:S(2)}, u32[]{:S(2)}) collective-permute-start(bf16[12,1,2,128,128]{4,3,2,1,0:T(8,128)(2,1)} %refs_5_.1), channel_id=1, source_target_pairs={{0,24},{4,28},{8,16},{12,20},{16,8},{20,12},{24,0},{28,4},{1,25},{... | collective-permute-start | bytes 2359304 | tf_op jit(solution)/shard_map/ppermute | solution.py:136
  30.6 0.7 pad_add_fusion.1
  31.3 0.1 multiply_reduce_fusion
  31.5 0.1 copy.21
  31.7 0.7 fusion
  32.4 3.5 %collective-permute-done.11.refs_7_ = bf16[12,1,2,128,128]{4,3,2,1,0:T(8,128)(2,1)S(1)} collective-permute-done((bf16[12,1,2,128,128]{4,3,2,1,0:T(8,128)(2,1)}, bf16[12,1,2,128,128]{4,3,2,1,0:T(8,128)(2,1)S(1)}, u32[]{:S(2)}, u32[]{:S(2)}) %collective-permute-start.11) | collective-permute-done | bytes 786464 | tf_op jit(solution)/shard_map/ppermute | solution.py:136
  36.0 0.5 collective-permute-start.12
  36.5 11.2 %collective-permute-done.6.refs_1_ = bf16[12,1,2,128,128]{4,3,2,1,0:T(8,128)(2,1)} collective-permute-done((bf16[12,1,2,128,128]{4,3,2,1,0:T(8,128)(2,1)}, bf16[12,1,2,128,128]{4,3,2,1,0:T(8,128)(2,1)}, u32[]{:S(2)}, u32[]{:S(2)}) %collective-permute-start.6) | collective-permute-done | bytes 786464 | tf_op jit(solution)/shard_map/ppermute | solution.py:137
  47.7 1.3 %collective-permute-start.8 = (bf16[12,1,2,128,128]{4,3,2,1,0:T(8,128)(2,1)}, bf16[12,1,2,128,128]{4,3,2,1,0:T(8,128)(2,1)}, u32[]{:S(2)}, u32[]{:S(2)}) collective-permute-start(bf16[12,1,2,128,128]{4,3,2,1,0:T(8,128)(2,1)} %collective-permute-done.6.refs_1_), channel_id=1, source_target_pairs={{2,3},{1,0},{6,7},{5,4},{10,11},{9,8},{14,15},{13,12},{18,19},{17,... | collective-permute-start | bytes 2359304 | tf_op jit(solution)/shard_map/ppermute | solution.py:141
  49.0 2.2 %collective-permute-done.15.refs_11_ = bf16[12,1,2,128,128]{4,3,2,1,0:T(8,128)(2,1)} collective-permute-done((bf16[12,1,2,128,128]{4,3,2,1,0:T(8,128)(2,1)}, bf16[12,1,2,128,128]{4,3,2,1,0:T(8,128)(2,1)}, u32[]{:S(2)}, u32[]{:S(2)}) %collective-permute-start.15) | collective-permute-done | bytes 786464 | tf_op jit(solution)/shard_map/ppermute | solution.py:136
  51.2 0.3 select_reduce_fusion
  51.5 0.1 copy.22
  51.7 0.1 copy.23.table
  51.8 20.1 %collective-permute-done.7.refs_2_ = bf16[12,1,2,128,128]{4,3,2,1,0:T(8,128)(2,1)} collective-permute-done((bf16[12,1,2,128,128]{4,3,2,1,0:T(8,128)(2,1)}, bf16[12,1,2,128,128]{4,3,2,1,0:T(8,128)(2,1)}, u32[]{:S(2)}, u32[]{:S(2)}) %collective-permute-start.7) | collective-permute-done | bytes 786464 | tf_op jit(solution)/shard_map/ppermute | solution.py:138
  72.0 16.7 %collective-permute-done.8.refs_3_ = bf16[12,1,2,128,128]{4,3,2,1,0:T(8,128)(2,1)} collective-permute-done((bf16[12,1,2,128,128]{4,3,2,1,0:T(8,128)(2,1)}, bf16[12,1,2,128,128]{4,3,2,1,0:T(8,128)(2,1)}, u32[]{:S(2)}, u32[]{:S(2)}) %collective-permute-start.8) | collective-permute-done | bytes 786464 | tf_op jit(solution)/shard_map/ppermute | solution.py:141
  88.7 1.1 %copy-done = bf16[12,1,2,128,128]{4,3,2,1,0:T(8,128)(2,1)S(1)} copy-done((bf16[12,1,2,128,128]{4,3,2,1,0:T(8,128)(2,1)S(1)}, bf16[12,1,2,128,128]{4,3,2,1,0:T(8,128)(2,1)}, u32[]{:S(2)}) %copy-start) | copy-done | bytes 786456
  89.9 10.5 %shard_map.82 = bf16[12,3,2,128,128]{4,3,2,1,0:T(8,128)(2,1)} custom-call(s32[3,12,4]{2,1,0:T(8,128)S(1)} %copy.23.table, s32[4]{0:T(128)S(1)} %select_reduce_fusion.2.which, bf16[12,1,2,128,128]{4,3,2,1,0:T(8,128)(2,1)S(1)} %copy-done, bf16[12,1,2,128,128]{4,3,2,1,0:T(8,128)(2,1)} %collective-permute-done.6.refs_1_, ...), custom_call_target="tpu_custom_call" | custom-call | flops 1610612736 | bytes 12582912 | tf_op jit(solution)/shard_map/pallas_call | solution.py:105
  (28 shorter events, 0.4 us)
Async XLA Ops:
  0.0 17.4 %collective-permute-start.1 = (s32[12,1]{0,1:T(1,128)}, s32[12,1]{0,1:T(1,128)S(1)}, u32[]{:S(2)}, u32[]{:S(2)}) collective-permute-start(s32[12,1]{0,1:T(1,128)} %param.9), channel_id=1, source_target_pairs={{1,3},{2,0},{0,1},{3,2},{5,7},{6,4},{4,5},{7,6},{9,11},{10,8},{8,9... | collective-permute-start | bytes 152 | tf_op jit(solution)/shard_map/ppermute | solution.py:154
  3.0 14.9 %collective-permute-start = (s32[12,1]{0,1:T(1,128)}, s32[12,1]{0,1:T(1,128)S(1)}, u32[]{:S(2)}, u32[]{:S(2)}) collective-permute-start(s32[12,1]{0,1:T(1,128)} %param.9), channel_id=1, source_target_pairs={{0,2},{2,3},{3,1},{1,0},{4,6},{6,7},{7,5},{5,4},{8,10},{10,11},{11... | collective-permute-start | bytes 152 | tf_op jit(solution)/shard_map/ppermute | solution.py:154
  4.0 13.9 %collective-permute-start.2 = (s32[12,1]{0,1:T(1,128)}, s32[12,1]{0,1:T(1,128)S(1)}, u32[]{:S(2)}, u32[]{:S(2)}) collective-permute-start(s32[12,1]{0,1:T(1,128)} %param.9), channel_id=1, source_target_pairs={{0,3},{3,0},{1,2},{2,1},{4,7},{7,4},{5,6},{6,5},{8,11},{11,8},{9,1... | collective-permute-start | bytes 152 | tf_op jit(solution)/shard_map/ppermute | solution.py:154
  8.0 3.0 %collective-permute-start.3 = (s32[1,12,1]{1,2,0:T(1,128)}, s32[1,12,1]{1,2,0:T(1,128)S(1)}, u32[]{:S(2)}, u32[]{:S(2)}) collective-permute-start(s32[1,12,1]{1,2,0:T(1,128)} %bitcast.22), channel_id=1, source_target_pairs={{0,4},{4,0},{8,12},{12,8},{16,20},{20,16},{24,28},{28,24},{1,5},{5... | collective-permute-start | bytes 152 | tf_op jit(solution)/shard_map/ppermute | solution.py:136
  8.0 20.2 %collective-permute-start.13 = (bf16[12,1,2,128,128]{4,3,2,1,0:T(8,128)(2,1)}, bf16[12,1,2,128,128]{4,3,2,1,0:T(8,128)(2,1)S(1)}, u32[]{:S(2)}, u32[]{:S(2)}) collective-permute-start(bf16[12,1,2,128,128]{4,3,2,1,0:T(8,128)(2,1)} %refs_5_.1), channel_id=1, source_target_pairs={{0,16},{4,20},{8,24},{12,28},{16,0},{20,4},{24,8},{28,12},{1,17},{... | collective-permute-start | bytes 2359304 | tf_op jit(solution)/shard_map/ppermute | solution.py:136
  11.7 3.6 %collective-permute-start.4 = (s32[2,12,1]{1,2,0:T(1,128)S(1)}, s32[2,12,1]{1,2,0:T(1,128)S(1)}, u32[]{:S(2)}, u32[]{:S(2)}) collective-permute-start(s32[2,12,1]{1,2,0:T(1,128)S(1)} %pad_add_fusion.3), channel_id=1, source_target_pairs={{0,8},{4,12},{8,0},{12,4},{16,24},{20,28},{24,16},{28,20},{1,9},{5... | collective-permute-start | bytes 296 | tf_op jit(solution)/shard_map/ppermute | solution.py:136
  15.3 20.7 %collective-permute-start.11 = (bf16[12,1,2,128,128]{4,3,2,1,0:T(8,128)(2,1)}, bf16[12,1,2,128,128]{4,3,2,1,0:T(8,128)(2,1)S(1)}, u32[]{:S(2)}, u32[]{:S(2)}) collective-permute-start(bf16[12,1,2,128,128]{4,3,2,1,0:T(8,128)(2,1)} %refs_5_.1), channel_id=1, source_target_pairs={{0,8},{4,12},{8,0},{12,4},{16,24},{20,28},{24,16},{28,20},{1,9},{5... | collective-permute-start | bytes 2359304 | tf_op jit(solution)/shard_map/ppermute | solution.py:136
  17.4 10.8 %collective-permute-start.5 = (s32[4,12,1]{1,2,0:T(1,128)S(1)}, s32[4,12,1]{1,2,0:T(1,128)S(1)}, u32[]{:S(2)}, u32[]{:S(2)}) collective-permute-start(s32[4,12,1]{1,2,0:T(1,128)S(1)} %pad_add_fusion.2), channel_id=1, source_target_pairs={{0,16},{4,20},{8,24},{12,28},{16,0},{20,4},{24,8},{28,12},{1,17},{... | collective-permute-start | bytes 584 | tf_op jit(solution)/shard_map/ppermute | solution.py:136
  17.9 18.0 %collective-permute-start.10 = (bf16[12,1,2,128,128]{4,3,2,1,0:T(8,128)(2,1)}, bf16[12,1,2,128,128]{4,3,2,1,0:T(8,128)(2,1)S(1)}, u32[]{:S(2)}, u32[]{:S(2)}) collective-permute-start(bf16[12,1,2,128,128]{4,3,2,1,0:T(8,128)(2,1)} %refs_5_.1), channel_id=1, source_target_pairs={{0,4},{4,0},{8,12},{12,8},{16,20},{20,16},{24,28},{28,24},{1,5},{5... | collective-permute-start | bytes 2359304 | tf_op jit(solution)/shard_map/ppermute | solution.py:136
  17.9 18.0 %collective-permute-start.9 = (bf16[12,1,2,128,128]{4,3,2,1,0:T(8,128)(2,1)}, bf16[12,1,2,128,128]{4,3,2,1,0:T(8,128)(2,1)S(1)}, u32[]{:S(2)}, u32[]{:S(2)}) collective-permute-start(bf16[12,1,2,128,128]{4,3,2,1,0:T(8,128)(2,1)} %refs_5_.1), channel_id=1, source_target_pairs={{2,1},{1,2},{6,5},{5,6},{10,9},{9,10},{14,13},{13,14},{18,17},{17,... | collective-permute-start | bytes 2359304 | tf_op jit(solution)/shard_map/ppermute | solution.py:140
  28.2 19.5 %collective-permute-start.6 = (bf16[12,1,2,128,128]{4,3,2,1,0:T(8,128)(2,1)}, bf16[12,1,2,128,128]{4,3,2,1,0:T(8,128)(2,1)}, u32[]{:S(2)}, u32[]{:S(2)}) collective-permute-start(bf16[12,1,2,128,128]{4,3,2,1,0:T(8,128)(2,1)} %refs_5_.1), channel_id=1, source_target_pairs={{0,2},{2,3},{3,1},{1,0},{4,6},{6,7},{7,5},{5,4},{8,10},{10,11},{11... | collective-permute-start | bytes 2359304 | tf_op jit(solution)/shard_map/ppermute | solution.py:137
  28.2 23.0 %collective-permute-start.15 = (bf16[12,1,2,128,128]{4,3,2,1,0:T(8,128)(2,1)}, bf16[12,1,2,128,128]{4,3,2,1,0:T(8,128)(2,1)}, u32[]{:S(2)}, u32[]{:S(2)}) collective-permute-start(bf16[12,1,2,128,128]{4,3,2,1,0:T(8,128)(2,1)} %refs_5_.1), channel_id=1, source_target_pairs={{0,24},{4,28},{8,16},{12,20},{16,8},{20,12},{24,0},{28,4},{1,25},{... | collective-permute-start | bytes 2359304 | tf_op jit(solution)/shard_map/ppermute | solution.py:136
  35.9 36.0 %collective-permute-start.7 = (bf16[12,1,2,128,128]{4,3,2,1,0:T(8,128)(2,1)}, bf16[12,1,2,128,128]{4,3,2,1,0:T(8,128)(2,1)}, u32[]{:S(2)}, u32[]{:S(2)}) collective-permute-start(bf16[12,1,2,128,128]{4,3,2,1,0:T(8,128)(2,1)} %refs_5_.1), channel_id=1, source_target_pairs={{1,3},{2,0},{0,1},{3,2},{5,7},{6,4},{4,5},{7,6},{9,11},{10,8},{8,9... | collective-permute-start | bytes 2359304 | tf_op jit(solution)/shard_map/ppermute | solution.py:138
  36.0 36.0 %collective-permute-start.14 = (bf16[12,1,2,128,128]{4,3,2,1,0:T(8,128)(2,1)S(1)}, bf16[12,1,2,128,128]{4,3,2,1,0:T(8,128)(2,1)}, u32[]{:S(2)}, u32[]{:S(2)}) collective-permute-start(bf16[12,1,2,128,128]{4,3,2,1,0:T(8,128)(2,1)S(1)} %collective-permute-done.13.refs_9_), channel_id=1, source_target_pairs={{0,4},{4,0},{8,12},{12,8},{16,20},{20,16},{24,28},{28,24},{1,5},{5... | collective-permute-start | bytes 2359304 | tf_op jit(solution)/shard_map/ppermute | solution.py:136
  36.0 36.0 %collective-permute-start.12 = (bf16[12,1,2,128,128]{4,3,2,1,0:T(8,128)(2,1)S(1)}, bf16[12,1,2,128,128]{4,3,2,1,0:T(8,128)(2,1)}, u32[]{:S(2)}, u32[]{:S(2)}) collective-permute-start(bf16[12,1,2,128,128]{4,3,2,1,0:T(8,128)(2,1)S(1)} %collective-permute-done.11.refs_7_), channel_id=1, source_target_pairs={{0,4},{4,0},{8,12},{12,8},{16,20},{20,16},{24,28},{28,24},{1,5},{5... | collective-permute-start | bytes 2359304 | tf_op jit(solution)/shard_map/ppermute | solution.py:136
  47.7 41.1 %collective-permute-start.8 = (bf16[12,1,2,128,128]{4,3,2,1,0:T(8,128)(2,1)}, bf16[12,1,2,128,128]{4,3,2,1,0:T(8,128)(2,1)}, u32[]{:S(2)}, u32[]{:S(2)}) collective-permute-start(bf16[12,1,2,128,128]{4,3,2,1,0:T(8,128)(2,1)} %collective-permute-done.6.refs_1_), channel_id=1, source_target_pairs={{2,3},{1,0},{6,7},{5,4},{10,11},{9,8},{14,15},{13,12},{18,19},{17,... | collective-permute-start | bytes 2359304 | tf_op jit(solution)/shard_map/ppermute | solution.py:141
  51.2 37.5 %collective-permute-start.16 = (bf16[12,1,2,128,128]{4,3,2,1,0:T(8,128)(2,1)}, bf16[12,1,2,128,128]{4,3,2,1,0:T(8,128)(2,1)}, u32[]{:S(2)}, u32[]{:S(2)}) collective-permute-start(bf16[12,1,2,128,128]{4,3,2,1,0:T(8,128)(2,1)} %collective-permute-done.15.refs_11_), channel_id=1, source_target_pairs={{0,4},{4,0},{8,12},{12,8},{16,20},{20,16},{24,28},{28,24},{1,5},{5... | collective-permute-start | bytes 2359304 | tf_op jit(solution)/shard_map/ppermute | solution.py:136
  88.7 1.1 %copy-start = (bf16[12,1,2,128,128]{4,3,2,1,0:T(8,128)(2,1)S(1)}, bf16[12,1,2,128,128]{4,3,2,1,0:T(8,128)(2,1)}, u32[]{:S(2)}) copy-start(bf16[12,1,2,128,128]{4,3,2,1,0:T(8,128)(2,1)} %refs_5_.1) | copy-start | bytes 2359300

commit v2 on v0

v2 whole, which is shorter than its diff:
```python
import functools

import jax
import jax.numpy as jnp
import numpy as np
from jax import lax
from jax.experimental import pallas as pl
from jax.experimental.pallas import tpu as pltpu
from jax.sharding import PartitionSpec as P

RING = (0, 2, 3, 1)
SMEM = pl.BlockSpec(memory_space=pltpu.SMEM)
HBM = pl.BlockSpec(memory_space=pl.ANY)
VMEM = pl.BlockSpec(memory_space=pltpu.VMEM)
LEFT_BUF, LEFT_ROW, RIGHT_BUF, RIGHT_ROW, RESULT, OPENS, CLOSES = range(7)
FIELDS = 7
UNROLL = 4


def plan_kernel(
    sizes, lookup, strip, pieces, c_cols, c_keep, count, terms, empty, column, right_buf, right_row
):
    rows, n_section, n_rows, panel_width, n_early, half = sizes
    left_table = lambda field, a: lookup[field * n_section + a]
    right_table = lambda field, g: lookup[4 * n_section + field * n_rows + g]
    results = c_cols.shape[1]
    count[0] = 0
    count[1] = 0

    def one_row(i, carry):
        in_upper = i >= half
        lefts = [left_table(jnp.where(in_upper, 1, 0), a) for a in range(n_section)]
        left_rows = [i - jnp.where(in_upper, left_table(2, a), 0) for a in range(n_section)]
        for a in range(n_section):
            col = strip[left_table(3, a), i]
            k = jnp.maximum(a * panel_width + col, 0)
            group = k // rows
            inside = k - group * rows
            far = pieces[right_table(3, group), inside]
            column[a] = jnp.where(col >= 0, far, -1)
            upper = inside >= half
            right_buf[a] = right_table(jnp.where(upper, 1, 0), group)
            right_row[a] = inside - jnp.where(upper, right_table(2, group), 0)
        for c in range(results):
            wanted = jnp.where(c_keep[i, c] > 0, c_cols[i, c], -2)
            matches = [(column[a] == wanted).astype(jnp.int32) for a in range(n_section)]
            late = functools.reduce(
                jnp.maximum,
                [m * (lefts[a] >= n_early).astype(jnp.int32) for a, m in enumerate(matches)],
            )
            n_matches = sum(matches)
            empty[i * results + c] = (n_matches == 0).astype(jnp.int32)
            base = count[late]
            seen = jnp.int32(0)
            for a in range(n_section):
                at = base + seen

                @pl.when(matches[a] > 0)
                def _(a=a, at=at, seen=seen):
                    entry = (
                        lefts[a], left_rows[a], right_buf[a], right_row[a], i * results + c,
                        (seen == 0).astype(jnp.int32), (seen == n_matches - 1).astype(jnp.int32),
                    )
                    for f, value in enumerate(entry):
                        terms[late, f, at] = value

                seen = seen + matches[a]
            count[late] = base + n_matches
        return carry

    lax.fori_loop(0, rows, one_row, 0)


def plan(sizes, lookup, strip, pieces, c_cols, c_keep):
    rows, n_section = sizes[:2]
    most = rows * n_section
    return pl.pallas_call(
        functools.partial(plan_kernel, sizes),
        out_shape=(
            jax.ShapeDtypeStruct((2,), jnp.int32),
            jax.ShapeDtypeStruct((2, FIELDS, most), jnp.int32),
            jax.ShapeDtypeStruct((c_cols.size,), jnp.int32),
        ),
        in_specs=[SMEM] * 5,
        out_specs=(SMEM,) * 3,
        scratch_shapes=[pltpu.SMEM((n_section,), jnp.int32)] * 3,
    )(lookup, strip, pieces, c_cols, c_keep)


def multiply_kernel(n_a, n_b, phase, count, terms, empty, *refs):
    a_bufs, b_bufs = refs[:n_a], refs[n_a : n_a + n_b]
    refs = refs[n_a + n_b + (1 if phase else 0) :]
    out, left, right, total, result, zeros, load_sem, store_sem = refs
    results, bs = out.shape[1], out.shape[-1]
    n_terms = count[phase]

    def load(t, side):
        dst = (left, right)[side].at[t]
        return pltpu.make_async_copy(dst, dst, load_sem.at[t, side])

    def store(source, r):
        return pltpu.make_async_copy(source, out.at[r // results, r % results], store_sem.at[r])

    def fetch(t, carry):
        sides = ((a_bufs, LEFT_BUF, LEFT_ROW, left), (b_bufs, RIGHT_BUF, RIGHT_ROW, right))
        for side, (bufs, which, row, dst) in enumerate(sides):
            for b, buf in enumerate(bufs):
                @pl.when(terms[phase, which, t] == b)
                def _():
                    pltpu.make_async_copy(
                        buf.at[pl.ds(pl.multiple_of(terms[phase, row, t] * 2 * bs, 2 * bs), 2 * bs)],
                        dst.at[t],
                        load_sem.at[t, side],
                    ).start()
        return carry

    lax.fori_loop(0, n_terms, fetch, 0)

    def each_empty(step):
        def one(r, carry):
            @pl.when(empty[r] > 0)
            def _():
                step(store(zeros, r))

            return carry

        lax.fori_loop(0, out.shape[0] * results, one, 0)

    if phase == 0:
        zeros[...] = jnp.zeros_like(zeros)
        each_empty(lambda copy: copy.start())

    def some_terms(step, carry):
        ids = [step * UNROLL + u for u in range(UNROLL)]
        for t in ids:
            @pl.when(t < n_terms)
            def _():
                load(t, 0).wait()
                load(t, 1).wait()

        so_far = total[...]
        for t in ids:
            b_re, b_im = right[t, :bs], right[t, bs:]
            lhs = jnp.concatenate([left[t, :bs], left[t, bs:]], axis=1)
            rhs = jnp.concatenate(
                [
                    jnp.concatenate([b_re, b_im], axis=1),
                    jnp.concatenate([-b_im, b_re], axis=1),
                ],
                axis=0,
            )
            product = jnp.dot(lhs, rhs, preferred_element_type=jnp.float32)
            opens = terms[phase, OPENS, t] > 0
            so_far = jnp.where(opens, product, so_far + product)
            for part in range(2):
                result[t, part] = so_far[:, part * bs : (part + 1) * bs].astype(result.dtype)
        total[...] = so_far
        for t in ids:
            @pl.when((t < n_terms) & (terms[phase, CLOSES, t] > 0))
            def _():
                store(result.at[t], terms[phase, RESULT, t]).start()

        return carry

    lax.fori_loop(0, (n_terms + UNROLL - 1) // UNROLL, some_terms, 0)

    def drain(t, carry):
        @pl.when(terms[phase, CLOSES, t] > 0)
        def _():
            store(result.at[t], terms[phase, RESULT, t]).wait()

        return carry

    lax.fori_loop(0, n_terms, drain, 0)
    if phase == 0:
        each_empty(lambda copy: copy.wait())


def multiply(phase, planned, a_bufs, b_bufs, out_shape, so_far=None):
    bs = out_shape[-1]
    n_results = out_shape[0] * out_shape[1]
    most = planned[1].shape[2]
    padded = most + -most % UNROLL
    operands = [*planned, *a_bufs, *b_bufs] + ([] if so_far is None else [so_far])
    return pl.pallas_call(
        functools.partial(multiply_kernel, len(a_bufs), len(b_bufs), phase),
        out_shape=jax.ShapeDtypeStruct(out_shape, jnp.bfloat16),
        in_specs=[SMEM] * 3 + [HBM] * (len(operands) - 3),
        out_specs=HBM,
        scratch_shapes=[
            pltpu.VMEM((padded, 2 * bs, bs), jnp.bfloat16),
            pltpu.VMEM((padded, 2 * bs, bs), jnp.bfloat16),
            pltpu.VMEM((bs, 2 * bs), jnp.float32),
            pltpu.VMEM((padded, 2, bs, bs), jnp.bfloat16),
            pltpu.VMEM((2, bs, bs), jnp.bfloat16),
            pltpu.SemaphoreType.DMA((most, 2)),
            pltpu.SemaphoreType.DMA((n_results,)),
        ],
        input_output_aliases={} if so_far is None else {len(operands) - 1: 0},
        compiler_params=pltpu.CompilerParams(vmem_limit_bytes=48 * 1024 * 1024),
        cost_estimate=pl.CostEstimate(
            flops=most * 16 * bs**3, bytes_accessed=8 * most * bs**2, transcendentals=0
        ),
    )(*operands)


def with_columns(blocks, columns, bs):
    tail = jnp.pad(columns.astype(blocks.dtype)[None], ((0, 15), (0, bs - columns.shape[0])))
    return jnp.concatenate([blocks, tail], axis=0)


def columns_of(sent, rows):
    return sent[-16, :rows].astype(jnp.int32)


def on_device(x_blocks, x_cols, c_cols, c_keep):
    n_rows = lax.axis_size("rows")
    n_section = lax.axis_size("section")
    me_row, me_section = lax.axis_index("rows"), lax.axis_index("section")
    rows, bs = x_blocks.shape[0], x_blocks.shape[-1]
    panel_width = rows * n_rows // n_section
    half = rows // 2
    blocks, columns = x_blocks.reshape(-1, bs), x_cols.reshape(-1)
    everyone = [(r, s) for r in range(n_rows) for s in range(n_section)]

    if (n_rows, n_section) == (8, 4):
        middle = half * 2 * bs
        swap = lambda x, m: lax.ppermute(x, "rows", [(r, r ^ m) for r in range(n_rows)])

        def along(x, way):
            pairs = [(RING[i], RING[(i + way) % 4]) for i in range(4)]
            return lax.ppermute(x, "section", pairs)

        low = [along(with_columns(blocks[:middle], columns, bs), 1)]
        high = [along(with_columns(blocks[middle:], columns, bs), -1)]
        for _ in range(2):
            low.append(along(low[-1], 1))
            high.append(along(high[-1], -1))
        a_bufs = [blocks, *low[:2], *high[:2], low[2], high[2]]
        n_early = 5

        mine = with_columns(blocks, columns, bs)
        b_bufs = [blocks, swap(mine, 1)]
        for m in (2, 4):
            came = swap(mine, m)
            b_bufs += [came, swap(came, 1)]
        across = swap(b_bufs[2][:middle], 4), swap(b_bufs[4][middle:], 2)
        b_bufs += [across[0], swap(across[0], 1), across[1], swap(across[1], 1)]

        strip = [columns] + [columns_of(x, rows) for x in (low[0], high[0], low[1])]
        pieces = [columns] + [columns_of(b_bufs[b], rows) for b in (1, 2, 3, 4, 5, 8, 9)]
        steps = lambda s, a: (RING.index(s) - RING.index(a)) % 4
        tables = [
            [(0, 1, 2, 5)[steps(s, a)] for a in range(4)]
            + [(0, 6, 4, 3)[steps(s, a)] for a in range(4)]
            + [(0, half, half, half)[steps(s, a)] for a in range(4)]
            + [(0, 1, 3, 2)[steps(s, a)] for a in range(4)]
            + [(0, 1, 2, 3, 4, 5, 6, 7)[g ^ r] for g in range(8)]
            + [(0, 1, 2, 3, 4, 5, 8, 9)[g ^ r] for g in range(8)]
            + [(0, 0, 0, 0, 0, 0, half, half)[g ^ r] for g in range(8)]
            + [g ^ r for g in range(8)]
            for r, s in everyone
        ]
    else:

        def shifts(x, axis, n):
            shift = lambda d: lax.ppermute(x, axis, [(p, (p + d) % n) for p in range(n)])
            return [x] + [shift(d) for d in range(1, n)]

        a_bufs, b_bufs = shifts(blocks, "section", n_section), shifts(blocks, "rows", n_rows)
        n_early = len(a_bufs)
        strip, pieces = shifts(columns, "section", n_section), shifts(columns, "rows", n_rows)
        tables = []
        for r, s in everyone:
            panels = [(s - a) % n_section for a in range(n_section)]
            groups = [(r - g) % n_rows for g in range(n_rows)]
            tables.append(panels * 2 + [0] * n_section + panels + groups * 2 + [0] * n_rows + groups)

    lookup = jnp.asarray(np.array(tables, np.int32))[me_row * n_section + me_section]
    sizes = (rows, n_section, n_rows, panel_width, n_early, half)
    planned = plan(sizes, lookup, jnp.stack(strip), jnp.stack(pieces), c_cols, c_keep)
    out_shape = (rows, c_cols.shape[1], *x_blocks.shape[2:])
    out = multiply(0, planned, a_bufs[:n_early], b_bufs, out_shape)
    if n_early < len(a_bufs):
        out = multiply(1, planned, a_bufs, b_bufs, out_shape, out)
    return out


def solution(mesh):
    in_specs = (
        P("rows", "section", None, None, None),
        P("rows", "section"),
        P("rows", "section"),
        P("rows", "section"),
    )
    out_specs = P("rows", "section", None, None, None)
    return jax.shard_map(
        on_device, mesh=mesh, in_specs=in_specs, out_specs=out_specs, check_vma=False
    )
```

time: 156 us -> 75.8 us (0.49)
  waiting for transfers between devices: 80.4 us -> 12.1 us
  starting transfers between devices: 0.04 us -> 24.3 us
  blocking collectives: 20.8 us -> 0 us
  Pallas kernels: 0 us -> 17.5 us
  between operations: 14.1 us -> 0.13 us
  matrix products: 13.3 us -> 0 us
  local copies, waits for them, and re-layouts: 19.8 us -> 12 us
  other arithmetic: 7.15 us -> 9.02 us
    all_gather x2 -> x0, waiting for transfers between devices: 79 us -> none  [the longest x1 54.4 us: on_device(): lax.all_gather(x_blocks, 'section', axis=1, tiled=True)]
    ppermute x0 -> x15, starting transfers between devices: none -> 24.3 us  [the longest x6 17.3 us: along(): return lax.ppermute(x, 'section', pairs)]
    all_gather x2 -> x0, blocking collectives: 20.8 us -> none  [the longest x1 12.7 us: on_device(): lax.all_gather(x_cols, 'section', axis=1, tiled=True)]
    pallas_call x0 -> x3, Pallas kernels: none -> 17.5 us  [the longest x2 13.3 us: multiply(): pl.pallas_call(functools.partial(multiply_kernel, len(a_bufs), len(b_bufs...]
    dot_general x3 -> x0, matrix products: 13.3 us -> none  [the longest x1 8.85 us: contribute(): jnp.einsum('ialc,ialrxz->icrxz', matched.astype(jnp.float32), terms, prec...]
    ppermute x0 -> x15, waiting for transfers between devices: none -> 12.1 us  [the longest x6 12.1 us: along(): return lax.ppermute(x, 'section', pairs)]
    gather x3 -> x0, local copies, waits for them, and re-layouts: 7.51 us -> none  [the longest x2 6.73 us: contribute(): b_blocks[row_index]]
    another operation x1, local copies, waits for them, and re-layouts: 7.6 us -> 1.29 us  [on_device(): jnp.stack(pieces)]
  transfers between devices with their start and end apart: 2 -> 15, of which waited for: 2 -> 2; matrix products, arithmetic and copies ran while one was open for 9% -> 16% of each run, Pallas kernels for 0% -> 17%
where the time goes in v2:
time: 75.8 us; the launch traced here: 75.1 us
  starting transfers between devices  24.3 us (32%)
  Pallas kernels  17.5 us (23%)
  waiting for transfers between devices  12.1 us (16%)
  local copies, waits for them, and re-layouts  12 us (16%)
  other arithmetic  9.02 us (12%)
    ppermute x6, starting transfers between devices, along(): return lax.ppermute(x, 'section', pairs)  17.3 us
    pallas_call x2, Pallas kernels, multiply(): pl.pallas_call(functools.partial(multiply_kernel, len(a_bufs), len(b_bufs...  13.3 us
    ppermute x6, waiting for transfers between devices, along(): return lax.ppermute(x, 'section', pairs)  12.1 us
    unnamed x28, local copies, waits for them, and re-layouts  7.14 us
    ppermute x9, starting transfers between devices, on_device(): lax.ppermute(x, 'rows', [(r, r ^ m) for r in range(n_rows)])  7 us
    convert_element_type x10, other arithmetic, columns_of(): return sent[-16, :rows].astype(jnp.int32)  5.21 us
    pallas_call x1, Pallas kernels, plan(): pl.pallas_call(functools.partial(plan_kernel, sizes), out_shape=(jax.Shap...  4.18 us
    concatenate x2, other arithmetic, with_columns(): return jnp.concatenate([blocks, tail], axis=0)  1.92 us
  transfers between devices with their start and end apart: 15, of which 2 were waited for; matrix products, arithmetic and copies ran while one was open for 16% of the time, Pallas kernels for 17%

profile of v2, /device:TPU:0, one launch (start us, length us, event | category | flops | bytes accessed | tf_op | source)
XLA Modules:
  0.0 75.1 jit_solution(444194790949189231)
XLA Ops:
  0.0 0.7 bitcast_convert_fusion
  0.7 1.2 %fusion = (bf16[6,1,2,128,128]{4,3,2,1,0:T(8,128)(2,1)S(1)}, bf16[6,1,2,128,128]{4,3,2,1,0:T(8,128)(2,1)S(1)}) fusion(bf16[12,1,2,128,128]{4,3,2,1,0:T(8,128)(2,1)} %param.5), kind=kLoop, calls=%fused_computation.16 | loop fusion | bytes 1572864 | tf_op jit(solution)/shard_map/slice | solution.py:235
  1.9 1.0 %pad_maximum_fusion.1 = (bf16[1552,128]{1,0:T(8,128)(2,1)}, bf16[1552,128]{1,0:T(8,128)(2,1)}) fusion(bf16[16,128]{1,0:T(8,128)(2,1)S(1)} %pad.6, bf16[1536,128]{1,0:T(8,128)(2,1)S(1)} %bitcast.12, bf16[1536,128]{1,0:T(8,128)(2,1)S(1)} %bitcast.13), kind=kLoop, calls=%fused_computation.1 | loop fusion | flops 1390592 | bytes 1585152 | tf_op jit(solution)/shard_map/concatenate | solution.py:209
  2.9 3.0 %collective-permute-start.1 = (bf16[1552,128]{1,0:T(8,128)(2,1)}, bf16[1552,128]{1,0:T(8,128)(2,1)S(1)}, u32[]{:S(2)}, u32[]{:S(2)}) collective-permute-start(bf16[1552,128]{1,0:T(8,128)(2,1)} %get-tuple-element.13), channel_id=1, source_target_pairs={{0,1},{2,0},{3,2},{1,3},{4,5},{6,4},{7,6},{5,7},{8,9},{10,8},{11,1... | collective-permute-start | bytes 1191944 | tf_op jit(solution)/shard_map/ppermute | solution.py:232
  6.0 1.0 %collective-permute-start = (bf16[1552,128]{1,0:T(8,128)(2,1)}, bf16[1552,128]{1,0:T(8,128)(2,1)S(1)}, u32[]{:S(2)}, u32[]{:S(2)}) collective-permute-start(bf16[1552,128]{1,0:T(8,128)(2,1)} %get-tuple-element.14), channel_id=1, source_target_pairs={{0,2},{2,3},{3,1},{1,0},{4,6},{6,7},{7,5},{5,4},{8,10},{10,11},{11... | collective-permute-start | bytes 1191944 | tf_op jit(solution)/shard_map/ppermute | solution.py:232
  7.0 0.9 %pad_maximum_fusion = bf16[3088,128]{1,0:T(8,128)(2,1)} fusion(bf16[16,128]{1,0:T(8,128)(2,1)S(1)} %pad.6, bf16[3072,128]{1,0:T(8,128)(2,1)S(1)} %bitcast.7), kind=kLoop, calls=%fused_computation | loop fusion | flops 1581056 | bytes 1581056 | tf_op jit(solution)/shard_map/concatenate | solution.py:209
  7.9 1.9 %collective-permute-start.6 = (bf16[3088,128]{1,0:T(8,128)(2,1)}, bf16[3088,128]{1,0:T(8,128)(2,1)}, u32[]{:S(2)}, u32[]{:S(2)}) collective-permute-start(bf16[3088,128]{1,0:T(8,128)(2,1)} %pad_maximum_fusion), channel_id=1, source_target_pairs={{0,16},{4,20},{8,24},{12,28},{16,0},{20,4},{24,8},{28,12},{1,17},{... | collective-permute-start | bytes 2371592 | tf_op jit(solution)/shard_map/ppermute | solution.py:228
  9.8 1.5 %collective-permute-start.4 = (bf16[3088,128]{1,0:T(8,128)(2,1)}, bf16[3088,128]{1,0:T(8,128)(2,1)S(1)}, u32[]{:S(2)}, u32[]{:S(2)}) collective-permute-start(bf16[3088,128]{1,0:T(8,128)(2,1)} %pad_maximum_fusion), channel_id=1, source_target_pairs={{0,8},{4,12},{8,0},{12,4},{16,24},{20,28},{24,16},{28,20},{1,9},{5... | collective-permute-start | bytes 2371592 | tf_op jit(solution)/shard_map/ppermute | solution.py:228
  11.3 0.7 copy.7.c_cols
  11.9 0.7 copy.8.c_keep
  12.6 1.3 %dynamic-slice_bitcast_fusion.lookup = s32[48]{0:T(128)} fusion(s32[32,48]{1,0:T(8,128)} %constant.19.clone, s32[]{:T(128)S(6)} %select_n.3), kind=kLoop, calls=%fused_computation.14 | loop fusion | bytes 388 | tf_op jit(solution)/shard_map/squeeze | solution.py:279
  13.9 2.6 %collective-permute-done.1.refs_3_ = bf16[1552,128]{1,0:T(8,128)(2,1)S(1)} collective-permute-done((bf16[1552,128]{1,0:T(8,128)(2,1)}, bf16[1552,128]{1,0:T(8,128)(2,1)S(1)}, u32[]{:S(2)}, u32[]{:S(2)}) %collective-permute-start.1) | collective-permute-done | bytes 397344 | tf_op jit(solution)/shard_map/ppermute | solution.py:232
  16.5 10.4 %collective-permute-start.10 = (bf16[1552,128]{1,0:T(8,128)(2,1)S(1)}, bf16[1552,128]{1,0:T(8,128)(2,1)}, u32[]{:S(2)}, u32[]{:S(2)}) collective-permute-start(bf16[1552,128]{1,0:T(8,128)(2,1)S(1)} %collective-permute-done.1.refs_3_), channel_id=1, source_target_pairs={{0,1},{2,0},{3,2},{1,3},{4,5},{6,4},{7,6},{5,7},{8,9},{10,8},{11,1... | collective-permute-start | bytes 1191944 | tf_op jit(solution)/shard_map/ppermute | solution.py:232
  26.9 0.8 %collective-permute-start.2 = (bf16[1552,128]{1,0:T(8,128)(2,1)S(1)}, bf16[1552,128]{1,0:T(8,128)(2,1)}, u32[]{:S(2)}, u32[]{:S(2)}) collective-permute-start(bf16[1552,128]{1,0:T(8,128)(2,1)S(1)} %collective-permute-done.refs_1_), channel_id=1, source_target_pairs={{0,2},{2,3},{3,1},{1,0},{4,6},{6,7},{7,5},{5,4},{8,10},{10,11},{11... | collective-permute-start | bytes 1191944 | tf_op jit(solution)/shard_map/ppermute | solution.py:232
  27.7 1.0 %slice.72 = bf16[1552,128]{1,0:T(8,128)(2,1)S(1)} slice(bf16[3088,128]{1,0:T(8,128)(2,1)} %collective-permute-done.6.refs_9_.refs_11_), slice={[1536:3088], [0:128]} | slice | bytes 794624 | tf_op jit(solution)/shard_map/slice | solution.py:247
  28.8 1.6 %collective-permute-start.8 = (bf16[1552,128]{1,0:T(8,128)(2,1)S(1)}, bf16[1552,128]{1,0:T(8,128)(2,1)S(1)}, u32[]{:S(2)}, u32[]{:S(2)}) collective-permute-start(bf16[1552,128]{1,0:T(8,128)(2,1)S(1)} %slice.72), channel_id=1, source_target_pairs={{0,8},{4,12},{8,0},{12,4},{16,24},{20,28},{24,16},{28,20},{1,9},{5... | collective-permute-start | bytes 1191944 | tf_op jit(solution)/shard_map/ppermute | solution.py:228
  30.3 1.2 %slice_convert_fusion.3 = s32[1,12]{1,0:T(1,128)} fusion(bf16[3088,128]{1,0:T(8,128)(2,1)} %collective-permute-done.6.refs_9_.refs_11_), kind=kLoop, calls=%fused_computation.7 | loop fusion | flops 12 | bytes 72 | tf_op jit(solution)/shard_map/convert_element_type | solution.py:213
  32.1 1.6 %collective-permute-start.13 = (bf16[1536,128]{1,0:T(8,128)(2,1)S(1)}, bf16[1536,128]{1,0:T(8,128)(2,1)S(1)}, u32[]{:S(2)}, u32[]{:S(2)}) collective-permute-start(bf16[1536,128]{1,0:T(8,128)(2,1)S(1)} %slice.75), channel_id=1, source_target_pairs={{0,16},{4,20},{8,24},{12,28},{16,0},{20,4},{24,8},{28,12},{1,17},{... | collective-permute-start | bytes 1179656 | tf_op jit(solution)/shard_map/ppermute | solution.py:228
  33.7 9.5 %collective-permute-done.2.refs_2_ = bf16[1552,128]{1,0:T(8,128)(2,1)} collective-permute-done((bf16[1552,128]{1,0:T(8,128)(2,1)S(1)}, bf16[1552,128]{1,0:T(8,128)(2,1)}, u32[]{:S(2)}, u32[]{:S(2)}) %collective-permute-start.2) | collective-permute-done | bytes 397344 | tf_op jit(solution)/shard_map/ppermute | solution.py:232
  43.7 0.7 slice_convert_fusion.7
  44.4 1.2 %pad_add_fusion.strip = s32[4,12]{1,0:T(4,128)} fusion(s32[1,12]{1,0:T(1,128)S(1)} %slice_convert_fusion.7, s32[1,12]{1,0:T(1,128)S(1)} %slice_convert_fusion.8, s32[1,12]{1,0:T(1,128)S(1)} %slice_convert_fusion.9, s32[1,12]{1,0:T(1,128)} %bitcast.14), kind=kLoop, calls=%fused_computation.3 | loop fusion | flops 144 | bytes 384 | tf_op jit(solution)/shard_map/stack | solution.py:281
  46.3 1.4 %collective-permute-start.12 = (bf16[1552,128]{1,0:T(8,128)(2,1)}, bf16[1552,128]{1,0:T(8,128)(2,1)}, u32[]{:S(2)}, u32[]{:S(2)}) collective-permute-start(bf16[1552,128]{1,0:T(8,128)(2,1)} %collective-permute-done.10.refs_4_), channel_id=1, source_target_pairs={{0,1},{2,0},{3,2},{1,3},{4,5},{6,4},{7,6},{5,7},{8,9},{10,8},{11,1... | collective-permute-start | bytes 1191944 | tf_op jit(solution)/shard_map/ppermute | solution.py:232
  48.7 0.7 copy-done.2
  51.4 0.8 %copy-done.4 = bf16[1552,128]{1,0:T(8,128)(2,1)} copy-done((bf16[1552,128]{1,0:T(8,128)(2,1)}, bf16[1552,128]{1,0:T(8,128)(2,1)S(1)}, u32[]{:S(2)}) %copy-start.4) | copy-done | bytes 397336
  52.2 1.3 %stack.5.pieces = s32[8,12]{1,0:T(8,128)} concatenate(s32[1,12]{1,0:T(1,128)} %bitcast.15, s32[1,12]{1,0:T(1,128)} %slice_convert_fusion.6, s32[1,12]{1,0:T(1,128)} %slice_convert_fusion.5, s32[1,12]{1,0:T(1,128)} %slice_convert_fusion.4, s32[1,12]{1,0:T(1,128)} %slice_convert_fusion.3, s32[1,12]{1,0:T(1,128)} %slice_convert_fusion.2, s32[1,12]{1,0:T(1,128)} %slice_convert_fusion.1, ...), dimensions={0} | concatenate | bytes 768 | tf_op jit(solution)/shard_map/stack | solution.py:281
  53.5 4.2 %shard_map.55 = (s32[2]{0:T(128)}, s32[2,7,48]{2,1,0:T(8,128)}, s32[36]{0:T(128)}) custom-call(s32[48]{0:T(128)} %dynamic-slice_bitcast_fusion.lookup, s32[4,12]{1,0:T(4,128)} %pad_add_fusion.strip, s32[8,12]{1,0:T(8,128)} %stack.5.pieces, s32[12,3]{1,0:T(8,128)} %copy.7.c_cols, s32[12,3]{1,0:T(8,128)} %copy.8.c_keep), custom_call_target="tpu_custom_call" | custom-call | tf_op jit(solution)/shard_map/pallas_call | solution.py:77
  57.7 1.0 %copy-done.3 = bf16[1552,128]{1,0:T(8,128)(2,1)S(1)} copy-done((bf16[1552,128]{1,0:T(8,128)(2,1)S(1)}, bf16[1552,128]{1,0:T(8,128)(2,1)}, u32[]{:S(2)}) %copy-start.3) | copy-done | bytes 397336
  58.7 1.0 %copy-done.5 = bf16[1552,128]{1,0:T(8,128)(2,1)S(1)} copy-done((bf16[1552,128]{1,0:T(8,128)(2,1)S(1)}, bf16[1552,128]{1,0:T(8,128)(2,1)}, u32[]{:S(2)}) %copy-start.5) | copy-done | bytes 397336
  59.7 0.7 copy-done.6
  61.0 0.7 copy-done.8
  61.7 8.4 %shard_map.56.refs_17_ = bf16[12,3,2,128,128]{4,3,2,1,0:T(8,128)(2,1)} custom-call(s32[2]{0:T(128)S(1)} %copy-done.7, s32[2,7,48]{2,1,0:T(8,128)S(1)} %copy-done.6, s32[36]{0:T(128)S(1)} %copy-done.8, bf16[3072,128]{1,0:T(8,128)(2,1)S(1)} %bitcast.8, bf16[1552,128]{1,0:T(8,128)(2,1)S(1)} %collective-permute-done.refs_1_, ...), custom_call_target="tpu_custom_call" | custom-call | flops 1610612736 | bytes 6291456 | tf_op jit(solution)/shard_map/pallas_call | solution.py:185
  70.1 5.0 %shard_map.57 = bf16[12,3,2,128,128]{4,3,2,1,0:T(8,128)(2,1)} custom-call(s32[2]{0:T(128)S(1)} %copy-done.7, s32[2,7,48]{2,1,0:T(8,128)S(1)} %copy-done.6, s32[36]{0:T(128)S(1)} %copy-done.8, bf16[3072,128]{1,0:T(8,128)(2,1)S(1)} %bitcast.10, bf16[1552,128]{1,0:T(8,128)(2,1)S(1)} %collective-permute-done.refs_1_, ...), custom_call_target="tpu_custom_call", output_to_operand_aliasing={{}: (20, {})} | custom-call | flops 1610612736 | bytes 6291456 | tf_op jit(solution)/shard_map/pallas_call | solution.py:185
  (49 shorter events, 5.5 us)
Async XLA Ops:
  0.7 6.3 %copy-start = (bf16[12,1,2,128,128]{4,3,2,1,0:T(8,128)(2,1)S(1)}, bf16[12,1,2,128,128]{4,3,2,1,0:T(8,128)(2,1)}, u32[]{:S(2)}) copy-start(bf16[12,1,2,128,128]{4,3,2,1,0:T(8,128)(2,1)} %param.5) | copy-start | bytes 2359300
  1.9 9.3 %copy-start.11 = (s32[12,3]{0,1:T(4,128)S(1)}, s32[12,3]{0,1:T(4,128)}, u32[]{:S(2)}) copy-start(s32[12,3]{0,1:T(4,128)} %param.7) | copy-start | bytes 436
  1.9 10.0 %copy-start.12 = (s32[12,3]{0,1:T(4,128)S(1)}, s32[12,3]{0,1:T(4,128)}, u32[]{:S(2)}) copy-start(s32[12,3]{0,1:T(4,128)} %param.8) | copy-start | bytes 436
  2.9 13.6 %collective-permute-start.1 = (bf16[1552,128]{1,0:T(8,128)(2,1)}, bf16[1552,128]{1,0:T(8,128)(2,1)S(1)}, u32[]{:S(2)}, u32[]{:S(2)}) collective-permute-start(bf16[1552,128]{1,0:T(8,128)(2,1)} %get-tuple-element.13), channel_id=1, source_target_pairs={{0,1},{2,0},{3,2},{1,3},{4,5},{6,4},{7,6},{5,7},{8,9},{10,8},{11,1... | collective-permute-start | bytes 1191944 | tf_op jit(solution)/shard_map/ppermute | solution.py:232
  6.0 20.9 %collective-permute-start = (bf16[1552,128]{1,0:T(8,128)(2,1)}, bf16[1552,128]{1,0:T(8,128)(2,1)S(1)}, u32[]{:S(2)}, u32[]{:S(2)}) collective-permute-start(bf16[1552,128]{1,0:T(8,128)(2,1)} %get-tuple-element.14), channel_id=1, source_target_pairs={{0,2},{2,3},{3,1},{1,0},{4,6},{6,7},{7,5},{5,4},{8,10},{10,11},{11... | collective-permute-start | bytes 1191944 | tf_op jit(solution)/shard_map/ppermute | solution.py:232
  7.9 19.8 %collective-permute-start.6 = (bf16[3088,128]{1,0:T(8,128)(2,1)}, bf16[3088,128]{1,0:T(8,128)(2,1)}, u32[]{:S(2)}, u32[]{:S(2)}) collective-permute-start(bf16[3088,128]{1,0:T(8,128)(2,1)} %pad_maximum_fusion), channel_id=1, source_target_pairs={{0,16},{4,20},{8,24},{12,28},{16,0},{20,4},{24,8},{28,12},{1,17},{... | collective-permute-start | bytes 2371592 | tf_op jit(solution)/shard_map/ppermute | solution.py:228
  9.8 21.7 %collective-permute-start.4 = (bf16[3088,128]{1,0:T(8,128)(2,1)}, bf16[3088,128]{1,0:T(8,128)(2,1)S(1)}, u32[]{:S(2)}, u32[]{:S(2)}) collective-permute-start(bf16[3088,128]{1,0:T(8,128)(2,1)} %pad_maximum_fusion), channel_id=1, source_target_pairs={{0,8},{4,12},{8,0},{12,4},{16,24},{20,28},{24,16},{28,20},{1,9},{5... | collective-permute-start | bytes 2371592 | tf_op jit(solution)/shard_map/ppermute | solution.py:228
  11.2 20.9 %collective-permute-start.3 = (bf16[3088,128]{1,0:T(8,128)(2,1)}, bf16[3088,128]{1,0:T(8,128)(2,1)S(1)}, u32[]{:S(2)}, u32[]{:S(2)}) collective-permute-start(bf16[3088,128]{1,0:T(8,128)(2,1)} %pad_maximum_fusion), channel_id=1, source_target_pairs={{0,4},{4,0},{8,12},{12,8},{16,20},{20,16},{24,28},{28,24},{1,5},{5... | collective-permute-start | bytes 2371592 | tf_op jit(solution)/shard_map/ppermute | solution.py:228
  16.5 29.2 %collective-permute-start.10 = (bf16[1552,128]{1,0:T(8,128)(2,1)S(1)}, bf16[1552,128]{1,0:T(8,128)(2,1)}, u32[]{:S(2)}, u32[]{:S(2)}) collective-permute-start(bf16[1552,128]{1,0:T(8,128)(2,1)S(1)} %collective-permute-done.1.refs_3_), channel_id=1, source_target_pairs={{0,1},{2,0},{3,2},{1,3},{4,5},{6,4},{7,6},{5,7},{8,9},{10,8},{11,1... | collective-permute-start | bytes 1191944 | tf_op jit(solution)/shard_map/ppermute | solution.py:232
  26.9 16.3 %collective-permute-start.2 = (bf16[1552,128]{1,0:T(8,128)(2,1)S(1)}, bf16[1552,128]{1,0:T(8,128)(2,1)}, u32[]{:S(2)}, u32[]{:S(2)}) collective-permute-start(bf16[1552,128]{1,0:T(8,128)(2,1)S(1)} %collective-permute-done.refs_1_), channel_id=1, source_target_pairs={{0,2},{2,3},{3,1},{1,0},{4,6},{6,7},{7,5},{5,4},{8,10},{10,11},{11... | collective-permute-start | bytes 1191944 | tf_op jit(solution)/shard_map/ppermute | solution.py:232
  28.8 18.9 %collective-permute-start.8 = (bf16[1552,128]{1,0:T(8,128)(2,1)S(1)}, bf16[1552,128]{1,0:T(8,128)(2,1)S(1)}, u32[]{:S(2)}, u32[]{:S(2)}) collective-permute-start(bf16[1552,128]{1,0:T(8,128)(2,1)S(1)} %slice.72), channel_id=1, source_target_pairs={{0,8},{4,12},{8,0},{12,4},{16,24},{20,28},{24,16},{28,20},{1,9},{5... | collective-permute-start | bytes 1191944 | tf_op jit(solution)/shard_map/ppermute | solution.py:228
  31.5 38.6 %copy-start.1 = (bf16[3088,128]{1,0:T(8,128)(2,1)}, bf16[3088,128]{1,0:T(8,128)(2,1)S(1)}, u32[]{:S(2)}) copy-start(bf16[3088,128]{1,0:T(8,128)(2,1)S(1)} %collective-permute-done.4.refs_7_.refs_9_) | copy-start | bytes 2371588
  31.5 16.7 %collective-permute-start.7 = (bf16[3088,128]{1,0:T(8,128)(2,1)}, bf16[3088,128]{1,0:T(8,128)(2,1)S(1)}, u32[]{:S(2)}, u32[]{:S(2)}) collective-permute-start(bf16[3088,128]{1,0:T(8,128)(2,1)} %collective-permute-done.6.refs_9_.refs_11_), channel_id=1, source_target_pairs={{0,4},{4,0},{8,12},{12,8},{16,20},{20,16},{24,28},{28,24},{1,5},{5... | collective-permute-start | bytes 2371592 | tf_op jit(solution)/shard_map/ppermute | solution.py:228
  32.1 14.1 %collective-permute-start.13 = (bf16[1536,128]{1,0:T(8,128)(2,1)S(1)}, bf16[1536,128]{1,0:T(8,128)(2,1)S(1)}, u32[]{:S(2)}, u32[]{:S(2)}) collective-permute-start(bf16[1536,128]{1,0:T(8,128)(2,1)S(1)} %slice.75), channel_id=1, source_target_pairs={{0,16},{4,20},{8,24},{12,28},{16,0},{20,4},{24,8},{28,12},{1,17},{... | collective-permute-start | bytes 1179656 | tf_op jit(solution)/shard_map/ppermute | solution.py:228
  43.2 6.8 %collective-permute-start.5 = (bf16[3088,128]{1,0:T(8,128)(2,1)S(1)}, bf16[3088,128]{1,0:T(8,128)(2,1)S(1)}, u32[]{:S(2)}, u32[]{:S(2)}) collective-permute-start(bf16[3088,128]{1,0:T(8,128)(2,1)S(1)} %collective-permute-done.4.refs_7_.refs_9_), channel_id=1, source_target_pairs={{0,4},{4,0},{8,12},{12,8},{16,20},{20,16},{24,28},{28,24},{1,5},{5... | collective-permute-start | bytes 2371592 | tf_op jit(solution)/shard_map/ppermute | solution.py:228
  45.7 24.4 %collective-permute-start.11 = (bf16[1552,128]{1,0:T(8,128)(2,1)}, bf16[1552,128]{1,0:T(8,128)(2,1)}, u32[]{:S(2)}, u32[]{:S(2)}) collective-permute-start(bf16[1552,128]{1,0:T(8,128)(2,1)} %collective-permute-done.2.refs_2_), channel_id=1, source_target_pairs={{0,2},{2,3},{3,1},{1,0},{4,6},{6,7},{7,5},{5,4},{8,10},{10,11},{11... | collective-permute-start | bytes 1191944 | tf_op jit(solution)/shard_map/ppermute | solution.py:232
  46.3 23.8 %collective-permute-start.12 = (bf16[1552,128]{1,0:T(8,128)(2,1)}, bf16[1552,128]{1,0:T(8,128)(2,1)}, u32[]{:S(2)}, u32[]{:S(2)}) collective-permute-start(bf16[1552,128]{1,0:T(8,128)(2,1)} %collective-permute-done.10.refs_4_), channel_id=1, source_target_pairs={{0,1},{2,0},{3,2},{1,3},{4,5},{6,4},{7,6},{5,7},{8,9},{10,8},{11,1... | collective-permute-start | bytes 1191944 | tf_op jit(solution)/shard_map/ppermute | solution.py:232
  47.7 10.0 %collective-permute-start.14 = (bf16[1536,128]{1,0:T(8,128)(2,1)S(1)}, bf16[1536,128]{1,0:T(8,128)(2,1)}, u32[]{:S(2)}, u32[]{:S(2)}) collective-permute-start(bf16[1536,128]{1,0:T(8,128)(2,1)S(1)} %collective-permute-done.13.refs_11_.refs_13_), channel_id=1, source_target_pairs={{0,4},{4,0},{8,12},{12,8},{16,20},{20,16},{24,28},{28,24},{1,5},{5... | collective-permute-start | bytes 1179656 | tf_op jit(solution)/shard_map/ppermute | solution.py:228
  48.2 2.4 %copy-start.9 = (bf16[3088,128]{1,0:T(8,128)(2,1)}, bf16[3088,128]{1,0:T(8,128)(2,1)S(1)}, u32[]{:S(2)}) copy-start(bf16[3088,128]{1,0:T(8,128)(2,1)S(1)} %collective-permute-done.7.refs_10_.refs_12_) | copy-start | bytes 2371588
  48.2 2.4 %collective-permute-start.9 = (bf16[1552,128]{1,0:T(8,128)(2,1)S(1)}, bf16[1552,128]{1,0:T(8,128)(2,1)S(1)}, u32[]{:S(2)}, u32[]{:S(2)}) collective-permute-start(bf16[1552,128]{1,0:T(8,128)(2,1)S(1)} %collective-permute-done.8.refs_13_.refs_15_), channel_id=1, source_target_pairs={{0,4},{4,0},{8,12},{12,8},{16,20},{20,16},{24,28},{28,24},{1,5},{5... | collective-permute-start | bytes 1191944 | tf_op jit(solution)/shard_map/ppermute | solution.py:228
  48.7 0.7 copy-start.2
  50.0 0.9 %copy-start.10 = (bf16[3088,128]{1,0:T(8,128)(2,1)}, bf16[3088,128]{1,0:T(8,128)(2,1)S(1)}, u32[]{:S(2)}) copy-start(bf16[3088,128]{1,0:T(8,128)(2,1)S(1)} %collective-permute-done.5.refs_8_.refs_10_) | copy-start | bytes 2371588
  51.4 0.8 %copy-start.4 = (bf16[1552,128]{1,0:T(8,128)(2,1)}, bf16[1552,128]{1,0:T(8,128)(2,1)S(1)}, u32[]{:S(2)}) copy-start(bf16[1552,128]{1,0:T(8,128)(2,1)S(1)} %collective-permute-done.9.refs_14_.refs_16_) | copy-start | bytes 1191940
  57.7 1.0 %copy-start.3 = (bf16[1552,128]{1,0:T(8,128)(2,1)S(1)}, bf16[1552,128]{1,0:T(8,128)(2,1)}, u32[]{:S(2)}) copy-start(bf16[1552,128]{1,0:T(8,128)(2,1)} %copy-done.2) | copy-start | bytes 1191940
  58.7 1.0 %copy-start.5 = (bf16[1552,128]{1,0:T(8,128)(2,1)S(1)}, bf16[1552,128]{1,0:T(8,128)(2,1)}, u32[]{:S(2)}) copy-start(bf16[1552,128]{1,0:T(8,128)(2,1)} %copy-done.4) | copy-start | bytes 1191940
  59.7 0.7 copy-start.6
  60.4 0.6 copy-start.7
  61.0 0.7 copy-start.8

commit v3 on v2

v3 whole, which is shorter than its diff:
```python
import functools

import jax
import jax.numpy as jnp
import numpy as np
from jax import lax
from jax.experimental import pallas as pl
from jax.experimental.pallas import tpu as pltpu
from jax.sharding import PartitionSpec as P

RING = (0, 2, 3, 1)
SMEM = pl.BlockSpec(memory_space=pltpu.SMEM)
HBM = pl.BlockSpec(memory_space=pl.ANY)
LEFT_BUF, LEFT_ROW, RIGHT_BUF, RIGHT_ROW, RESULT, OPENS, CLOSES = range(7)
FIELDS = 7
UNROLL = 4
TAIL = 16
VMEM_BYTES = 60 * 1024 * 1024


def pick(index, low, high, act):
    if high - low == 1:
        act(low)
        return
    middle = (low + high) // 2

    @pl.when(index < middle)
    def _():
        pick(index, low, middle, act)

    @pl.when(index >= middle)
    def _():
        pick(index, middle, high, act)


def make_plan(sizes, lookup, strip, pieces, c_cols, c_keep, results, count, lists, empty):
    rows, n_section, n_rows, panel_width, n_early, half = sizes
    left_table = lambda field, a: lookup(field * n_section + a)
    right_table = lambda field, g: lookup(4 * n_section + field * n_rows + g)
    count[0] = 0
    count[1] = 0

    def one_row(i, carry):
        in_upper = i >= half
        halves = jnp.where(in_upper, 1, 0)
        slots = []
        for a in range(n_section):
            col = strip(left_table(3, a), i)
            k = jnp.maximum(a * panel_width + col, 0)
            group = k // rows
            inside = k - group * rows
            far = jnp.where(col >= 0, pieces(right_table(3, group), inside), -1)
            upper = inside >= half
            slots.append(
                (
                    far, left_table(halves, a), i - jnp.where(in_upper, left_table(2, a), 0),
                    right_table(jnp.where(upper, 1, 0), group),
                    inside - jnp.where(upper, right_table(2, group), 0),
                )
            )
        for c in range(results):
            wanted = jnp.where(c_keep(i, c) > 0, c_cols(i, c), -2)
            matches = [(slot[0] == wanted).astype(jnp.int32) for slot in slots]
            late = functools.reduce(
                jnp.maximum,
                [m * (slot[1] >= n_early).astype(jnp.int32) for m, slot in zip(matches, slots)],
            )
            n_matches = sum(matches)
            empty[i * results + c] = (n_matches == 0).astype(jnp.int32)

            @pl.when(n_matches > 0)
            def _():
                base = count[late]
                seen = jnp.int32(0)
                for m, slot in zip(matches, slots):
                    @pl.when(m > 0)
                    def _():
                        entry = slot[1:] + (
                            i * results + c,
                            (seen == 0).astype(jnp.int32),
                            (seen == n_matches - 1).astype(jnp.int32),
                        )
                        for f, value in enumerate(entry):
                            lists[late, f, base + seen] = value

                    seen = seen + m
                count[late] = base + n_matches

        return carry

    lax.fori_loop(0, rows, one_row, 0)


def multiply(count, terms, empty, a_bufs, b_bufs, out, scratch):
    left, right, total, result, zeros, load_sem, store_sem = scratch
    results, bs = out.shape[1], out.shape[-1]

    def load(t, side):
        dst = (left, right)[side].at[t]
        return pltpu.make_async_copy(dst, dst, load_sem.at[t, side])

    def store(source, r):
        return pltpu.make_async_copy(source, out.at[r // results, r % results], store_sem.at[r])

    def fetch(t, carry):
        sides = ((a_bufs, LEFT_BUF, LEFT_ROW, left), (b_bufs, RIGHT_BUF, RIGHT_ROW, right))
        for side, (bufs, which, row, dst) in enumerate(sides):
            start = pl.multiple_of(terms(row, t) * 2 * bs, 2 * bs)

            def act(b):
                source = bufs[b].at[pl.ds(start, 2 * bs)]
                pltpu.make_async_copy(source, dst.at[t], load_sem.at[t, side]).start()

            pick(terms(which, t), 0, len(bufs), act)
        return carry

    lax.fori_loop(0, count, fetch, 0)

    def each_empty(step):
        def one(r, carry):
            @pl.when(empty[r] > 0)
            def _():
                step(store(zeros, r))

            return carry

        lax.fori_loop(0, out.shape[0] * results, one, 0)

    if empty is not None:
        zeros[...] = jnp.zeros_like(zeros)
        each_empty(lambda copy: copy.start())

    def some_terms(step, carry):
        ids = [step * UNROLL + u for u in range(UNROLL)]
        for t in ids:
            @pl.when(t < count)
            def _():
                load(t, 0).wait()
                load(t, 1).wait()

        so_far = total[...]
        for t in ids:
            b_re, b_im = right[t, :bs], right[t, bs:]
            lhs = jnp.concatenate([left[t, :bs], left[t, bs:]], axis=1)
            rhs = jnp.concatenate(
                [
                    jnp.concatenate([b_re, b_im], axis=1),
                    jnp.concatenate([-b_im, b_re], axis=1),
                ],
                axis=0,
            )
            product = jnp.dot(lhs, rhs, preferred_element_type=jnp.float32)
            so_far = jnp.where(terms(OPENS, t) > 0, product, so_far + product)
            for part in range(2):
                result[t, part] = so_far[:, part * bs : (part + 1) * bs].astype(result.dtype)
        total[...] = so_far
        for t in ids:
            @pl.when((t < count) & (terms(CLOSES, t) > 0))
            def _():
                store(result.at[t], terms(RESULT, t)).start()

        return carry

    lax.fori_loop(0, (count + UNROLL - 1) // UNROLL, some_terms, 0)

    def drain(t, carry):
        @pl.when(terms(CLOSES, t) > 0)
        def _():
            store(result.at[t], terms(RESULT, t)).wait()

        return carry

    lax.fori_loop(0, count, drain, 0)
    if empty is not None:
        each_empty(lambda copy: copy.wait())


def early_kernel(sizes, n_a, n_b, pieces_from, tables, c_cols, c_keep, *refs):
    rows, n_section, n_rows = sizes[:3]
    strips, refs = refs[:n_section], refs[n_section:]
    a_bufs, b_bufs = refs[:n_a], refs[n_a : n_a + n_b]
    (
        out, count_out, late_terms, lists, count, empty, tails, table, numbers, scalars, sem, *scratch
    ) = refs[n_a + n_b :]
    pieces_at = n_section
    wanted_at = pieces_at + n_rows
    keep_at = wanted_at + rows
    lookup_at = keep_at + rows
    me = lax.axis_index("rows") * n_section + lax.axis_index("section")
    copies = [pltpu.make_async_copy(tables.at[me], table, sem.at[0])]
    sources = [*strips, *(b_bufs[b] for b in pieces_from)]
    for n, source in enumerate(sources):
        tail = source.at[pl.ds(source.shape[0] - TAIL, TAIL)]
        copies.append(pltpu.make_async_copy(tail, tails.at[n], sem.at[1 + n]))
    for copy in copies:
        copy.start()
    results = c_cols.shape[1]
    numbers[wanted_at : wanted_at + rows, :results] = c_cols[...]
    numbers[keep_at : keep_at + rows, :results] = c_keep[...]
    for copy in copies:
        copy.wait()
    for n in range(len(sources)):
        numbers[n : n + 1] = tails[n].astype(jnp.float32)[:1].astype(jnp.int32)
    numbers[lookup_at : lookup_at + table.shape[0]] = table[...]
    to_scalars = pltpu.make_async_copy(numbers, scalars, sem.at[0])
    to_scalars.start()
    to_scalars.wait()
    lanes = numbers.shape[1]
    make_plan(
        sizes, lambda n: scalars[lookup_at + n // lanes, n % lanes], lambda n, i: scalars[n, i],
        lambda n, i: scalars[pieces_at + n, i], lambda i, c: scalars[wanted_at + i, c],
        lambda i, c: scalars[keep_at + i, c], results, count, lists, empty,
    )
    count_out[0] = count[1]

    def hand_on(t, carry):
        for f in range(FIELDS):
            late_terms[f, t] = lists[1, f, t]
        return carry

    lax.fori_loop(0, count[1], hand_on, 0)
    multiply(count[0], lambda f, t: lists[0, f, t], empty, a_bufs, b_bufs, out, scratch)


def late_kernel(n_a, n_b, count, terms, *refs):
    a_bufs, b_bufs = refs[:n_a], refs[n_a : n_a + n_b]
    out, *scratch = refs[n_a + n_b + 1 :]
    multiply(count[0], lambda f, t: terms[f, t], None, a_bufs, b_bufs, out, scratch)


def scratch_for(most, n_results, bs):
    padded = most + -most % UNROLL
    return [
        pltpu.VMEM((padded, 2 * bs, bs), jnp.bfloat16),
        pltpu.VMEM((padded, 2 * bs, bs), jnp.bfloat16),
        pltpu.VMEM((bs, 2 * bs), jnp.float32),
        pltpu.VMEM((padded, 2, bs, bs), jnp.bfloat16),
        pltpu.VMEM((2, bs, bs), jnp.bfloat16),
        pltpu.SemaphoreType.DMA((most, 2)),
        pltpu.SemaphoreType.DMA((n_results,)),
    ]


def cost(terms, bs):
    return pl.CostEstimate(
        flops=terms * 16, bytes_accessed=12 * terms, transcendentals=0
    )


def multiply_early(sizes, pieces_from, tables, c_cols, c_keep, strips, a_bufs, b_bufs, out_shape):
    rows, n_section, n_rows = sizes[:3]
    bs, most = out_shape[-1], rows * n_section
    n_results = c_cols.size
    padded = most + -most % UNROLL
    n_numbers = n_section + n_rows + 2 * rows + tables.shape[1]
    vmem = pl.BlockSpec(memory_space=pltpu.VMEM)
    operands = [*strips, *a_bufs, *b_bufs]
    return pl.pallas_call(
        functools.partial(early_kernel, sizes, len(a_bufs), len(b_bufs), pieces_from),
        out_shape=(
            jax.ShapeDtypeStruct(out_shape, jnp.bfloat16),
            jax.ShapeDtypeStruct((1,), jnp.int32),
            jax.ShapeDtypeStruct((FIELDS, padded), jnp.int32),
        ),
        in_specs=[HBM, vmem, vmem] + [HBM] * len(operands),
        out_specs=(HBM, SMEM, SMEM),
        scratch_shapes=[
            pltpu.SMEM((2, FIELDS, padded), jnp.int32),
            pltpu.SMEM((2,), jnp.int32),
            pltpu.SMEM((n_results,), jnp.int32),
            pltpu.VMEM((n_section + n_rows, TAIL, bs), jnp.bfloat16),
            pltpu.VMEM(tables.shape[1:], jnp.int32),
            pltpu.VMEM((n_numbers, bs), jnp.int32),
            pltpu.SMEM((n_numbers, bs), jnp.int32),
            pltpu.SemaphoreType.DMA((1 + n_section + n_rows,)),
            *scratch_for(most, n_results, bs),
        ],
        compiler_params=pltpu.CompilerParams(vmem_limit_bytes=VMEM_BYTES),
        cost_estimate=cost(most, bs),
    )(tables, c_cols, c_keep, *operands)


def multiply_late(count, terms, a_bufs, b_bufs, so_far):
    bs = so_far.shape[-1]
    operands = [count, terms, *a_bufs, *b_bufs, so_far]
    return pl.pallas_call(
        functools.partial(late_kernel, len(a_bufs), len(b_bufs)),
        out_shape=jax.ShapeDtypeStruct(so_far.shape, so_far.dtype),
        in_specs=[SMEM] * 2 + [HBM] * (len(operands) - 2),
        out_specs=HBM,
        scratch_shapes=scratch_for(terms.shape[1], so_far.shape[0] * so_far.shape[1], bs),
        input_output_aliases={len(operands) - 1: 0},
        compiler_params=pltpu.CompilerParams(vmem_limit_bytes=VMEM_BYTES),
        cost_estimate=cost(terms.shape[1] // 4, bs),
    )(*operands)


def with_columns(blocks, *columns):
    bs = blocks.shape[1]
    lines = [jnp.pad(c.astype(blocks.dtype), (0, bs - c.shape[0])) for c in columns]
    tail = jnp.pad(jnp.stack(lines), ((0, TAIL - len(lines)), (0, 0)))
    return jnp.concatenate([blocks, tail], axis=0)


def on_device(x_blocks, x_cols, c_cols, c_keep):
    n_rows = lax.axis_size("rows")
    n_section = lax.axis_size("section")
    rows, bs = x_blocks.shape[0], x_blocks.shape[-1]
    panel_width = rows * n_rows // n_section
    half = rows // 2
    blocks, columns = x_blocks.reshape(-1, bs), x_cols.reshape(-1)
    everyone = [(r, s) for r in range(n_rows) for s in range(n_section)]
    mine = with_columns(blocks, columns)

    if (n_rows, n_section) == (8, 4):
        middle = half * 2 * bs
        swap = lambda x, m: lax.ppermute(x, "rows", [(r, r ^ m) for r in range(n_rows)])

        pairs = [(RING[i], RING[(i + 1) % 4]) for i in range(4)]
        line = jnp.pad(columns.astype(blocks.dtype)[None], ((0, TAIL - 1), (0, bs - rows)))
        line = lax.ppermute(line, "section", [(d, s) for s, d in pairs])
        came = [swap(mine, m) for m in (2, 4, 6)]
        came[0], own, line = lax.optimization_barrier((came[0], mine, line))
        b_bufs = []
        for x in [own, *came]:
            b_bufs += [x, swap(x, 1)]
        pieces_from = tuple(range(8))

        low, high = [with_columns(blocks[:middle], columns)], [blocks[middle:]]
        for _ in range(3):
            low.append(lax.ppermute(low[-1], "section", pairs))
            high.append(lax.ppermute(high[-1], "section", pairs))
        a_bufs = [mine, *low[1:3], *high[1:3], low[3], high[3]]
        n_early = 5
        strips = [mine, *low[1:3], line]

        steps = lambda s, a: (RING.index(s) - RING.index(a)) % 4
        tables = [
            [(0, 1, 2, 5)[steps(s, a)] for a in range(4)]
            + [(0, 3, 4, 6)[steps(s, a)] for a in range(4)]
            + [(0, half, half, half)[steps(s, a)] for a in range(4)]
            + [steps(s, a) for a in range(4)]
            + [g ^ r for g in range(8)] * 2
            + [0] * 8
            + [g ^ r for g in range(8)]
            for r, s in everyone
        ]
    else:

        def shifts(x, axis, n):
            shift = lambda d: lax.ppermute(x, axis, [(p, (p + d) % n) for p in range(n)])
            return [x] + [shift(d) for d in range(1, n)]

        a_bufs, b_bufs = shifts(mine, "section", n_section), shifts(mine, "rows", n_rows)
        strips = a_bufs
        n_early, pieces_from = n_section, tuple(range(n_rows))
        tables = []
        for r, s in everyone:
            panels = [(s - a) % n_section for a in range(n_section)]
            groups = [(r - g) % n_rows for g in range(n_rows)]
            tables.append(panels * 2 + [0] * n_section + panels + groups * 2 + [0] * n_rows + groups)

    tables = np.array(tables, np.int32)
    tables = np.pad(tables, ((0, 0), (0, -tables.shape[1] % (8 * bs)))).reshape(len(everyone), -1, bs)
    sizes = (rows, n_section, n_rows, panel_width, n_early, half)
    out_shape = (rows, c_cols.shape[1], *x_blocks.shape[2:])
    out, count, terms = multiply_early(
        sizes, pieces_from, jnp.asarray(tables), c_cols, c_keep, strips, a_bufs[:n_early], b_bufs, out_shape
    )
    if n_early < len(a_bufs):
        out = multiply_late(count, terms, a_bufs, b_bufs, out)
    return out


def solution(mesh):
    in_specs = (
        P("rows", "section", None, None, None),
        P("rows", "section"),
        P("rows", "section"),
        P("rows", "section"),
    )
    out_specs = P("rows", "section", None, None, None)
    return jax.shard_map(
        on_device, mesh=mesh, in_specs=in_specs, out_specs=out_specs, check_vma=False
    )
```

time: 75.8 us -> 67 us (0.88)
  waiting for transfers between devices: 12.1 us -> 29.6 us
  local copies, waits for them, and re-layouts: 12 us -> 2.38 us
  starting transfers between devices: 24.3 us -> 17 us
  other arithmetic: 9.02 us -> 1.94 us
  Pallas kernels: 17.5 us -> 15.7 us
    ppermute x9 -> x7, waiting for transfers between devices: 0.02 us -> 11.9 us  [on_device(): lax.ppermute(x, 'rows', [(r, r ^ m) for r in range(n_rows)])]
    ppermute x6 -> x7, waiting for transfers between devices: 12.1 us -> 17.7 us  [the longest x3 8.18 us: on_device(): low.append(lax.ppermute(low[-1], 'section', pairs))]
    ppermute x6 -> x7, starting transfers between devices: 17.3 us -> 11.9 us  [the longest x3 7.7 us: on_device(): low.append(lax.ppermute(low[-1], 'section', pairs))]
    convert_element_type x11 -> x1, other arithmetic: 5.87 us -> 0.73 us  [with_columns(): c.astype(blocks.dtype)]
    unnamed x28 -> x24, local copies, waits for them, and re-layouts: 7.14 us -> 2.31 us
    slice x3 -> x1, local copies, waits for them, and re-layouts: 2.29 us -> 0.05 us  [on_device(): low, high = ([with_columns(blocks[:middle], columns)], [blocks[middle:]])]
    pallas_call x3 -> x2, Pallas kernels: 17.5 us -> 15.7 us  [the longest x1 10.8 us: multiply_early(): pl.pallas_call(functools.partial(early_kernel, sizes, len(a_bufs), len(b_...]
    ppermute x9 -> x7, starting transfers between devices: 7 us -> 5.19 us  [on_device(): lax.ppermute(x, 'rows', [(r, r ^ m) for r in range(n_rows)])]
  transfers between devices with their start and end apart: 15 -> 14, of which waited for: 2 -> 6; matrix products, arithmetic and copies ran while one was open for 16% -> 2% of each run, Pallas kernels for 17% -> 16%
where the time goes in v3:
time: 67 us; the launch traced here: 66.8 us
  waiting for transfers between devices  29.6 us (44%)
  starting transfers between devices  17 us (25%)
  Pallas kernels  15.7 us (23%)
  local copies, waits for them, and re-layouts  2.38 us (4%)
  other arithmetic  1.94 us (3%)
    ppermute x7, waiting for transfers between devices, on_device(): lax.ppermute(x, 'rows', [(r, r ^ m) for r in range(n_rows)])  11.9 us
    pallas_call x1, Pallas kernels, multiply_early(): pl.pallas_call(functools.partial(early_kernel, sizes, len(a_bufs), len(b_...  10.8 us
    ppermute x3, waiting for transfers between devices, on_device(): low.append(lax.ppermute(low[-1], 'section', pairs))  8.18 us
    ppermute x3, starting transfers between devices, on_device(): low.append(lax.ppermute(low[-1], 'section', pairs))  7.7 us
    ppermute x1, waiting for transfers between devices, on_device(): line = lax.ppermute(line, 'section', [(d, s) for s, d in pairs])  7.61 us
    ppermute x7, starting transfers between devices, on_device(): lax.ppermute(x, 'rows', [(r, r ^ m) for r in range(n_rows)])  5.19 us
    pallas_call x1, Pallas kernels, multiply_late(): pl.pallas_call(functools.partial(late_kernel, len(a_bufs), len(b_bufs)),...  4.87 us
    ppermute x3, starting transfers between devices, on_device(): high.append(lax.ppermute(high[-1], 'section', pairs))  4.15 us
  transfers between devices with their start and end apart: 14, of which 6 were waited for; matrix products, arithmetic and copies ran while one was open for 2% of the time, Pallas kernels for 16%

profile of v3, /device:TPU:0, one launch (start us, length us, event | category | flops | bytes accessed | tf_op | source)
XLA Modules:
  0.0 66.8 jit_solution(8178296856358754956)
XLA Ops:
  0.0 0.7 %convert_bitcast_fusion = (bf16[1,12]{1,0:T(2,128)(2,1)S(1)}, bf16[12]{0:T(256)(128)(2,1)S(1)}) fusion(s32[12,1]{0,1:T(1,128)} %param.6), kind=kLoop, calls=%fused_computation.3 | loop fusion | flops 12 | bytes 96 | tf_op jit(solution)/shard_map/convert_element_type | solution.py:300
  0.8 1.2 %pad_maximum_fusion.refs_0_.refs_4_.refs_9_.refs_7_ = bf16[3088,128]{1,0:T(8,128)(2,1)S(1)} fusion(bf16[16,128]{1,0:T(8,128)(2,1)S(1)} %pad.15, bf16[3072,128]{1,0:T(8,128)(2,1)} %bitcast.9), kind=kLoop, calls=%fused_computation | loop fusion | flops 1581056 | bytes 1581056 | tf_op jit(solution)/shard_map/concatenate | solution.py:302
  1.9 0.0 copy-start.9
  2.0 0.0 copy-start.10
  2.0 4.0 %collective-permute-start.10 = (bf16[3088,128]{1,0:T(8,128)(2,1)S(1)}, bf16[3088,128]{1,0:T(8,128)(2,1)S(1)}, u32[]{:S(2)}, u32[]{:S(2)}) collective-permute-start(bf16[3088,128]{1,0:T(8,128)(2,1)S(1)} %pad_maximum_fusion.refs_0_.refs_4_.refs_9_.refs_7_), channel_id=1, source_target_pairs={{0,24},{4,28},{8,16},{12,20},{16,8},{20,12},{24,0},{28,4},{1,25},{... | collective-permute-start | bytes 2371592 | tf_op jit(solution)/shard_map/ppermute | solution.py:317
  5.9 0.5 collective-permute-start.8
  6.4 0.1 collective-permute-start.2
  6.6 0.1 fusion
  6.6 3.0 %collective-permute-start.4 = (bf16[1536,128]{1,0:T(8,128)(2,1)S(1)}, bf16[1536,128]{1,0:T(8,128)(2,1)S(1)}, u32[]{:S(2)}, u32[]{:S(2)}) collective-permute-start(bf16[1536,128]{1,0:T(8,128)(2,1)S(1)} %bitcast.11), channel_id=1, source_target_pairs={{0,2},{2,3},{3,1},{1,0},{4,6},{6,7},{7,5},{5,4},{8,10},{10,11},{11... | collective-permute-start | bytes 1179656 | tf_op jit(solution)/shard_map/ppermute | solution.py:332
  9.7 0.0 collective-permute-start.3
  9.7 7.6 %collective-permute-done.3.refs_3_ = bf16[16,128]{1,0:T(8,128)(2,1)S(1)} collective-permute-done((bf16[16,128]{1,0:T(8,128)(2,1)S(1)}, bf16[16,128]{1,0:T(8,128)(2,1)S(1)}, u32[]{:S(2)}, u32[]{:S(2)}) %collective-permute-start.3) | collective-permute-done | bytes 4128 | tf_op jit(solution)/shard_map/ppermute | solution.py:321
  17.3 2.4 %collective-permute-start = (bf16[1552,128]{1,0:T(8,128)(2,1)S(1)}, bf16[1552,128]{1,0:T(8,128)(2,1)S(1)}, u32[]{:S(2)}, u32[]{:S(2)}) collective-permute-start(bf16[1552,128]{1,0:T(8,128)(2,1)S(1)} %pad_maximum_fusion.1), channel_id=1, source_target_pairs={{0,2},{2,3},{3,1},{1,0},{4,6},{6,7},{7,5},{5,4},{8,10},{10,11},{11... | collective-permute-start | bytes 1191944 | tf_op jit(solution)/shard_map/ppermute | solution.py:331
  19.7 0.0 collective-permute-done.4.refs_7_.refs_3_
  19.7 1.0 %collective-permute-start.5 = (bf16[1536,128]{1,0:T(8,128)(2,1)S(1)}, bf16[1536,128]{1,0:T(8,128)(2,1)}, u32[]{:S(2)}, u32[]{:S(2)}) collective-permute-start(bf16[1536,128]{1,0:T(8,128)(2,1)S(1)} %collective-permute-done.4.refs_7_.refs_3_), channel_id=1, source_target_pairs={{0,2},{2,3},{3,1},{1,0},{4,6},{6,7},{7,5},{5,4},{8,10},{10,11},{11... | collective-permute-start | bytes 1179656 | tf_op jit(solution)/shard_map/ppermute | solution.py:332
  20.7 3.8 %collective-permute-done.10.refs_15_.refs_13_ = bf16[3088,128]{1,0:T(8,128)(2,1)S(1)} collective-permute-done((bf16[3088,128]{1,0:T(8,128)(2,1)S(1)}, bf16[3088,128]{1,0:T(8,128)(2,1)S(1)}, u32[]{:S(2)}, u32[]{:S(2)}) %collective-permute-start.10) | collective-permute-done | bytes 790560 | tf_op jit(solution)/shard_map/ppermute | solution.py:317
  24.4 0.0 collective-permute-start.11
  24.4 5.5 %collective-permute-done.refs_1_.refs_5_ = bf16[1552,128]{1,0:T(8,128)(2,1)S(1)} collective-permute-done((bf16[1552,128]{1,0:T(8,128)(2,1)S(1)}, bf16[1552,128]{1,0:T(8,128)(2,1)S(1)}, u32[]{:S(2)}, u32[]{:S(2)}) %collective-permute-start) | collective-permute-done | bytes 397344 | tf_op jit(solution)/shard_map/ppermute | solution.py:331
  29.9 2.8 %collective-permute-start.1 = (bf16[1552,128]{1,0:T(8,128)(2,1)S(1)}, bf16[1552,128]{1,0:T(8,128)(2,1)S(1)}, u32[]{:S(2)}, u32[]{:S(2)}) collective-permute-start(bf16[1552,128]{1,0:T(8,128)(2,1)S(1)} %collective-permute-done.refs_1_.refs_5_), channel_id=1, source_target_pairs={{0,2},{2,3},{3,1},{1,0},{4,6},{6,7},{7,5},{5,4},{8,10},{10,11},{11... | collective-permute-start | bytes 1191944 | tf_op jit(solution)/shard_map/ppermute | solution.py:331
  32.7 8.2 %collective-permute-done.2.refs_11_.refs_9_ = bf16[3088,128]{1,0:T(8,128)(2,1)} collective-permute-done((bf16[3088,128]{1,0:T(8,128)(2,1)S(1)}, bf16[3088,128]{1,0:T(8,128)(2,1)}, u32[]{:S(2)}, u32[]{:S(2)}) %collective-permute-start.2) | collective-permute-done | bytes 790560 | tf_op jit(solution)/shard_map/ppermute | solution.py:317
  40.9 0.5 collective-permute-start.9
  41.4 0.1 collective-permute-start.7
  41.5 2.7 %collective-permute-done.1.refs_2_.refs_6_ = bf16[1552,128]{1,0:T(8,128)(2,1)S(1)} collective-permute-done((bf16[1552,128]{1,0:T(8,128)(2,1)S(1)}, bf16[1552,128]{1,0:T(8,128)(2,1)S(1)}, u32[]{:S(2)}, u32[]{:S(2)}) %collective-permute-start.1) | collective-permute-done | bytes 397344 | tf_op jit(solution)/shard_map/ppermute | solution.py:331
  44.2 2.5 %collective-permute-start.12 = (bf16[1552,128]{1,0:T(8,128)(2,1)S(1)}, bf16[1552,128]{1,0:T(8,128)(2,1)}, u32[]{:S(2)}, u32[]{:S(2)}) collective-permute-start(bf16[1552,128]{1,0:T(8,128)(2,1)S(1)} %collective-permute-done.1.refs_2_.refs_6_), channel_id=1, source_target_pairs={{0,2},{2,3},{3,1},{1,0},{4,6},{6,7},{7,5},{5,4},{8,10},{10,11},{11... | collective-permute-start | bytes 1191944 | tf_op jit(solution)/shard_map/ppermute | solution.py:331
  46.7 0.0 collective-permute-done.11.refs_16_.refs_14_
  46.7 0.9 %copy-done.5 = bf16[3088,128]{1,0:T(8,128)(2,1)} copy-done((bf16[3088,128]{1,0:T(8,128)(2,1)}, bf16[3088,128]{1,0:T(8,128)(2,1)S(1)}, u32[]{:S(2)}) %copy-start.5) | copy-done | bytes 790552
  47.6 0.1 collective-permute-start.13
  47.8 0.7 %copy.7.c_cols = s32[12,3]{1,0:T(8,128)} copy(s32[12,3]{0,1:T(4,128)S(1)} %copy-done.9) | data formatting | bytes 288 | tf_op args[2]
  48.5 0.7 %copy.8.c_keep = s32[12,3]{1,0:T(8,128)} copy(s32[12,3]{0,1:T(4,128)S(1)} %copy-done.10) | data formatting | bytes 288 | tf_op args[3]
  49.1 0.0 collective-permute-done.9.refs_14_.refs_12_
  49.2 10.8 %shard_map.55 = (bf16[12,3,2,128,128]{4,3,2,1,0:T(8,128)(2,1)}, s32[1]{0:T(128)}, s32[7,48]{1,0:T(8,128)}) custom-call(s32[32,8,128]{2,1,0:T(8,128)} %constant.5.clone.tables, s32[12,3]{1,0:T(8,128)} %copy.7.c_cols, s32[12,3]{1,0:T(8,128)} %copy.8.c_keep, bf16[3088,128]{1,0:T(8,128)(2,1)} %copy-done, bf16[1552,128]{1,0:T(8,128)(2,1)} %copy-done.1, ...), custom_call_target="tpu_custom_call" | custom-call | flops 768 | bytes 576 | tf_op jit(solution)/shard_map/pallas_call | solution.py:258
  60.0 1.9 %collective-permute-done.13.refs_6_ = bf16[1536,128]{1,0:T(8,128)(2,1)} collective-permute-done((bf16[1536,128]{1,0:T(8,128)(2,1)}, bf16[1536,128]{1,0:T(8,128)(2,1)}, u32[]{:S(2)}, u32[]{:S(2)}) %collective-permute-start.13) | collective-permute-done | bytes 393248 | tf_op jit(solution)/shard_map/ppermute | solution.py:332
  61.9 4.9 %shard_map.56 = bf16[12,3,2,128,128]{4,3,2,1,0:T(8,128)(2,1)} custom-call(s32[1]{0:T(128)} %get-tuple-element.14.count, s32[7,48]{1,0:T(8,128)} %get-tuple-element.15.terms, bf16[3088,128]{1,0:T(8,128)(2,1)} %copy-done, bf16[1552,128]{1,0:T(8,128)(2,1)} %copy-done.1, bf16[1552,128]{1,0:T(8,128)(2,1)} %copy-done.2, ...), custom_call_target="tpu_custom_call", output_to_operand_aliasing={{}: (17, {})} | custom-call | flops 192 | bytes 144 | tf_op jit(solution)/shard_map/pallas_call | solution.py:286
  (29 shorter events, 0.1 us)
Async XLA Ops:
  0.0 6.6 %copy-start.6 = (bf16[12,1,2,128,128]{4,3,2,1,0:T(8,128)(2,1)S(1)}, bf16[12,1,2,128,128]{4,3,2,1,0:T(8,128)(2,1)}, u32[]{:S(2)}) copy-start(bf16[12,1,2,128,128]{4,3,2,1,0:T(8,128)(2,1)} %param.5) | copy-start | bytes 2359300
  1.9 47.2 %copy-start = (bf16[3088,128]{1,0:T(8,128)(2,1)}, bf16[3088,128]{1,0:T(8,128)(2,1)S(1)}, u32[]{:S(2)}) copy-start(bf16[3088,128]{1,0:T(8,128)(2,1)S(1)} %pad_maximum_fusion.refs_0_.refs_4_.refs_9_.refs_7_) | copy-start | bytes 2371588
  1.9 45.8 %copy-start.9 = (s32[12,3]{0,1:T(4,128)S(1)}, s32[12,3]{0,1:T(4,128)}, u32[]{:S(2)}) copy-start(s32[12,3]{0,1:T(4,128)} %param.7) | copy-start | bytes 436
  2.0 46.5 %copy-start.10 = (s32[12,3]{0,1:T(4,128)S(1)}, s32[12,3]{0,1:T(4,128)}, u32[]{:S(2)}) copy-start(s32[12,3]{0,1:T(4,128)} %param.8) | copy-start | bytes 436
  2.0 22.5 %collective-permute-start.10 = (bf16[3088,128]{1,0:T(8,128)(2,1)S(1)}, bf16[3088,128]{1,0:T(8,128)(2,1)S(1)}, u32[]{:S(2)}, u32[]{:S(2)}) collective-permute-start(bf16[3088,128]{1,0:T(8,128)(2,1)S(1)} %pad_maximum_fusion.refs_0_.refs_4_.refs_9_.refs_7_), channel_id=1, source_target_pairs={{0,24},{4,28},{8,16},{12,20},{16,8},{20,12},{24,0},{28,4},{1,25},{... | collective-permute-start | bytes 2371592 | tf_op jit(solution)/shard_map/ppermute | solution.py:317
  5.9 35.0 %collective-permute-start.8 = (bf16[3088,128]{1,0:T(8,128)(2,1)S(1)}, bf16[3088,128]{1,0:T(8,128)(2,1)S(1)}, u32[]{:S(2)}, u32[]{:S(2)}) collective-permute-start(bf16[3088,128]{1,0:T(8,128)(2,1)S(1)} %pad_maximum_fusion.refs_0_.refs_4_.refs_9_.refs_7_), channel_id=1, source_target_pairs={{0,16},{4,20},{8,24},{12,28},{16,0},{20,4},{24,8},{28,12},{1,17},{... | collective-permute-start | bytes 2371592 | tf_op jit(solution)/shard_map/ppermute | solution.py:317
  6.4 34.5 %collective-permute-start.2 = (bf16[3088,128]{1,0:T(8,128)(2,1)S(1)}, bf16[3088,128]{1,0:T(8,128)(2,1)}, u32[]{:S(2)}, u32[]{:S(2)}) collective-permute-start(bf16[3088,128]{1,0:T(8,128)(2,1)S(1)} %pad_maximum_fusion.refs_0_.refs_4_.refs_9_.refs_7_), channel_id=1, source_target_pairs={{0,8},{4,12},{8,0},{12,4},{16,24},{20,28},{24,16},{28,20},{1,9},{5... | collective-permute-start | bytes 2371592 | tf_op jit(solution)/shard_map/ppermute | solution.py:317
  6.6 13.1 %collective-permute-start.4 = (bf16[1536,128]{1,0:T(8,128)(2,1)S(1)}, bf16[1536,128]{1,0:T(8,128)(2,1)S(1)}, u32[]{:S(2)}, u32[]{:S(2)}) collective-permute-start(bf16[1536,128]{1,0:T(8,128)(2,1)S(1)} %bitcast.11), channel_id=1, source_target_pairs={{0,2},{2,3},{3,1},{1,0},{4,6},{6,7},{7,5},{5,4},{8,10},{10,11},{11... | collective-permute-start | bytes 1179656 | tf_op jit(solution)/shard_map/ppermute | solution.py:332
  9.7 7.6 %collective-permute-start.3 = (bf16[16,128]{1,0:T(8,128)(2,1)S(1)}, bf16[16,128]{1,0:T(8,128)(2,1)S(1)}, u32[]{:S(2)}, u32[]{:S(2)}) collective-permute-start(bf16[16,128]{1,0:T(8,128)(2,1)S(1)} %pad.16), channel_id=1, source_target_pairs={{2,0},{3,2},{1,3},{0,1},{6,4},{7,6},{5,7},{4,5},{10,8},{11,10},{9,... | collective-permute-start | bytes 12296 | tf_op jit(solution)/shard_map/ppermute | solution.py:321
  17.3 31.8 %copy-start.8 = (bf16[16,128]{1,0:T(8,128)(2,1)}, bf16[16,128]{1,0:T(8,128)(2,1)S(1)}, u32[]{:S(2)}) copy-start(bf16[16,128]{1,0:T(8,128)(2,1)S(1)} %collective-permute-done.3.refs_3_) | copy-start | bytes 12292
  17.3 12.6 %collective-permute-start = (bf16[1552,128]{1,0:T(8,128)(2,1)S(1)}, bf16[1552,128]{1,0:T(8,128)(2,1)S(1)}, u32[]{:S(2)}, u32[]{:S(2)}) collective-permute-start(bf16[1552,128]{1,0:T(8,128)(2,1)S(1)} %pad_maximum_fusion.1), channel_id=1, source_target_pairs={{0,2},{2,3},{3,1},{1,0},{4,6},{6,7},{7,5},{5,4},{8,10},{10,11},{11... | collective-permute-start | bytes 1191944 | tf_op jit(solution)/shard_map/ppermute | solution.py:331
  19.7 27.0 %copy-start.7 = (bf16[1536,128]{1,0:T(8,128)(2,1)}, bf16[1536,128]{1,0:T(8,128)(2,1)S(1)}, u32[]{:S(2)}) copy-start(bf16[1536,128]{1,0:T(8,128)(2,1)S(1)} %collective-permute-done.4.refs_7_.refs_3_) | copy-start | bytes 1179652
  19.7 21.7 %collective-permute-start.5 = (bf16[1536,128]{1,0:T(8,128)(2,1)S(1)}, bf16[1536,128]{1,0:T(8,128)(2,1)}, u32[]{:S(2)}, u32[]{:S(2)}) collective-permute-start(bf16[1536,128]{1,0:T(8,128)(2,1)S(1)} %collective-permute-done.4.refs_7_.refs_3_), channel_id=1, source_target_pairs={{0,2},{2,3},{3,1},{1,0},{4,6},{6,7},{7,5},{5,4},{8,10},{10,11},{11... | collective-permute-start | bytes 1179656 | tf_op jit(solution)/shard_map/ppermute | solution.py:332
  24.4 24.7 %copy-start.3 = (bf16[3088,128]{1,0:T(8,128)(2,1)}, bf16[3088,128]{1,0:T(8,128)(2,1)S(1)}, u32[]{:S(2)}) copy-start(bf16[3088,128]{1,0:T(8,128)(2,1)S(1)} %collective-permute-done.10.refs_15_.refs_13_) | copy-start | bytes 2371588
  24.4 22.3 %collective-permute-start.11 = (bf16[3088,128]{1,0:T(8,128)(2,1)S(1)}, bf16[3088,128]{1,0:T(8,128)(2,1)S(1)}, u32[]{:S(2)}, u32[]{:S(2)}) collective-permute-start(bf16[3088,128]{1,0:T(8,128)(2,1)S(1)} %collective-permute-done.10.refs_15_.refs_13_), channel_id=1, source_target_pairs={{0,4},{4,0},{8,12},{12,8},{16,20},{20,16},{24,28},{28,24},{1,5},{5... | collective-permute-start | bytes 2371592 | tf_op jit(solution)/shard_map/ppermute | solution.py:317
  29.9 19.2 %copy-start.1 = (bf16[1552,128]{1,0:T(8,128)(2,1)}, bf16[1552,128]{1,0:T(8,128)(2,1)S(1)}, u32[]{:S(2)}) copy-start(bf16[1552,128]{1,0:T(8,128)(2,1)S(1)} %collective-permute-done.refs_1_.refs_5_) | copy-start | bytes 1191940
  29.9 14.3 %collective-permute-start.1 = (bf16[1552,128]{1,0:T(8,128)(2,1)S(1)}, bf16[1552,128]{1,0:T(8,128)(2,1)S(1)}, u32[]{:S(2)}, u32[]{:S(2)}) collective-permute-start(bf16[1552,128]{1,0:T(8,128)(2,1)S(1)} %collective-permute-done.refs_1_.refs_5_), channel_id=1, source_target_pairs={{0,2},{2,3},{3,1},{1,0},{4,6},{6,7},{7,5},{5,4},{8,10},{10,11},{11... | collective-permute-start | bytes 1191944 | tf_op jit(solution)/shard_map/ppermute | solution.py:331
  40.9 8.2 %collective-permute-start.6 = (bf16[3088,128]{1,0:T(8,128)(2,1)S(1)}, bf16[3088,128]{1,0:T(8,128)(2,1)}, u32[]{:S(2)}, u32[]{:S(2)}) collective-permute-start(bf16[3088,128]{1,0:T(8,128)(2,1)S(1)} %pad_maximum_fusion.refs_0_.refs_4_.refs_9_.refs_7_), channel_id=1, source_target_pairs={{0,4},{4,0},{8,12},{12,8},{16,20},{20,16},{24,28},{28,24},{1,5},{5... | collective-permute-start | bytes 2371592 | tf_op jit(solution)/shard_map/ppermute | solution.py:317
  40.9 8.3 %copy-start.4 = (bf16[3088,128]{1,0:T(8,128)(2,1)}, bf16[3088,128]{1,0:T(8,128)(2,1)S(1)}, u32[]{:S(2)}) copy-start(bf16[3088,128]{1,0:T(8,128)(2,1)S(1)} %collective-permute-done.8.refs_13_.refs_11_) | copy-start | bytes 2371588
  40.9 8.2 %collective-permute-start.9 = (bf16[3088,128]{1,0:T(8,128)(2,1)S(1)}, bf16[3088,128]{1,0:T(8,128)(2,1)}, u32[]{:S(2)}, u32[]{:S(2)}) collective-permute-start(bf16[3088,128]{1,0:T(8,128)(2,1)S(1)} %collective-permute-done.8.refs_13_.refs_11_), channel_id=1, source_target_pairs={{0,4},{4,0},{8,12},{12,8},{16,20},{20,16},{24,28},{28,24},{1,5},{5... | collective-permute-start | bytes 2371592 | tf_op jit(solution)/shard_map/ppermute | solution.py:317
  41.4 7.7 %collective-permute-start.7 = (bf16[3088,128]{1,0:T(8,128)(2,1)}, bf16[3088,128]{1,0:T(8,128)(2,1)}, u32[]{:S(2)}, u32[]{:S(2)}) collective-permute-start(bf16[3088,128]{1,0:T(8,128)(2,1)} %collective-permute-done.2.refs_11_.refs_9_), channel_id=1, source_target_pairs={{0,4},{4,0},{8,12},{12,8},{16,20},{20,16},{24,28},{28,24},{1,5},{5... | collective-permute-start | bytes 2371592 | tf_op jit(solution)/shard_map/ppermute | solution.py:317
  44.2 5.0 %copy-start.2 = (bf16[1552,128]{1,0:T(8,128)(2,1)}, bf16[1552,128]{1,0:T(8,128)(2,1)S(1)}, u32[]{:S(2)}) copy-start(bf16[1552,128]{1,0:T(8,128)(2,1)S(1)} %collective-permute-done.1.refs_2_.refs_6_) | copy-start | bytes 1191940
  44.2 17.7 %collective-permute-start.12 = (bf16[1552,128]{1,0:T(8,128)(2,1)S(1)}, bf16[1552,128]{1,0:T(8,128)(2,1)}, u32[]{:S(2)}, u32[]{:S(2)}) collective-permute-start(bf16[1552,128]{1,0:T(8,128)(2,1)S(1)} %collective-permute-done.1.refs_2_.refs_6_), channel_id=1, source_target_pairs={{0,2},{2,3},{3,1},{1,0},{4,6},{6,7},{7,5},{5,4},{8,10},{10,11},{11... | collective-permute-start | bytes 1191944 | tf_op jit(solution)/shard_map/ppermute | solution.py:331
  46.7 0.9 %copy-start.5 = (bf16[3088,128]{1,0:T(8,128)(2,1)}, bf16[3088,128]{1,0:T(8,128)(2,1)S(1)}, u32[]{:S(2)}) copy-start(bf16[3088,128]{1,0:T(8,128)(2,1)S(1)} %collective-permute-done.11.refs_16_.refs_14_) | copy-start | bytes 2371588
  47.6 14.2 %collective-permute-start.13 = (bf16[1536,128]{1,0:T(8,128)(2,1)}, bf16[1536,128]{1,0:T(8,128)(2,1)}, u32[]{:S(2)}, u32[]{:S(2)}) collective-permute-start(bf16[1536,128]{1,0:T(8,128)(2,1)} %collective-permute-done.5.refs_8_.refs_4_), channel_id=1, source_target_pairs={{0,2},{2,3},{3,1},{1,0},{4,6},{6,7},{7,5},{5,4},{8,10},{10,11},{11... | collective-permute-start | bytes 1179656 | tf_op jit(solution)/shard_map/ppermute | solution.py:332

commit v4 on v0

v4 whole, which is shorter than its diff:
```python
import functools

import jax
import jax.numpy as jnp
import numpy as np
from jax import lax
from jax.experimental import pallas as pl
from jax.experimental.pallas import tpu as pltpu
from jax.sharding import PartitionSpec as P

RING = (0, 2, 3, 1)
SMEM = pl.BlockSpec(memory_space=pltpu.SMEM)
VMEM = pl.BlockSpec(memory_space=pltpu.VMEM)
HBM = pl.BlockSpec(memory_space=pl.ANY)
UNROLL = 4
TAIL = 16
VMEM_BYTES = 60 * 1024 * 1024
FIELDS = dict(closes=1, opens=1, result=10, left_row=5, left_buf=5, right_row=5, right_buf=4)


def put(**values):
    code, shift = jnp.int32(0), 0
    for field, bits in FIELDS.items():
        if field in values:
            code = code + (values[field] << shift if shift else values[field])
        shift += bits
    return code


def get(code, field):
    shift = 0
    for name, bits in FIELDS.items():
        if name == field:
            return (code >> shift) & ((1 << bits) - 1)
        shift += bits


def pick(index, low, high, act):
    if high - low == 1:
        act(low)
        return
    middle = (low + high) // 2

    @pl.when(index < middle)
    def _():
        pick(index, low, middle, act)

    @pl.when(index >= middle)
    def _():
        pick(index, middle, high, act)


def fetch(t, code, a_bufs, b_bufs, left, right, load_sem):
    size = left.shape[1]
    for side, (bufs, dst, name) in enumerate(((a_bufs, left, "left"), (b_bufs, right, "right"))):
        start = pl.multiple_of(get(code, name + "_row") * size, size)

        def act(b):
            source = bufs[b].at[pl.ds(start, size)]
            pltpu.make_async_copy(source, dst.at[t], load_sem.at[t // UNROLL]).start()

        pick(get(code, name + "_buf"), 0, len(bufs), act)


def store(source, out, r, sem):
    results = out.shape[1]
    return pltpu.make_async_copy(source, out.at[r // results, r % results], sem)


def multiply(count, codes, out, left, right, total, result, load_sem, store_sem):
    bs = out.shape[-1]

    def some_terms(step, carry):
        ids = [step * UNROLL + u for u in range(UNROLL)]
        for t in ids:
            @pl.when(t < count)
            def _():
                for dst in (left, right):
                    pltpu.make_async_copy(dst.at[t], dst.at[t], load_sem.at[step]).wait()

        so_far = total[...]
        for t in ids:
            b_re, b_im = right[t, :bs], right[t, bs:]
            lhs = jnp.concatenate([left[t, :bs], left[t, bs:]], axis=1)
            rhs = jnp.concatenate(
                [
                    jnp.concatenate([b_re, b_im], axis=1),
                    jnp.concatenate([-b_im, b_re], axis=1),
                ],
                axis=0,
            )
            product = jnp.dot(lhs, rhs, preferred_element_type=jnp.float32)
            so_far = jnp.where(get(codes(t), "opens") > 0, product, so_far + product)
            for part in range(2):
                result[t, part] = so_far[:, part * bs : (part + 1) * bs].astype(result.dtype)
        total[...] = so_far
        for t in ids:
            code = codes(t)

            @pl.when((t < count) & (get(code, "closes") > 0))
            def _():
                store(result.at[t], out, get(code, "result"), store_sem).start()

        return carry

    lax.fori_loop(0, (count + UNROLL - 1) // UNROLL, some_terms, 0)

    def drain(t, carry):
        code = codes(t)

        @pl.when(get(code, "closes") > 0)
        def _():
            store(result.at[t], out, get(code, "result"), store_sem).wait()

        return carry

    lax.fori_loop(0, count, drain, 0)


def early_kernel(sizes, n_a, n_b, tables, c_cols, c_keep, *refs):
    rows, n_section, n_rows, panel_width, n_early, half = sizes
    strips, refs = refs[:n_section], refs[n_section:]
    a_bufs, b_bufs = refs[:n_a], refs[n_a : n_a + n_b]
    (
        out, late_codes, codes, empty, tails, table, numbers, scalars, zeros, sem, *scratch
    ) = refs[n_a + n_b :]
    left, right, _, _, load_sem, store_sem = scratch
    pieces_at = n_section
    wanted_at = pieces_at + n_rows
    keep_at = wanted_at + rows
    lookup_at = keep_at + rows
    results = c_cols.shape[1]
    me = lax.axis_index("rows") * n_section + lax.axis_index("section")
    copies = [pltpu.make_async_copy(tables.at[me], table, sem.at[0])]
    sources = [*strips, *b_bufs]
    for n, source in enumerate(sources):
        tail = source.at[pl.ds(source.shape[0] - TAIL, TAIL)]
        copies.append(pltpu.make_async_copy(tail, tails.at[n], sem.at[1]))
    for copy in copies:
        copy.start()
    zeros[...] = jnp.zeros_like(zeros)
    numbers[wanted_at : wanted_at + rows, :results] = jnp.where(c_keep[...] > 0, c_cols[...], -2)
    for copy in copies:
        copy.wait()
    for n in range(len(sources)):
        numbers[n : n + 1] = tails[n].astype(jnp.float32)[:1].astype(jnp.int32)
    numbers[lookup_at : lookup_at + table.shape[0]] = table[...]
    to_scalars = pltpu.make_async_copy(numbers, scalars, sem.at[0])
    to_scalars.start()
    to_scalars.wait()
    lanes = numbers.shape[1]

    def lookup(n):
        return scalars[lookup_at + n // lanes, n % lanes]

    def one_row(i, counts):
        in_upper = i >= half
        columns, lates, parts = [], [], []
        for a in range(n_section):
            col = scalars[lookup(3 * n_section + a), i]
            k = jnp.maximum(a * panel_width + col, 0)
            group = k // rows
            inside = k - group * rows
            piece = scalars[lookup_at + (4 * n_section) // lanes, (4 * n_section) % lanes + group]
            columns.append(jnp.where(col >= 0, scalars[pieces_at + piece, inside], -1))
            buf = jnp.where(in_upper, lookup(n_section + a), lookup(a))
            lates.append((buf >= n_early).astype(jnp.int32))
            row = i - jnp.where(in_upper, lookup(2 * n_section + a), 0)
            parts.append(put(left_buf=buf, left_row=row, right_buf=piece, right_row=inside))
        n_now, n_late = counts
        for c in range(results):
            r = i * results + c
            wanted = scalars[wanted_at + i, c]
            matches = [(column == wanted).astype(jnp.int32) for column in columns]
            n_matches = sum(matches)
            late = functools.reduce(jnp.maximum, [m * l for m, l in zip(matches, lates)])
            empty[r] = n_matches

            @pl.when(n_matches == 0)
            def _():
                store(zeros, out, r, store_sem).start()

            @pl.when(n_matches > 0)
            def _():
                seen = jnp.int32(0)
                for m, part in zip(matches, parts):
                    @pl.when(m > 0)
                    def _():
                        opens = (seen == 0).astype(jnp.int32)
                        closes = (seen == n_matches - 1).astype(jnp.int32)
                        code = part + put(result=r, opens=opens, closes=closes)

                        @pl.when(late > 0)
                        def _():
                            late_codes[1 + n_late + seen] = code

                        @pl.when(late == 0)
                        def _():
                            codes[n_now + seen] = code
                            fetch(n_now + seen, code, a_bufs, b_bufs, left, right, load_sem)

                    seen = seen + m

            n_late = n_late + n_matches * late
            n_now = n_now + n_matches * (1 - late)
        return n_now, n_late

    n_now, n_late = lax.fori_loop(0, rows, one_row, (jnp.int32(0), jnp.int32(0)))
    late_codes[0] = n_late
    multiply(n_now, lambda t: codes[t], out, *scratch)

    def drain(r, carry):
        @pl.when(empty[r] == 0)
        def _():
            store(zeros, out, r, store_sem).wait()

        return carry

    lax.fori_loop(0, rows * results, drain, 0)


def late_kernel(n_a, n_b, codes, *refs):
    a_bufs, b_bufs = refs[:n_a], refs[n_a : n_a + n_b]
    out, *scratch = refs[n_a + n_b + 1 :]
    left, right, _, _, load_sem, _ = scratch

    def one(t, carry):
        fetch(t, codes[1 + t], a_bufs, b_bufs, left, right, load_sem)
        return carry

    lax.fori_loop(0, codes[0], one, 0)
    multiply(codes[0], lambda t: codes[1 + t], out, *scratch)


def scratch_for(most, bs):
    return [
        pltpu.VMEM((most, 2 * bs, bs), jnp.bfloat16),
        pltpu.VMEM((most, 2 * bs, bs), jnp.bfloat16),
        pltpu.VMEM((bs, 2 * bs), jnp.float32),
        pltpu.VMEM((most, 2, bs, bs), jnp.bfloat16),
        pltpu.SemaphoreType.DMA((most // UNROLL,)),
        pltpu.SemaphoreType.DMA,
    ]


def multiply_early(sizes, tables, c_cols, c_keep, strips, a_bufs, b_bufs, out_shape):
    rows, n_section, n_rows = sizes[:3]
    operands = [*strips, *a_bufs, *b_bufs]
    bs, n_results = out_shape[-1], c_cols.size
    most = rows * n_section + -(rows * n_section) % UNROLL
    n_tails = n_section + n_rows
    n_numbers = n_tails + 2 * rows + tables.shape[1]
    return pl.pallas_call(
        functools.partial(early_kernel, sizes, len(a_bufs), len(b_bufs)),
        out_shape=(
            jax.ShapeDtypeStruct(out_shape, jnp.bfloat16),
            jax.ShapeDtypeStruct((1 + most,), jnp.int32),
        ),
        in_specs=[HBM, VMEM, VMEM] + [HBM] * len(operands),
        out_specs=(HBM, SMEM),
        scratch_shapes=[
            pltpu.SMEM((most,), jnp.int32),
            pltpu.SMEM((n_results,), jnp.int32),
            pltpu.VMEM((n_tails, TAIL, bs), jnp.bfloat16),
            pltpu.VMEM(tables.shape[1:], jnp.int32),
            pltpu.VMEM((n_numbers, bs), jnp.int32),
            pltpu.SMEM((n_numbers, bs), jnp.int32),
            pltpu.VMEM((2, bs, bs), jnp.bfloat16),
            pltpu.SemaphoreType.DMA((2,)),
            *scratch_for(most, bs),
        ],
        compiler_params=pltpu.CompilerParams(vmem_limit_bytes=VMEM_BYTES),
        cost_estimate=pl.CostEstimate(flops=1000, bytes_accessed=1000, transcendentals=0),
    )(tables, c_cols, c_keep, *operands)


def multiply_late(codes, a_bufs, b_bufs, so_far):
    operands = [codes, *a_bufs, *b_bufs, so_far]
    return pl.pallas_call(
        functools.partial(late_kernel, len(a_bufs), len(b_bufs)),
        out_shape=jax.ShapeDtypeStruct(so_far.shape, so_far.dtype),
        in_specs=[SMEM] + [HBM] * (len(operands) - 1),
        out_specs=HBM,
        scratch_shapes=scratch_for(codes.shape[0] - 1, so_far.shape[-1]),
        input_output_aliases={len(operands) - 1: 0},
        compiler_params=pltpu.CompilerParams(vmem_limit_bytes=VMEM_BYTES),
    )(*operands)


def on_device(x_blocks, x_cols, c_cols, c_keep):
    n_rows = lax.axis_size("rows")
    n_section = lax.axis_size("section")
    rows, bs = x_blocks.shape[0], x_blocks.shape[-1]
    panel_width = rows * n_rows // n_section
    half = rows // 2
    blocks, columns = x_blocks.reshape(-1, bs), x_cols.reshape(-1)
    everyone = [(r, s) for r in range(n_rows) for s in range(n_section)]
    tail = jnp.pad(columns.astype(blocks.dtype)[None], ((0, TAIL - 1), (0, bs - rows)))
    mine = jnp.concatenate([blocks, tail])

    if (n_rows, n_section) == (8, 4):
        swap = lambda x, m: lax.ppermute(x, "rows", [(r, r ^ m) for r in range(n_rows)])

        pairs = [(RING[i], RING[(i + 1) % 4]) for i in range(4)]
        step = lambda x: lax.ppermute(x, "section", pairs)
        half = 3
        middle = half * 2 * bs
        small, big = [jnp.concatenate([blocks[:middle], tail])], [blocks[middle:]]
        small.append(step(small[0]))
        big.append(step(big[0]))
        for_across = own = mine
        for_across, small[1] = lax.optimization_barrier((mine, small[1]))
        for _ in range(2):
            small.append(step(small[-1]))
            big.append(step(big[-1]))

        came = [swap(mine, 2), swap(mine, 4), swap(for_across, 6)]
        b_bufs = []
        for x in [own, *came]:
            b_bufs += [x, swap(x, 1)]
        a_bufs = [mine, *small[1:], *big[1:]]
        n_early = 6
        strips = [mine, *small[1:]]

        steps = lambda s, a: (RING.index(s) - RING.index(a)) % 4
        tables = [
            [steps(s, a) for a in range(4)]
            + [(0, 4, 5, 6)[steps(s, a)] for a in range(4)]
            + [(0, half, half, half)[steps(s, a)] for a in range(4)]
            + [steps(s, a) for a in range(4)]
            + [g ^ r for g in range(8)]
            for r, s in everyone
        ]
    else:

        def shifts(x, axis, n):
            shift = lambda d: lax.ppermute(x, axis, [(p, (p + d) % n) for p in range(n)])
            return [x] + [shift(d) for d in range(1, n)]

        a_bufs, b_bufs = shifts(mine, "section", n_section), shifts(mine, "rows", n_rows)
        n_early, strips = n_section, a_bufs
        tables = []
        for r, s in everyone:
            panels = [(s - a) % n_section for a in range(n_section)]
            groups = [(r - g) % n_rows for g in range(n_rows)]
            tables.append(panels * 2 + [0] * n_section + panels + groups)

    tables = np.array(tables, np.int32)
    tables = np.pad(tables, ((0, 0), (0, -tables.shape[1] % (8 * bs)))).reshape(len(everyone), -1, bs)
    sizes = (rows, n_section, n_rows, panel_width, n_early, half)
    out_shape = (rows, c_cols.shape[1], *x_blocks.shape[2:])
    out, codes = multiply_early(
        sizes, jnp.asarray(tables), c_cols, c_keep, strips, a_bufs[:n_early], b_bufs, out_shape
    )
    if n_early < len(a_bufs):
        out = multiply_late(codes, a_bufs, b_bufs, out)
    return out


def solution(mesh):
    in_specs = (
        P("rows", "section", None, None, None),
        P("rows", "section"),
        P("rows", "section"),
        P("rows", "section"),
    )
    out_specs = P("rows", "section", None, None, None)
    return jax.shard_map(
        on_device, mesh=mesh, in_specs=in_specs, out_specs=out_specs, check_vma=False
    )
```

time: 156 us -> 65.1 us (0.42)
  waiting for transfers between devices: 80.4 us -> 25.4 us
  starting transfers between devices: 0.04 us -> 24.3 us
  blocking collectives: 20.8 us -> 0 us
  local copies, waits for them, and re-layouts: 19.8 us -> 3.46 us
  between operations: 14.1 us -> 0.16 us
  matrix products: 13.3 us -> 0 us
  Pallas kernels: 0 us -> 10.3 us
  other arithmetic: 7.15 us -> 0.8 us
    all_gather x2 -> x0, waiting for transfers between devices: 79 us -> none  [the longest x1 54.4 us: on_device(): lax.all_gather(x_blocks, 'section', axis=1, tiled=True)]
    ppermute x0 -> x13, waiting for transfers between devices: none -> 25.4 us  [the longest x6 24.3 us: on_device(): step = lambda x: lax.ppermute(x, 'section', pairs)]
    ppermute x0 -> x13, starting transfers between devices: none -> 24.3 us  [the longest x6 18.7 us: on_device(): step = lambda x: lax.ppermute(x, 'section', pairs)]
    all_gather x2 -> x0, blocking collectives: 20.8 us -> none  [the longest x1 12.7 us: on_device(): lax.all_gather(x_cols, 'section', axis=1, tiled=True)]
    dot_general x3 -> x0, matrix products: 13.3 us -> none  [the longest x1 8.85 us: contribute(): jnp.einsum('ialc,ialrxz->icrxz', matched.astype(jnp.float32), terms, prec...]
    pallas_call x0 -> x2, Pallas kernels: none -> 10.3 us  [the longest x1 7.61 us: multiply_early(): pl.pallas_call(functools.partial(early_kernel, sizes, len(a_bufs), len(b_...]
    another operation x1 -> x0, local copies, waits for them, and re-layouts: 7.6 us -> none
    gather x3 -> x0, local copies, waits for them, and re-layouts: 7.51 us -> none  [the longest x2 6.73 us: contribute(): b_blocks[row_index]]
  transfers between devices with their start and end apart: 2 -> 13, of which waited for: 2 -> 5; matrix products, arithmetic and copies ran while one was open for 9% -> 4% of each run, Pallas kernels for 0% -> 12%
where the time goes in v4:
time: 65.1 us; the launch traced here: 64.5 us
  waiting for transfers between devices  25.4 us (39%)
  starting transfers between devices  24.3 us (37%)
  Pallas kernels  10.3 us (16%)
  local copies, waits for them, and re-layouts  3.46 us (5%)
  other arithmetic  0.8 us (1%)
    ppermute x6, waiting for transfers between devices, on_device(): step = lambda x: lax.ppermute(x, 'section', pairs)  24.3 us
    ppermute x6, starting transfers between devices, on_device(): step = lambda x: lax.ppermute(x, 'section', pairs)  18.7 us
    pallas_call x1, Pallas kernels, multiply_early(): pl.pallas_call(functools.partial(early_kernel, sizes, len(a_bufs), len(b_...  7.61 us
    ppermute x7, starting transfers between devices, on_device(): lax.ppermute(x, 'rows', [(r, r ^ m) for r in range(n_rows)])  5.63 us
    pallas_call x1, Pallas kernels, multiply_late(): pl.pallas_call(functools.partial(late_kernel, len(a_bufs), len(b_bufs)),...  2.74 us
    slice x2, local copies, waits for them, and re-layouts, on_device(): small, big = ([jnp.concatenate([blocks[:middle], tail])], [blocks[middle:]])  2.04 us
    unnamed x24, local copies, waits for them, and re-layouts  1.41 us
  transfers between devices with their start and end apart: 13, of which 5 were waited for; matrix products, arithmetic and copies ran while one was open for 4% of the time, Pallas kernels for 12%

profile of v4, /device:TPU:0, one launch (start us, length us, event | category | flops | bytes accessed | tf_op | source)
XLA Modules:
  0.0 64.5 jit_solution(6222821464301164635)
XLA Ops:
  0.0 0.7 %convert_bitcast_fusion = bf16[1,12]{1,0:T(2,128)(2,1)S(1)} fusion(s32[12,1]{0,1:T(1,128)} %param.6), kind=kLoop, calls=%fused_computation.2 | loop fusion | flops 12 | bytes 72 | tf_op jit(solution)/shard_map/convert_element_type | solution.py:298
  0.7 0.9 %slice.12 = bf16[3,1,2,128,128]{4,3,2,1,0:T(8,128)(2,1)S(1)} slice(bf16[12,1,2,128,128]{4,3,2,1,0:T(8,128)(2,1)} %param.5), slice={[0:3], [0:1], [0:2], [0:128], [0:128]} | slice | bytes 393216 | tf_op jit(solution)/shard_map/slice | solution.py:308
  1.7 0.0 copy-start.9
  1.7 0.0 copy-start.10
  1.7 4.1 %collective-permute-start = (bf16[784,128]{1,0:T(8,128)(2,1)S(1)}, bf16[784,128]{1,0:T(8,128)(2,1)S(1)}, u32[]{:S(2)}, u32[]{:S(2)}) collective-permute-start(bf16[784,128]{1,0:T(8,128)(2,1)S(1)} %pad_maximum_fusion.1), channel_id=1, source_target_pairs={{0,2},{2,3},{3,1},{1,0},{4,6},{6,7},{7,5},{5,4},{8,10},{10,11},{11... | collective-permute-start | bytes 602120 | tf_op jit(solution)/shard_map/ppermute | solution.py:305
  5.8 1.1 %slice.14 = bf16[9,1,2,128,128]{4,3,2,1,0:T(8,128)(2,1)S(1)} slice(bf16[12,1,2,128,128]{4,3,2,1,0:T(8,128)(2,1)} %param.5), slice={[3:12], [0:1], [0:2], [0:128], [0:128]} | slice | bytes 1179648 | tf_op jit(solution)/shard_map/slice | solution.py:308
  6.9 1.6 %collective-permute-start.3 = (bf16[2304,128]{1,0:T(8,128)(2,1)S(1)}, bf16[2304,128]{1,0:T(8,128)(2,1)S(1)}, u32[]{:S(2)}, u32[]{:S(2)}) collective-permute-start(bf16[2304,128]{1,0:T(8,128)(2,1)S(1)} %bitcast.7), channel_id=1, source_target_pairs={{0,2},{2,3},{3,1},{1,0},{4,6},{6,7},{7,5},{5,4},{8,10},{10,11},{11... | collective-permute-start | bytes 1769480 | tf_op jit(solution)/shard_map/ppermute | solution.py:305
  8.6 0.1 pad_maximum_fusion.refs_0_.refs_4_.refs_10_.refs_7_
  8.6 1.6 %collective-permute-start.8 = (bf16[3088,128]{1,0:T(8,128)(2,1)S(1)}, bf16[3088,128]{1,0:T(8,128)(2,1)S(1)}, u32[]{:S(2)}, u32[]{:S(2)}) collective-permute-start(bf16[3088,128]{1,0:T(8,128)(2,1)S(1)} %pad_maximum_fusion.refs_0_.refs_4_.refs_10_.refs_7_), channel_id=1, source_target_pairs={{0,16},{4,20},{8,24},{12,28},{16,0},{20,4},{24,8},{28,12},{1,17},{... | collective-permute-start | bytes 2371592 | tf_op jit(solution)/shard_map/ppermute | solution.py:302
  10.2 1.5 %collective-permute-start.6 = (bf16[3088,128]{1,0:T(8,128)(2,1)S(1)}, bf16[3088,128]{1,0:T(8,128)(2,1)S(1)}, u32[]{:S(2)}, u32[]{:S(2)}) collective-permute-start(bf16[3088,128]{1,0:T(8,128)(2,1)S(1)} %pad_maximum_fusion.refs_0_.refs_4_.refs_10_.refs_7_), channel_id=1, source_target_pairs={{0,8},{4,12},{8,0},{12,4},{16,24},{20,28},{24,16},{28,20},{1,9},{5... | collective-permute-start | bytes 2371592 | tf_op jit(solution)/shard_map/ppermute | solution.py:302
  11.7 0.0 collective-permute-done.refs_1_.refs_5_
  11.7 2.0 %collective-permute-start.10 = (bf16[3088,128]{1,0:T(8,128)(2,1)S(1)}, bf16[3088,128]{1,0:T(8,128)(2,1)S(1)}, u32[]{:S(2)}, u32[]{:S(2)}) collective-permute-start(bf16[3088,128]{1,0:T(8,128)(2,1)S(1)} %pad_maximum_fusion.refs_0_.refs_4_.refs_10_.refs_7_), channel_id=1, source_target_pairs={{0,24},{4,28},{8,16},{12,20},{16,8},{20,12},{24,0},{28,4},{1,25},{... | collective-permute-start | bytes 2371592 | tf_op jit(solution)/shard_map/ppermute | solution.py:302
  13.7 3.4 %collective-permute-start.1 = (bf16[784,128]{1,0:T(8,128)(2,1)S(1)}, bf16[784,128]{1,0:T(8,128)(2,1)S(1)}, u32[]{:S(2)}, u32[]{:S(2)}) collective-permute-start(bf16[784,128]{1,0:T(8,128)(2,1)S(1)} %collective-permute-done.refs_1_.refs_5_), channel_id=1, source_target_pairs={{0,2},{2,3},{3,1},{1,0},{4,6},{6,7},{7,5},{5,4},{8,10},{10,11},{11... | collective-permute-start | bytes 602120 | tf_op jit(solution)/shard_map/ppermute | solution.py:305
  17.1 6.8 %collective-permute-done.3.refs_8_.refs_4_ = bf16[2304,128]{1,0:T(8,128)(2,1)S(1)} collective-permute-done((bf16[2304,128]{1,0:T(8,128)(2,1)S(1)}, bf16[2304,128]{1,0:T(8,128)(2,1)S(1)}, u32[]{:S(2)}, u32[]{:S(2)}) %collective-permute-start.3) | collective-permute-done | bytes 589856 | tf_op jit(solution)/shard_map/ppermute | solution.py:305
  23.9 3.4 %collective-permute-start.4 = (bf16[2304,128]{1,0:T(8,128)(2,1)S(1)}, bf16[2304,128]{1,0:T(8,128)(2,1)}, u32[]{:S(2)}, u32[]{:S(2)}) collective-permute-start(bf16[2304,128]{1,0:T(8,128)(2,1)S(1)} %collective-permute-done.3.refs_8_.refs_4_), channel_id=1, source_target_pairs={{0,2},{2,3},{3,1},{1,0},{4,6},{6,7},{7,5},{5,4},{8,10},{10,11},{11... | collective-permute-start | bytes 1769480 | tf_op jit(solution)/shard_map/ppermute | solution.py:305
  27.2 0.9 %collective-permute-done.1.refs_2_.refs_6_ = bf16[784,128]{1,0:T(8,128)(2,1)S(1)} collective-permute-done((bf16[784,128]{1,0:T(8,128)(2,1)S(1)}, bf16[784,128]{1,0:T(8,128)(2,1)S(1)}, u32[]{:S(2)}, u32[]{:S(2)}) %collective-permute-start.1) | collective-permute-done | bytes 200736 | tf_op jit(solution)/shard_map/ppermute | solution.py:305
  28.2 3.4 %collective-permute-start.2 = (bf16[784,128]{1,0:T(8,128)(2,1)S(1)}, bf16[784,128]{1,0:T(8,128)(2,1)S(1)}, u32[]{:S(2)}, u32[]{:S(2)}) collective-permute-start(bf16[784,128]{1,0:T(8,128)(2,1)S(1)} %collective-permute-done.1.refs_2_.refs_6_), channel_id=1, source_target_pairs={{0,2},{2,3},{3,1},{1,0},{4,6},{6,7},{7,5},{5,4},{8,10},{10,11},{11... | collective-permute-start | bytes 602120 | tf_op jit(solution)/shard_map/ppermute | solution.py:305
  31.5 12.4 %collective-permute-done.2.refs_3_.refs_7_ = bf16[784,128]{1,0:T(8,128)(2,1)S(1)} collective-permute-done((bf16[784,128]{1,0:T(8,128)(2,1)S(1)}, bf16[784,128]{1,0:T(8,128)(2,1)S(1)}, u32[]{:S(2)}, u32[]{:S(2)}) %collective-permute-start.2) | collective-permute-done | bytes 200736 | tf_op jit(solution)/shard_map/ppermute | solution.py:305
  44.0 0.0 collective-permute-start.5
  44.0 0.0 collective-permute-done.8.refs_14_.refs_11_
  44.0 0.5 collective-permute-start.9
  44.5 0.1 collective-permute-start.7
  44.6 1.1 %collective-permute-done.10.refs_16_.refs_13_ = bf16[3088,128]{1,0:T(8,128)(2,1)S(1)} collective-permute-done((bf16[3088,128]{1,0:T(8,128)(2,1)S(1)}, bf16[3088,128]{1,0:T(8,128)(2,1)S(1)}, u32[]{:S(2)}, u32[]{:S(2)}) %collective-permute-start.10) | collective-permute-done | bytes 790560 | tf_op jit(solution)/shard_map/ppermute | solution.py:302
  45.6 0.0 collective-permute-start.11
  45.6 0.0 collective-permute-done.4.refs_9_.refs_5_
  45.7 2.8 %collective-permute-start.12 = (bf16[2304,128]{1,0:T(8,128)(2,1)}, bf16[2304,128]{1,0:T(8,128)(2,1)}, u32[]{:S(2)}, u32[]{:S(2)}) collective-permute-start(bf16[2304,128]{1,0:T(8,128)(2,1)} %collective-permute-done.4.refs_9_.refs_5_), channel_id=1, source_target_pairs={{0,2},{2,3},{3,1},{1,0},{4,6},{6,7},{7,5},{5,4},{8,10},{10,11},{11... | collective-permute-start | bytes 1769480 | tf_op jit(solution)/shard_map/ppermute | solution.py:305
  48.5 0.7 %copy.7.c_cols = s32[12,3]{1,0:T(8,128)} copy(s32[12,3]{0,1:T(4,128)S(1)} %copy-done.9) | data formatting | bytes 288 | tf_op args[2]
  49.2 0.7 %copy.8.c_keep = s32[12,3]{1,0:T(8,128)} copy(s32[12,3]{0,1:T(4,128)S(1)} %copy-done.10) | data formatting | bytes 288 | tf_op args[3]
  49.9 0.0 collective-permute-done.5.refs_11_.refs_8_
  50.0 7.6 %shard_map.55 = (bf16[12,3,2,128,128]{4,3,2,1,0:T(8,128)(2,1)}, s32[49]{0:T(128)}) custom-call(s32[32,8,128]{2,1,0:T(8,128)} %constant.5.clone.tables, s32[12,3]{1,0:T(8,128)} %copy.7.c_cols, s32[12,3]{1,0:T(8,128)} %copy.8.c_keep, bf16[3088,128]{1,0:T(8,128)(2,1)} %copy-done, bf16[784,128]{1,0:T(8,128)(2,1)} %copy-done.6, bf16[784,128]{1,0:T(8,128)(2,1)} %copy-done.7, ...), custom_call_target="tpu_custom_call" | custom-call | flops 1000 | bytes 1000 | tf_op jit(solution)/shard_map/pallas_call | solution.py:253
  57.6 4.2 %collective-permute-done.12.refs_6_ = bf16[2304,128]{1,0:T(8,128)(2,1)} collective-permute-done((bf16[2304,128]{1,0:T(8,128)(2,1)}, bf16[2304,128]{1,0:T(8,128)(2,1)}, u32[]{:S(2)}, u32[]{:S(2)}) %collective-permute-start.12) | collective-permute-done | bytes 589856 | tf_op jit(solution)/shard_map/ppermute | solution.py:305
  61.8 2.7 %shard_map.56 = bf16[12,3,2,128,128]{4,3,2,1,0:T(8,128)(2,1)} custom-call(s32[49]{0:T(128)} %get-tuple-element.11.codes, bf16[3088,128]{1,0:T(8,128)(2,1)} %copy-done, bf16[784,128]{1,0:T(8,128)(2,1)} %copy-done.6, bf16[784,128]{1,0:T(8,128)(2,1)} %copy-done.7, bf16[784,128]{1,0:T(8,128)(2,1)} %copy-done.8, ...), custom_call_target="tpu_custom_call", output_to_operand_aliasing={{}: (16, {})} | custom-call | tf_op jit(solution)/shard_map/pallas_call | solution.py:279
  (26 shorter events, 0.1 us)
Async XLA Ops:
  0.0 8.6 %copy-start.4 = (bf16[12,1,2,128,128]{4,3,2,1,0:T(8,128)(2,1)S(1)}, bf16[12,1,2,128,128]{4,3,2,1,0:T(8,128)(2,1)}, u32[]{:S(2)}) copy-start(bf16[12,1,2,128,128]{4,3,2,1,0:T(8,128)(2,1)} %param.5) | copy-start | bytes 2359300
  1.7 46.8 %copy-start.9 = (s32[12,3]{0,1:T(4,128)S(1)}, s32[12,3]{0,1:T(4,128)}, u32[]{:S(2)}) copy-start(s32[12,3]{0,1:T(4,128)} %param.7) | copy-start | bytes 436
  1.7 47.5 %copy-start.10 = (s32[12,3]{0,1:T(4,128)S(1)}, s32[12,3]{0,1:T(4,128)}, u32[]{:S(2)}) copy-start(s32[12,3]{0,1:T(4,128)} %param.8) | copy-start | bytes 436
  1.7 10.0 %collective-permute-start = (bf16[784,128]{1,0:T(8,128)(2,1)S(1)}, bf16[784,128]{1,0:T(8,128)(2,1)S(1)}, u32[]{:S(2)}, u32[]{:S(2)}) collective-permute-start(bf16[784,128]{1,0:T(8,128)(2,1)S(1)} %pad_maximum_fusion.1), channel_id=1, source_target_pairs={{0,2},{2,3},{3,1},{1,0},{4,6},{6,7},{7,5},{5,4},{8,10},{10,11},{11... | collective-permute-start | bytes 602120 | tf_op jit(solution)/shard_map/ppermute | solution.py:305
  6.9 16.9 %collective-permute-start.3 = (bf16[2304,128]{1,0:T(8,128)(2,1)S(1)}, bf16[2304,128]{1,0:T(8,128)(2,1)S(1)}, u32[]{:S(2)}, u32[]{:S(2)}) collective-permute-start(bf16[2304,128]{1,0:T(8,128)(2,1)S(1)} %bitcast.7), channel_id=1, source_target_pairs={{0,2},{2,3},{3,1},{1,0},{4,6},{6,7},{7,5},{5,4},{8,10},{10,11},{11... | collective-permute-start | bytes 1769480 | tf_op jit(solution)/shard_map/ppermute | solution.py:305
  8.6 41.3 %copy-start = (bf16[3088,128]{1,0:T(8,128)(2,1)}, bf16[3088,128]{1,0:T(8,128)(2,1)S(1)}, u32[]{:S(2)}) copy-start(bf16[3088,128]{1,0:T(8,128)(2,1)S(1)} %pad_maximum_fusion.refs_0_.refs_4_.refs_10_.refs_7_) | copy-start | bytes 2371588
  8.6 35.3 %collective-permute-start.8 = (bf16[3088,128]{1,0:T(8,128)(2,1)S(1)}, bf16[3088,128]{1,0:T(8,128)(2,1)S(1)}, u32[]{:S(2)}, u32[]{:S(2)}) collective-permute-start(bf16[3088,128]{1,0:T(8,128)(2,1)S(1)} %pad_maximum_fusion.refs_0_.refs_4_.refs_10_.refs_7_), channel_id=1, source_target_pairs={{0,16},{4,20},{8,24},{12,28},{16,0},{20,4},{24,8},{28,12},{1,17},{... | collective-permute-start | bytes 2371592 | tf_op jit(solution)/shard_map/ppermute | solution.py:302
  10.2 34.3 %collective-permute-start.6 = (bf16[3088,128]{1,0:T(8,128)(2,1)S(1)}, bf16[3088,128]{1,0:T(8,128)(2,1)S(1)}, u32[]{:S(2)}, u32[]{:S(2)}) collective-permute-start(bf16[3088,128]{1,0:T(8,128)(2,1)S(1)} %pad_maximum_fusion.refs_0_.refs_4_.refs_10_.refs_7_), channel_id=1, source_target_pairs={{0,8},{4,12},{8,0},{12,4},{16,24},{20,28},{24,16},{28,20},{1,9},{5... | collective-permute-start | bytes 2371592 | tf_op jit(solution)/shard_map/ppermute | solution.py:302
  11.7 38.2 %copy-start.6 = (bf16[784,128]{1,0:T(8,128)(2,1)}, bf16[784,128]{1,0:T(8,128)(2,1)S(1)}, u32[]{:S(2)}) copy-start(bf16[784,128]{1,0:T(8,128)(2,1)S(1)} %collective-permute-done.refs_1_.refs_5_) | copy-start | bytes 602116
  11.7 33.9 %collective-permute-start.10 = (bf16[3088,128]{1,0:T(8,128)(2,1)S(1)}, bf16[3088,128]{1,0:T(8,128)(2,1)S(1)}, u32[]{:S(2)}, u32[]{:S(2)}) collective-permute-start(bf16[3088,128]{1,0:T(8,128)(2,1)S(1)} %pad_maximum_fusion.refs_0_.refs_4_.refs_10_.refs_7_), channel_id=1, source_target_pairs={{0,24},{4,28},{8,16},{12,20},{16,8},{20,12},{24,0},{28,4},{1,25},{... | collective-permute-start | bytes 2371592 | tf_op jit(solution)/shard_map/ppermute | solution.py:302
  13.7 14.5 %collective-permute-start.1 = (bf16[784,128]{1,0:T(8,128)(2,1)S(1)}, bf16[784,128]{1,0:T(8,128)(2,1)S(1)}, u32[]{:S(2)}, u32[]{:S(2)}) collective-permute-start(bf16[784,128]{1,0:T(8,128)(2,1)S(1)} %collective-permute-done.refs_1_.refs_5_), channel_id=1, source_target_pairs={{0,2},{2,3},{3,1},{1,0},{4,6},{6,7},{7,5},{5,4},{8,10},{10,11},{11... | collective-permute-start | bytes 602120 | tf_op jit(solution)/shard_map/ppermute | solution.py:305
  23.9 21.8 %copy-start.5 = (bf16[2304,128]{1,0:T(8,128)(2,1)}, bf16[2304,128]{1,0:T(8,128)(2,1)S(1)}, u32[]{:S(2)}) copy-start(bf16[2304,128]{1,0:T(8,128)(2,1)S(1)} %collective-permute-done.3.refs_8_.refs_4_) | copy-start | bytes 1769476
  23.9 21.8 %collective-permute-start.4 = (bf16[2304,128]{1,0:T(8,128)(2,1)S(1)}, bf16[2304,128]{1,0:T(8,128)(2,1)}, u32[]{:S(2)}, u32[]{:S(2)}) collective-permute-start(bf16[2304,128]{1,0:T(8,128)(2,1)S(1)} %collective-permute-done.3.refs_8_.refs_4_), channel_id=1, source_target_pairs={{0,2},{2,3},{3,1},{1,0},{4,6},{6,7},{7,5},{5,4},{8,10},{10,11},{11... | collective-permute-start | bytes 1769480 | tf_op jit(solution)/shard_map/ppermute | solution.py:305
  28.2 17.5 %copy-start.7 = (bf16[784,128]{1,0:T(8,128)(2,1)}, bf16[784,128]{1,0:T(8,128)(2,1)S(1)}, u32[]{:S(2)}) copy-start(bf16[784,128]{1,0:T(8,128)(2,1)S(1)} %collective-permute-done.1.refs_2_.refs_6_) | copy-start | bytes 602116
  28.2 15.8 %collective-permute-start.2 = (bf16[784,128]{1,0:T(8,128)(2,1)S(1)}, bf16[784,128]{1,0:T(8,128)(2,1)S(1)}, u32[]{:S(2)}, u32[]{:S(2)}) collective-permute-start(bf16[784,128]{1,0:T(8,128)(2,1)S(1)} %collective-permute-done.1.refs_2_.refs_6_), channel_id=1, source_target_pairs={{0,2},{2,3},{3,1},{1,0},{4,6},{6,7},{7,5},{5,4},{8,10},{10,11},{11... | collective-permute-start | bytes 602120 | tf_op jit(solution)/shard_map/ppermute | solution.py:305
  44.0 1.7 %copy-start.8 = (bf16[784,128]{1,0:T(8,128)(2,1)}, bf16[784,128]{1,0:T(8,128)(2,1)S(1)}, u32[]{:S(2)}) copy-start(bf16[784,128]{1,0:T(8,128)(2,1)S(1)} %collective-permute-done.2.refs_3_.refs_7_) | copy-start | bytes 602116
  44.0 5.9 %collective-permute-start.5 = (bf16[3088,128]{1,0:T(8,128)(2,1)S(1)}, bf16[3088,128]{1,0:T(8,128)(2,1)}, u32[]{:S(2)}, u32[]{:S(2)}) collective-permute-start(bf16[3088,128]{1,0:T(8,128)(2,1)S(1)} %pad_maximum_fusion.refs_0_.refs_4_.refs_10_.refs_7_), channel_id=1, source_target_pairs={{0,4},{4,0},{8,12},{12,8},{16,20},{20,16},{24,28},{28,24},{1,5},{5... | collective-permute-start | bytes 2371592 | tf_op jit(solution)/shard_map/ppermute | solution.py:302
  44.0 6.0 %copy-start.1 = (bf16[3088,128]{1,0:T(8,128)(2,1)}, bf16[3088,128]{1,0:T(8,128)(2,1)S(1)}, u32[]{:S(2)}) copy-start(bf16[3088,128]{1,0:T(8,128)(2,1)S(1)} %collective-permute-done.8.refs_14_.refs_11_) | copy-start | bytes 2371588
  44.0 5.9 %collective-permute-start.9 = (bf16[3088,128]{1,0:T(8,128)(2,1)S(1)}, bf16[3088,128]{1,0:T(8,128)(2,1)}, u32[]{:S(2)}, u32[]{:S(2)}) collective-permute-start(bf16[3088,128]{1,0:T(8,128)(2,1)S(1)} %collective-permute-done.8.refs_14_.refs_11_), channel_id=1, source_target_pairs={{0,4},{4,0},{8,12},{12,8},{16,20},{20,16},{24,28},{28,24},{1,5},{5... | collective-permute-start | bytes 2371592 | tf_op jit(solution)/shard_map/ppermute | solution.py:302
  44.5 5.5 %copy-start.2 = (bf16[3088,128]{1,0:T(8,128)(2,1)}, bf16[3088,128]{1,0:T(8,128)(2,1)S(1)}, u32[]{:S(2)}) copy-start(bf16[3088,128]{1,0:T(8,128)(2,1)S(1)} %collective-permute-done.6.refs_12_.refs_9_) | copy-start | bytes 2371588
  44.5 5.4 %collective-permute-start.7 = (bf16[3088,128]{1,0:T(8,128)(2,1)S(1)}, bf16[3088,128]{1,0:T(8,128)(2,1)}, u32[]{:S(2)}, u32[]{:S(2)}) collective-permute-start(bf16[3088,128]{1,0:T(8,128)(2,1)S(1)} %collective-permute-done.6.refs_12_.refs_9_), channel_id=1, source_target_pairs={{0,4},{4,0},{8,12},{12,8},{16,20},{20,16},{24,28},{28,24},{1,5},{5... | collective-permute-start | bytes 2371592 | tf_op jit(solution)/shard_map/ppermute | solution.py:302
  45.6 4.3 %copy-start.3 = (bf16[3088,128]{1,0:T(8,128)(2,1)}, bf16[3088,128]{1,0:T(8,128)(2,1)S(1)}, u32[]{:S(2)}) copy-start(bf16[3088,128]{1,0:T(8,128)(2,1)S(1)} %collective-permute-done.10.refs_16_.refs_13_) | copy-start | bytes 2371588
  45.6 4.3 %collective-permute-start.11 = (bf16[3088,128]{1,0:T(8,128)(2,1)S(1)}, bf16[3088,128]{1,0:T(8,128)(2,1)}, u32[]{:S(2)}, u32[]{:S(2)}) collective-permute-start(bf16[3088,128]{1,0:T(8,128)(2,1)S(1)} %collective-permute-done.10.refs_16_.refs_13_), channel_id=1, source_target_pairs={{0,4},{4,0},{8,12},{12,8},{16,20},{20,16},{24,28},{28,24},{1,5},{5... | collective-permute-start | bytes 2371592 | tf_op jit(solution)/shard_map/ppermute | solution.py:302
  45.7 16.1 %collective-permute-start.12 = (bf16[2304,128]{1,0:T(8,128)(2,1)}, bf16[2304,128]{1,0:T(8,128)(2,1)}, u32[]{:S(2)}, u32[]{:S(2)}) collective-permute-start(bf16[2304,128]{1,0:T(8,128)(2,1)} %collective-permute-done.4.refs_9_.refs_5_), channel_id=1, source_target_pairs={{0,2},{2,3},{3,1},{1,0},{4,6},{6,7},{7,5},{5,4},{8,10},{10,11},{11... | collective-permute-start | bytes 1769480 | tf_op jit(solution)/shard_map/ppermute | solution.py:305

commit v5 on v4

--- a/solution.py
+++ b/solution.py
@@ -117,7 +117,7 @@
     lax.fori_loop(0, count, drain, 0)
 
 
-def early_kernel(sizes, n_a, n_b, tables, c_cols, c_keep, *refs):
+def early_kernel(sizes, n_a, n_b, pieces_from, tables, c_cols, c_keep, *refs):
     rows, n_section, n_rows, panel_width, n_early, half = sizes
     strips, refs = refs[:n_section], refs[n_section:]
     a_bufs, b_bufs = refs[:n_a], refs[n_a : n_a + n_b]
@@ -127,12 +127,11 @@
     left, right, _, _, load_sem, store_sem = scratch
     pieces_at = n_section
     wanted_at = pieces_at + n_rows
-    keep_at = wanted_at + rows
-    lookup_at = keep_at + rows
+    lookup_at = wanted_at + rows
     results = c_cols.shape[1]
     me = lax.axis_index("rows") * n_section + lax.axis_index("section")
     copies = [pltpu.make_async_copy(tables.at[me], table, sem.at[0])]
-    sources = [*strips, *b_bufs]
+    sources = [*strips, *(b_bufs[b] for b in pieces_from)]
     for n, source in enumerate(sources):
         tail = source.at[pl.ds(source.shape[0] - TAIL, TAIL)]
         copies.append(pltpu.make_async_copy(tail, tails.at[n], sem.at[1]))
@@ -144,29 +143,38 @@
         copy.wait()
     for n in range(len(sources)):
         numbers[n : n + 1] = tails[n].astype(jnp.float32)[:1].astype(jnp.int32)
-    numbers[lookup_at : lookup_at + table.shape[0]] = table[...]
+    numbers[lookup_at : lookup_at + 1] = table[:1]
     to_scalars = pltpu.make_async_copy(numbers, scalars, sem.at[0])
     to_scalars.start()
     to_scalars.wait()
-    lanes = numbers.shape[1]
 
     def lookup(n):
-        return scalars[lookup_at + n // lanes, n % lanes]
+        return scalars[lookup_at, n]
+
+    reciprocal = -(-(1 << 16) // rows)
+    ks = np.arange(n_rows * rows)
+    assert (ks * reciprocal >> 16 == ks // rows).all()
+    low_bufs, high_bufs, cuts, strip_of = (
+        [lookup(f * n_section + a) for a in range(n_section)] for f in range(4)
+    )
 
     def one_row(i, counts):
         in_upper = i >= half
         columns, lates, parts = [], [], []
         for a in range(n_section):
-            col = scalars[lookup(3 * n_section + a), i]
+            col = scalars[strip_of[a], i]
             k = jnp.maximum(a * panel_width + col, 0)
-            group = k // rows
+            group = (k * reciprocal) >> 16
             inside = k - group * rows
-            piece = scalars[lookup_at + (4 * n_section) // lanes, (4 * n_section) % lanes + group]
+            piece = lookup(4 * n_section + 3 * n_rows + group)
             columns.append(jnp.where(col >= 0, scalars[pieces_at + piece, inside], -1))
-            buf = jnp.where(in_upper, lookup(n_section + a), lookup(a))
+            upper = inside >= rows // 2
+            source = lookup(4 * n_section + jnp.where(upper, n_rows, 0) + group)
+            inside = inside - jnp.where(upper, lookup(4 * n_section + 2 * n_rows + group), 0)
+            buf = jnp.where(in_upper, high_bufs[a], low_bufs[a])
             lates.append((buf >= n_early).astype(jnp.int32))
-            row = i - jnp.where(in_upper, lookup(2 * n_section + a), 0)
-            parts.append(put(left_buf=buf, left_row=row, right_buf=piece, right_row=inside))
+            row = i - jnp.where(in_upper, cuts[a], 0)
+            parts.append(put(left_buf=buf, left_row=row, right_buf=source, right_row=inside))
         n_now, n_late = counts
         for c in range(results):
             r = i * results + c
@@ -243,15 +251,15 @@
     ]
 
 
-def multiply_early(sizes, tables, c_cols, c_keep, strips, a_bufs, b_bufs, out_shape):
+def multiply_early(sizes, pieces_from, tables, c_cols, c_keep, strips, a_bufs, b_bufs, out_shape):
     rows, n_section, n_rows = sizes[:3]
     operands = [*strips, *a_bufs, *b_bufs]
     bs, n_results = out_shape[-1], c_cols.size
     most = rows * n_section + -(rows * n_section) % UNROLL
     n_tails = n_section + n_rows
-    n_numbers = n_tails + 2 * rows + tables.shape[1]
+    n_numbers = n_tails + rows + 1
     return pl.pallas_call(
-        functools.partial(early_kernel, sizes, len(a_bufs), len(b_bufs)),
+        functools.partial(early_kernel, sizes, len(a_bufs), len(b_bufs), pieces_from),
         out_shape=(
             jax.ShapeDtypeStruct(out_shape, jnp.bfloat16),
             jax.ShapeDtypeStruct((1 + most,), jnp.int32),
@@ -303,31 +311,40 @@
 
         pairs = [(RING[i], RING[(i + 1) % 4]) for i in range(4)]
         step = lambda x: lax.ppermute(x, "section", pairs)
-        half = 3
+        half = 4
         middle = half * 2 * bs
         small, big = [jnp.concatenate([blocks[:middle], tail])], [blocks[middle:]]
         small.append(step(small[0]))
         big.append(step(big[0]))
-        for_across = own = mine
-        for_across, small[1] = lax.optimization_barrier((mine, small[1]))
-        for _ in range(2):
-            small.append(step(small[-1]))
-            big.append(step(big[-1]))
-
-        came = [swap(mine, 2), swap(mine, 4), swap(for_across, 6)]
-        b_bufs = []
-        for x in [own, *came]:
-            b_bufs += [x, swap(x, 1)]
+
+        for_d, small[1] = lax.optimization_barrier((mine, small[1]))
+        came = [swap(mine, 2), swap(mine, 4), swap(for_d, 6)]
+        beside = swap(mine, 1)
+        small.append(step(small[1]))
+        big.append(step(big[1]))
+        small.append(step(small[2]))
+        past = [swap(came[0], 1), swap(came[1], 1)]
+        big[2], beside = lax.optimization_barrier((big[2], beside))
+        big.append(step(big[2]))
+
+        cut = rows // 2 * 2 * bs
+        lower, upper = came[2][:cut], came[2][cut:]
+        lower, small[3] = lax.optimization_barrier((lower, small[3]))
+        b_bufs = [mine, beside, *came, *past, swap(lower, 1), swap(upper, 1)]
         a_bufs = [mine, *small[1:], *big[1:]]
         n_early = 6
         strips = [mine, *small[1:]]
 
+        pieces_from = (0, 1, 2, 5, 3, 6, 4, 8)
         steps = lambda s, a: (RING.index(s) - RING.index(a)) % 4
         tables = [
             [steps(s, a) for a in range(4)]
             + [(0, 4, 5, 6)[steps(s, a)] for a in range(4)]
             + [(0, half, half, half)[steps(s, a)] for a in range(4)]
             + [steps(s, a) for a in range(4)]
+            + [(0, 1, 2, 5, 3, 6, 4, 7)[g ^ r] for g in range(8)]
+            + [(0, 1, 2, 5, 3, 6, 4, 8)[g ^ r] for g in range(8)]
+            + [(0, 0, 0, 0, 0, 0, 0, rows // 2)[g ^ r] for g in range(8)]
             + [g ^ r for g in range(8)]
             for r, s in everyone
         ]
@@ -339,18 +356,20 @@
 
         a_bufs, b_bufs = shifts(mine, "section", n_section), shifts(mine, "rows", n_rows)
         n_early, strips = n_section, a_bufs
+        pieces_from = tuple(range(n_rows))
         tables = []
         for r, s in everyone:
             panels = [(s - a) % n_section for a in range(n_section)]
             groups = [(r - g) % n_rows for g in range(n_rows)]
-            tables.append(panels * 2 + [0] * n_section + panels + groups)
+            tables.append(panels * 2 + [0] * n_section + panels + groups * 2 + [0] * n_rows + groups)
 
     tables = np.array(tables, np.int32)
-    tables = np.pad(tables, ((0, 0), (0, -tables.shape[1] % (8 * bs)))).reshape(len(everyone), -1, bs)
+    assert tables.shape[1] <= bs
+    tables = np.pad(tables, ((0, 0), (0, 8 * bs - tables.shape[1]))).reshape(len(everyone), 8, bs)
     sizes = (rows, n_section, n_rows, panel_width, n_early, half)
     out_shape = (rows, c_cols.shape[1], *x_blocks.shape[2:])
     out, codes = multiply_early(
-        sizes, jnp.asarray(tables), c_cols, c_keep, strips, a_bufs[:n_early], b_bufs, out_shape
+        sizes, pieces_from, jnp.asarray(tables), c_cols, c_keep, strips, a_bufs[:n_early], b_bufs, out_shape
     )
     if n_early < len(a_bufs):
         out = multiply_late(codes, a_bufs, b_bufs, out)

time: 65.1 us -> 64.1 us (0.985)
  local copies, waits for them, and re-layouts: 3.46 us -> 5.85 us
  waiting for transfers between devices: 25.4 us -> 23.3 us
  starting transfers between devices: 24.3 us -> 22.7 us
    ppermute x6, starting transfers between devices: 18.7 us -> 16.6 us  [on_device(): step = lambda x: lax.ppermute(x, 'section', pairs)]
    ppermute x6, waiting for transfers between devices: 24.3 us -> 22.6 us  [on_device(): step = lambda x: lax.ppermute(x, 'section', pairs)]
    slice x0 -> x2, local copies, waits for them, and re-layouts: none -> 1.67 us  [on_device(): lower, upper = (came[2][:cut], came[2][cut:])]
    unnamed x24 -> x26, local copies, waits for them, and re-layouts: 1.41 us -> 2.12 us
    ppermute x7 -> x8, starting transfers between devices: 5.63 us -> 6.02 us  [on_device(): lax.ppermute(x, 'rows', [(r, r ^ m) for r in range(n_rows)])]
  transfers between devices with their start and end apart: 13 -> 14, of which waited for: 5 -> 6; matrix products, arithmetic and copies ran while one was open for 4% -> 7% of each run, Pallas kernels for 12% -> 12%
where the time goes in v5:
time: 64.1 us; the launch traced here: 63.3 us
  waiting for transfers between devices  23.3 us (36%)
  starting transfers between devices  22.7 us (35%)
  Pallas kernels  10.5 us (16%)
  local copies, waits for them, and re-layouts  5.85 us (9%)
  other arithmetic  0.8 us (1%)
    ppermute x6, waiting for transfers between devices, on_device(): step = lambda x: lax.ppermute(x, 'section', pairs)  22.6 us
    ppermute x6, starting transfers between devices, on_device(): step = lambda x: lax.ppermute(x, 'section', pairs)  16.6 us
    pallas_call x1, Pallas kernels, multiply_early(): pl.pallas_call(functools.partial(early_kernel, sizes, len(a_bufs), len(b_...  7.76 us
    ppermute x8, starting transfers between devices, on_device(): lax.ppermute(x, 'rows', [(r, r ^ m) for r in range(n_rows)])  6.02 us
    pallas_call x1, Pallas kernels, multiply_late(): pl.pallas_call(functools.partial(late_kernel, len(a_bufs), len(b_bufs)),...  2.74 us
    unnamed x26, local copies, waits for them, and re-layouts  2.12 us
    slice x2, local copies, waits for them, and re-layouts, on_device(): small, big = ([jnp.concatenate([blocks[:middle], tail])], [blocks[middle:]])  2.04 us
    slice x2, local copies, waits for them, and re-layouts, on_device(): lower, upper = (came[2][:cut], came[2][cut:])  1.67 us
  transfers between devices with their start and end apart: 14, of which 6 were waited for; matrix products, arithmetic and copies ran while one was open for 7% of the time, Pallas kernels for 12%

profile of v5, /device:TPU:0, one launch (start us, length us, event | category | flops | bytes accessed | tf_op | source)
XLA Modules:
  0.0 63.3 jit_solution(8123454193854292988)
XLA Ops:
  0.0 0.7 %convert_bitcast_fusion = bf16[1,12]{1,0:T(2,128)(2,1)S(1)} fusion(s32[12,1]{0,1:T(1,128)} %param.6), kind=kLoop, calls=%fused_computation.2 | loop fusion | flops 12 | bytes 72 | tf_op jit(solution)/shard_map/convert_element_type | solution.py:306
  0.7 1.0 %slice.18 = bf16[4,1,2,128,128]{4,3,2,1,0:T(8,128)(2,1)S(1)} slice(bf16[12,1,2,128,128]{4,3,2,1,0:T(8,128)(2,1)} %param.5), slice={[0:4], [0:1], [0:2], [0:128], [0:128]} | slice | bytes 524288 | tf_op jit(solution)/shard_map/slice | solution.py:316
  1.7 4.1 %collective-permute-start = (bf16[1040,128]{1,0:T(8,128)(2,1)S(1)}, bf16[1040,128]{1,0:T(8,128)(2,1)S(1)}, u32[]{:S(2)}, u32[]{:S(2)}) collective-permute-start(bf16[1040,128]{1,0:T(8,128)(2,1)S(1)} %pad_maximum_fusion.1), channel_id=1, source_target_pairs={{0,2},{2,3},{3,1},{1,0},{4,6},{6,7},{7,5},{5,4},{8,10},{10,11},{11... | collective-permute-start | bytes 798728 | tf_op jit(solution)/shard_map/ppermute | solution.py:313
  5.8 1.1 %slice.21 = bf16[8,1,2,128,128]{4,3,2,1,0:T(8,128)(2,1)S(1)} slice(bf16[12,1,2,128,128]{4,3,2,1,0:T(8,128)(2,1)} %param.5), slice={[4:12], [0:1], [0:2], [0:128], [0:128]} | slice | bytes 1048576 | tf_op jit(solution)/shard_map/slice | solution.py:316
  6.9 1.6 %collective-permute-start.4 = (bf16[2048,128]{1,0:T(8,128)(2,1)S(1)}, bf16[2048,128]{1,0:T(8,128)(2,1)S(1)}, u32[]{:S(2)}, u32[]{:S(2)}) collective-permute-start(bf16[2048,128]{1,0:T(8,128)(2,1)S(1)} %bitcast.7), channel_id=1, source_target_pairs={{0,2},{2,3},{3,1},{1,0},{4,6},{6,7},{7,5},{5,4},{8,10},{10,11},{11... | collective-permute-start | bytes 1572872 | tf_op jit(solution)/shard_map/ppermute | solution.py:313
  8.6 0.1 pad_maximum_fusion.refs_0_.refs_4_.refs_10_.refs_7_
  8.6 1.6 %collective-permute-start.8 = (bf16[3088,128]{1,0:T(8,128)(2,1)S(1)}, bf16[3088,128]{1,0:T(8,128)(2,1)S(1)}, u32[]{:S(2)}, u32[]{:S(2)}) collective-permute-start(bf16[3088,128]{1,0:T(8,128)(2,1)S(1)} %pad_maximum_fusion.refs_0_.refs_4_.refs_10_.refs_7_), channel_id=1, source_target_pairs={{0,16},{4,20},{8,24},{12,28},{16,0},{20,4},{24,8},{28,12},{1,17},{... | collective-permute-start | bytes 2371592 | tf_op jit(solution)/shard_map/ppermute | solution.py:310
  10.2 1.5 %collective-permute-start.7 = (bf16[3088,128]{1,0:T(8,128)(2,1)S(1)}, bf16[3088,128]{1,0:T(8,128)(2,1)S(1)}, u32[]{:S(2)}, u32[]{:S(2)}) collective-permute-start(bf16[3088,128]{1,0:T(8,128)(2,1)S(1)} %pad_maximum_fusion.refs_0_.refs_4_.refs_10_.refs_7_), channel_id=1, source_target_pairs={{0,8},{4,12},{8,0},{12,4},{16,24},{20,28},{24,16},{28,20},{1,9},{5... | collective-permute-start | bytes 2371592 | tf_op jit(solution)/shard_map/ppermute | solution.py:310
  11.7 0.9 %collective-permute-done.refs_1_.refs_5_ = bf16[1040,128]{1,0:T(8,128)(2,1)S(1)} collective-permute-done((bf16[1040,128]{1,0:T(8,128)(2,1)S(1)}, bf16[1040,128]{1,0:T(8,128)(2,1)S(1)}, u32[]{:S(2)}, u32[]{:S(2)}) %collective-permute-start) | collective-permute-done | bytes 266272 | tf_op jit(solution)/shard_map/ppermute | solution.py:313
  12.6 3.4 %collective-permute-start.1 = (bf16[1040,128]{1,0:T(8,128)(2,1)S(1)}, bf16[1040,128]{1,0:T(8,128)(2,1)S(1)}, u32[]{:S(2)}, u32[]{:S(2)}) collective-permute-start(bf16[1040,128]{1,0:T(8,128)(2,1)S(1)} %collective-permute-done.refs_1_.refs_5_), channel_id=1, source_target_pairs={{0,2},{2,3},{3,1},{1,0},{4,6},{6,7},{7,5},{5,4},{8,10},{10,11},{11... | collective-permute-start | bytes 798728 | tf_op jit(solution)/shard_map/ppermute | solution.py:313
  16.0 7.9 %collective-permute-done.4.refs_8_.refs_4_ = bf16[2048,128]{1,0:T(8,128)(2,1)S(1)} collective-permute-done((bf16[2048,128]{1,0:T(8,128)(2,1)S(1)}, bf16[2048,128]{1,0:T(8,128)(2,1)S(1)}, u32[]{:S(2)}, u32[]{:S(2)}) %collective-permute-start.4) | collective-permute-done | bytes 524320 | tf_op jit(solution)/shard_map/ppermute | solution.py:313
  23.9 2.4 %collective-permute-start.2 = (bf16[3088,128]{1,0:T(8,128)(2,1)S(1)}, bf16[3088,128]{1,0:T(8,128)(2,1)S(1)}, u32[]{:S(2)}, u32[]{:S(2)}) collective-permute-start(bf16[3088,128]{1,0:T(8,128)(2,1)S(1)} %pad_maximum_fusion.refs_0_.refs_4_.refs_10_.refs_7_), channel_id=1, source_target_pairs={{0,24},{4,28},{8,16},{12,20},{16,8},{20,12},{24,0},{28,4},{1,25},{... | collective-permute-start | bytes 2371592 | tf_op jit(solution)/shard_map/ppermute | solution.py:310
  26.3 2.1 %collective-permute-done.1.refs_2_.refs_6_ = bf16[1040,128]{1,0:T(8,128)(2,1)S(1)} collective-permute-done((bf16[1040,128]{1,0:T(8,128)(2,1)S(1)}, bf16[1040,128]{1,0:T(8,128)(2,1)S(1)}, u32[]{:S(2)}, u32[]{:S(2)}) %collective-permute-start.1) | collective-permute-done | bytes 266272 | tf_op jit(solution)/shard_map/ppermute | solution.py:313
  28.4 3.4 %collective-permute-start.5 = (bf16[2048,128]{1,0:T(8,128)(2,1)S(1)}, bf16[2048,128]{1,0:T(8,128)(2,1)}, u32[]{:S(2)}, u32[]{:S(2)}) collective-permute-start(bf16[2048,128]{1,0:T(8,128)(2,1)S(1)} %collective-permute-done.4.refs_8_.refs_4_), channel_id=1, source_target_pairs={{0,2},{2,3},{3,1},{1,0},{4,6},{6,7},{7,5},{5,4},{8,10},{10,11},{11... | collective-permute-start | bytes 1572872 | tf_op jit(solution)/shard_map/ppermute | solution.py:313
  31.8 0.0 collective-permute-done.8.refs_13_.refs_10_
  31.8 0.0 collective-permute-start.10
  31.8 0.5 collective-permute-start.9
  32.3 0.7 %collective-permute-start.3 = (bf16[1040,128]{1,0:T(8,128)(2,1)S(1)}, bf16[1040,128]{1,0:T(8,128)(2,1)S(1)}, u32[]{:S(2)}, u32[]{:S(2)}) collective-permute-start(bf16[1040,128]{1,0:T(8,128)(2,1)S(1)} %collective-permute-done.1.refs_2_.refs_6_), channel_id=1, source_target_pairs={{0,2},{2,3},{3,1},{1,0},{4,6},{6,7},{7,5},{5,4},{8,10},{10,11},{11... | collective-permute-start | bytes 798728 | tf_op jit(solution)/shard_map/ppermute | solution.py:313
  33.0 11.2 %collective-permute-done.5.refs_9_.refs_5_ = bf16[2048,128]{1,0:T(8,128)(2,1)} collective-permute-done((bf16[2048,128]{1,0:T(8,128)(2,1)S(1)}, bf16[2048,128]{1,0:T(8,128)(2,1)}, u32[]{:S(2)}, u32[]{:S(2)}) %collective-permute-start.5) | collective-permute-done | bytes 524320 | tf_op jit(solution)/shard_map/ppermute | solution.py:313
  44.2 3.5 %collective-permute-start.13 = (bf16[2048,128]{1,0:T(8,128)(2,1)}, bf16[2048,128]{1,0:T(8,128)(2,1)}, u32[]{:S(2)}, u32[]{:S(2)}) collective-permute-start(bf16[2048,128]{1,0:T(8,128)(2,1)} %collective-permute-done.5.refs_9_.refs_5_), channel_id=1, source_target_pairs={{0,2},{2,3},{3,1},{1,0},{4,6},{6,7},{7,5},{5,4},{8,10},{10,11},{11... | collective-permute-start | bytes 1572872 | tf_op jit(solution)/shard_map/ppermute | solution.py:313
  47.7 0.8 %slice.25 = bf16[1552,128]{1,0:T(8,128)(2,1)} slice(bf16[3088,128]{1,0:T(8,128)(2,1)S(1)} %collective-permute-done.2.refs_14_.refs_11_), slice={[1536:3088], [0:128]} | slice | bytes 794624 | tf_op jit(solution)/shard_map/slice | solution.py:331
  48.5 0.0 collective-permute-start.12
  48.5 0.8 %slice.24 = bf16[1536,128]{1,0:T(8,128)(2,1)} slice(bf16[3088,128]{1,0:T(8,128)(2,1)S(1)} %collective-permute-done.2.refs_14_.refs_11_), slice={[0:1536], [0:128]} | slice | bytes 786432 | tf_op jit(solution)/shard_map/slice | solution.py:331
  49.4 0.5 collective-permute-done.3.refs_3_.refs_7_
  49.9 0.7 %copy-done.8 = bf16[1040,128]{1,0:T(8,128)(2,1)} copy-done((bf16[1040,128]{1,0:T(8,128)(2,1)}, bf16[1040,128]{1,0:T(8,128)(2,1)S(1)}, u32[]{:S(2)}) %copy-start.8) | copy-done | bytes 266264
  50.6 0.0 collective-permute-start.11
  50.6 0.7 %copy.7.c_cols = s32[12,3]{1,0:T(8,128)} copy(s32[12,3]{0,1:T(4,128)S(1)} %copy-done.10) | data formatting | bytes 288 | tf_op args[2]
  51.3 0.7 %copy.8.c_keep = s32[12,3]{1,0:T(8,128)} copy(s32[12,3]{0,1:T(4,128)S(1)} %copy-done.11) | data formatting | bytes 288 | tf_op args[3]
  52.0 0.7 %collective-permute-done.11.refs_17_.refs_14_ = bf16[1536,128]{1,0:T(8,128)(2,1)} collective-permute-done((bf16[1536,128]{1,0:T(8,128)(2,1)}, bf16[1536,128]{1,0:T(8,128)(2,1)}, u32[]{:S(2)}, u32[]{:S(2)}) %collective-permute-start.11) | collective-permute-done | bytes 393248 | tf_op jit(solution)/shard_map/ppermute | solution.py:310
  52.7 0.0 collective-permute-done.10.refs_16_.refs_13_
  52.8 7.8 %shard_map.55 = (bf16[12,3,2,128,128]{4,3,2,1,0:T(8,128)(2,1)}, s32[49]{0:T(128)}) custom-call(s32[32,8,128]{2,1,0:T(8,128)} %constant.5.clone.tables, s32[12,3]{1,0:T(8,128)} %copy.7.c_cols, s32[12,3]{1,0:T(8,128)} %copy.8.c_keep, bf16[3088,128]{1,0:T(8,128)(2,1)} %copy-done, bf16[1040,128]{1,0:T(8,128)(2,1)} %copy-done.6, bf16[1040,128]{1,0:T(8,128)(2,1)} %copy-done.7, ...), custom_call_target="tpu_custom_call" | custom-call | flops 1000 | bytes 1000 | tf_op jit(solution)/shard_map/pallas_call | solution.py:261
  60.5 2.7 %shard_map.56 = bf16[12,3,2,128,128]{4,3,2,1,0:T(8,128)(2,1)} custom-call(s32[49]{0:T(128)} %get-tuple-element.19.codes, bf16[3088,128]{1,0:T(8,128)(2,1)} %copy-done, bf16[1040,128]{1,0:T(8,128)(2,1)} %copy-done.6, bf16[1040,128]{1,0:T(8,128)(2,1)} %copy-done.7, bf16[1040,128]{1,0:T(8,128)(2,1)} %copy-done.8, ...), custom_call_target="tpu_custom_call", output_to_operand_aliasing={{}: (17, {})} | custom-call | tf_op jit(solution)/shard_map/pallas_call | solution.py:287
  (32 shorter events, 0.1 us)
Async XLA Ops:
  0.0 8.5 %copy-start.5 = (bf16[12,1,2,128,128]{4,3,2,1,0:T(8,128)(2,1)S(1)}, bf16[12,1,2,128,128]{4,3,2,1,0:T(8,128)(2,1)}, u32[]{:S(2)}) copy-start(bf16[12,1,2,128,128]{4,3,2,1,0:T(8,128)(2,1)} %param.5) | copy-start | bytes 2359300
  1.7 10.9 %collective-permute-start = (bf16[1040,128]{1,0:T(8,128)(2,1)S(1)}, bf16[1040,128]{1,0:T(8,128)(2,1)S(1)}, u32[]{:S(2)}, u32[]{:S(2)}) collective-permute-start(bf16[1040,128]{1,0:T(8,128)(2,1)S(1)} %pad_maximum_fusion.1), channel_id=1, source_target_pairs={{0,2},{2,3},{3,1},{1,0},{4,6},{6,7},{7,5},{5,4},{8,10},{10,11},{11... | collective-permute-start | bytes 798728 | tf_op jit(solution)/shard_map/ppermute | solution.py:313
  6.9 17.0 %collective-permute-start.4 = (bf16[2048,128]{1,0:T(8,128)(2,1)S(1)}, bf16[2048,128]{1,0:T(8,128)(2,1)S(1)}, u32[]{:S(2)}, u32[]{:S(2)}) collective-permute-start(bf16[2048,128]{1,0:T(8,128)(2,1)S(1)} %bitcast.7), channel_id=1, source_target_pairs={{0,2},{2,3},{3,1},{1,0},{4,6},{6,7},{7,5},{5,4},{8,10},{10,11},{11... | collective-permute-start | bytes 1572872 | tf_op jit(solution)/shard_map/ppermute | solution.py:313
  8.5 42.1 %copy-start.10 = (s32[12,3]{0,1:T(4,128)S(1)}, s32[12,3]{0,1:T(4,128)}, u32[]{:S(2)}) copy-start(s32[12,3]{0,1:T(4,128)} %param.7) | copy-start | bytes 436
  8.6 42.8 %copy-start.11 = (s32[12,3]{0,1:T(4,128)S(1)}, s32[12,3]{0,1:T(4,128)}, u32[]{:S(2)}) copy-start(s32[12,3]{0,1:T(4,128)} %param.8) | copy-start | bytes 436
  8.6 44.1 %copy-start = (bf16[3088,128]{1,0:T(8,128)(2,1)}, bf16[3088,128]{1,0:T(8,128)(2,1)S(1)}, u32[]{:S(2)}) copy-start(bf16[3088,128]{1,0:T(8,128)(2,1)S(1)} %pad_maximum_fusion.refs_0_.refs_4_.refs_10_.refs_7_) | copy-start | bytes 2371588
  8.6 23.2 %collective-permute-start.8 = (bf16[3088,128]{1,0:T(8,128)(2,1)S(1)}, bf16[3088,128]{1,0:T(8,128)(2,1)S(1)}, u32[]{:S(2)}, u32[]{:S(2)}) collective-permute-start(bf16[3088,128]{1,0:T(8,128)(2,1)S(1)} %pad_maximum_fusion.refs_0_.refs_4_.refs_10_.refs_7_), channel_id=1, source_target_pairs={{0,16},{4,20},{8,24},{12,28},{16,0},{20,4},{24,8},{28,12},{1,17},{... | collective-permute-start | bytes 2371592 | tf_op jit(solution)/shard_map/ppermute | solution.py:310
  10.2 21.6 %collective-permute-start.7 = (bf16[3088,128]{1,0:T(8,128)(2,1)S(1)}, bf16[3088,128]{1,0:T(8,128)(2,1)S(1)}, u32[]{:S(2)}, u32[]{:S(2)}) collective-permute-start(bf16[3088,128]{1,0:T(8,128)(2,1)S(1)} %pad_maximum_fusion.refs_0_.refs_4_.refs_10_.refs_7_), channel_id=1, source_target_pairs={{0,8},{4,12},{8,0},{12,4},{16,24},{20,28},{24,16},{28,20},{1,9},{5... | collective-permute-start | bytes 2371592 | tf_op jit(solution)/shard_map/ppermute | solution.py:310
  11.7 20.6 %collective-permute-start.6 = (bf16[3088,128]{1,0:T(8,128)(2,1)S(1)}, bf16[3088,128]{1,0:T(8,128)(2,1)S(1)}, u32[]{:S(2)}, u32[]{:S(2)}) collective-permute-start(bf16[3088,128]{1,0:T(8,128)(2,1)S(1)} %pad_maximum_fusion.refs_0_.refs_4_.refs_10_.refs_7_), channel_id=1, source_target_pairs={{0,4},{4,0},{8,12},{12,8},{16,20},{20,16},{24,28},{28,24},{1,5},{5... | collective-permute-start | bytes 2371592 | tf_op jit(solution)/shard_map/ppermute | solution.py:310
  12.6 40.1 %copy-start.6 = (bf16[1040,128]{1,0:T(8,128)(2,1)}, bf16[1040,128]{1,0:T(8,128)(2,1)S(1)}, u32[]{:S(2)}) copy-start(bf16[1040,128]{1,0:T(8,128)(2,1)S(1)} %collective-permute-done.refs_1_.refs_5_) | copy-start | bytes 798724
  12.6 15.8 %collective-permute-start.1 = (bf16[1040,128]{1,0:T(8,128)(2,1)S(1)}, bf16[1040,128]{1,0:T(8,128)(2,1)S(1)}, u32[]{:S(2)}, u32[]{:S(2)}) collective-permute-start(bf16[1040,128]{1,0:T(8,128)(2,1)S(1)} %collective-permute-done.refs_1_.refs_5_), channel_id=1, source_target_pairs={{0,2},{2,3},{3,1},{1,0},{4,6},{6,7},{7,5},{5,4},{8,10},{10,11},{11... | collective-permute-start | bytes 798728 | tf_op jit(solution)/shard_map/ppermute | solution.py:313
  23.9 26.0 %copy-start.9 = (bf16[2048,128]{1,0:T(8,128)(2,1)}, bf16[2048,128]{1,0:T(8,128)(2,1)S(1)}, u32[]{:S(2)}) copy-start(bf16[2048,128]{1,0:T(8,128)(2,1)S(1)} %collective-permute-done.4.refs_8_.refs_4_) | copy-start | bytes 1572868
  23.9 23.8 %collective-permute-start.2 = (bf16[3088,128]{1,0:T(8,128)(2,1)S(1)}, bf16[3088,128]{1,0:T(8,128)(2,1)S(1)}, u32[]{:S(2)}, u32[]{:S(2)}) collective-permute-start(bf16[3088,128]{1,0:T(8,128)(2,1)S(1)} %pad_maximum_fusion.refs_0_.refs_4_.refs_10_.refs_7_), channel_id=1, source_target_pairs={{0,24},{4,28},{8,16},{12,20},{16,8},{20,12},{24,0},{28,4},{1,25},{... | collective-permute-start | bytes 2371592 | tf_op jit(solution)/shard_map/ppermute | solution.py:310
  28.4 19.3 %copy-start.7 = (bf16[1040,128]{1,0:T(8,128)(2,1)}, bf16[1040,128]{1,0:T(8,128)(2,1)S(1)}, u32[]{:S(2)}) copy-start(bf16[1040,128]{1,0:T(8,128)(2,1)S(1)} %collective-permute-done.1.refs_2_.refs_6_) | copy-start | bytes 798724
  28.4 15.8 %collective-permute-start.5 = (bf16[2048,128]{1,0:T(8,128)(2,1)S(1)}, bf16[2048,128]{1,0:T(8,128)(2,1)}, u32[]{:S(2)}, u32[]{:S(2)}) collective-permute-start(bf16[2048,128]{1,0:T(8,128)(2,1)S(1)} %collective-permute-done.4.refs_8_.refs_4_), channel_id=1, source_target_pairs={{0,2},{2,3},{3,1},{1,0},{4,6},{6,7},{7,5},{5,4},{8,10},{10,11},{11... | collective-permute-start | bytes 1572872 | tf_op jit(solution)/shard_map/ppermute | solution.py:313
  31.8 20.9 %copy-start.2 = (bf16[3088,128]{1,0:T(8,128)(2,1)}, bf16[3088,128]{1,0:T(8,128)(2,1)S(1)}, u32[]{:S(2)}) copy-start(bf16[3088,128]{1,0:T(8,128)(2,1)S(1)} %collective-permute-done.8.refs_13_.refs_10_) | copy-start | bytes 2371588
  31.8 20.9 %collective-permute-start.10 = (bf16[3088,128]{1,0:T(8,128)(2,1)S(1)}, bf16[3088,128]{1,0:T(8,128)(2,1)}, u32[]{:S(2)}, u32[]{:S(2)}) collective-permute-start(bf16[3088,128]{1,0:T(8,128)(2,1)S(1)} %collective-permute-done.8.refs_13_.refs_10_), channel_id=1, source_target_pairs={{0,4},{4,0},{8,12},{12,8},{16,20},{20,16},{24,28},{28,24},{1,5},{5... | collective-permute-start | bytes 2371592 | tf_op jit(solution)/shard_map/ppermute | solution.py:310
  31.8 20.9 %copy-start.3 = (bf16[3088,128]{1,0:T(8,128)(2,1)}, bf16[3088,128]{1,0:T(8,128)(2,1)S(1)}, u32[]{:S(2)}) copy-start(bf16[3088,128]{1,0:T(8,128)(2,1)S(1)} %collective-permute-done.7.refs_12_.refs_9_) | copy-start | bytes 2371588
  31.8 20.9 %collective-permute-start.9 = (bf16[3088,128]{1,0:T(8,128)(2,1)S(1)}, bf16[3088,128]{1,0:T(8,128)(2,1)}, u32[]{:S(2)}, u32[]{:S(2)}) collective-permute-start(bf16[3088,128]{1,0:T(8,128)(2,1)S(1)} %collective-permute-done.7.refs_12_.refs_9_), channel_id=1, source_target_pairs={{0,4},{4,0},{8,12},{12,8},{16,20},{20,16},{24,28},{28,24},{1,5},{5... | collective-permute-start | bytes 2371592 | tf_op jit(solution)/shard_map/ppermute | solution.py:310
  32.3 11.9 %copy-start.4 = (bf16[3088,128]{1,0:T(8,128)(2,1)}, bf16[3088,128]{1,0:T(8,128)(2,1)S(1)}, u32[]{:S(2)}) copy-start(bf16[3088,128]{1,0:T(8,128)(2,1)S(1)} %collective-permute-done.6.refs_11_.refs_8_) | copy-start | bytes 2371588
  32.3 17.6 %collective-permute-start.3 = (bf16[1040,128]{1,0:T(8,128)(2,1)S(1)}, bf16[1040,128]{1,0:T(8,128)(2,1)S(1)}, u32[]{:S(2)}, u32[]{:S(2)}) collective-permute-start(bf16[1040,128]{1,0:T(8,128)(2,1)S(1)} %collective-permute-done.1.refs_2_.refs_6_), channel_id=1, source_target_pairs={{0,2},{2,3},{3,1},{1,0},{4,6},{6,7},{7,5},{5,4},{8,10},{10,11},{11... | collective-permute-start | bytes 798728 | tf_op jit(solution)/shard_map/ppermute | solution.py:313
  44.2 16.3 %collective-permute-start.13 = (bf16[2048,128]{1,0:T(8,128)(2,1)}, bf16[2048,128]{1,0:T(8,128)(2,1)}, u32[]{:S(2)}, u32[]{:S(2)}) collective-permute-start(bf16[2048,128]{1,0:T(8,128)(2,1)} %collective-permute-done.5.refs_9_.refs_5_), channel_id=1, source_target_pairs={{0,2},{2,3},{3,1},{1,0},{4,6},{6,7},{7,5},{5,4},{8,10},{10,11},{11... | collective-permute-start | bytes 1572872 | tf_op jit(solution)/shard_map/ppermute | solution.py:313
  47.7 5.1 %copy-start.1 = (bf16[3088,128]{1,0:T(8,128)(2,1)}, bf16[3088,128]{1,0:T(8,128)(2,1)S(1)}, u32[]{:S(2)}) copy-start(bf16[3088,128]{1,0:T(8,128)(2,1)S(1)} %collective-permute-done.2.refs_14_.refs_11_) | copy-start | bytes 2371588
  48.5 4.2 %collective-permute-start.12 = (bf16[1552,128]{1,0:T(8,128)(2,1)}, bf16[1552,128]{1,0:T(8,128)(2,1)}, u32[]{:S(2)}, u32[]{:S(2)}) collective-permute-start(bf16[1552,128]{1,0:T(8,128)(2,1)} %slice.25), channel_id=1, source_target_pairs={{0,4},{4,0},{8,12},{12,8},{16,20},{20,16},{24,28},{28,24},{1,5},{5... | collective-permute-start | bytes 1191944 | tf_op jit(solution)/shard_map/ppermute | solution.py:310
  49.9 0.7 %copy-start.8 = (bf16[1040,128]{1,0:T(8,128)(2,1)}, bf16[1040,128]{1,0:T(8,128)(2,1)S(1)}, u32[]{:S(2)}) copy-start(bf16[1040,128]{1,0:T(8,128)(2,1)S(1)} %collective-permute-done.3.refs_3_.refs_7_) | copy-start | bytes 798724
  50.6 2.1 %collective-permute-start.11 = (bf16[1536,128]{1,0:T(8,128)(2,1)}, bf16[1536,128]{1,0:T(8,128)(2,1)}, u32[]{:S(2)}, u32[]{:S(2)}) collective-permute-start(bf16[1536,128]{1,0:T(8,128)(2,1)} %slice.24), channel_id=1, source_target_pairs={{0,4},{4,0},{8,12},{12,8},{16,20},{20,16},{24,28},{28,24},{1,5},{5... | collective-permute-start | bytes 1179656 | tf_op jit(solution)/shard_map/ppermute | solution.py:310

commit v6 on v5

--- a/solution.py
+++ b/solution.py
@@ -12,7 +12,7 @@
 SMEM = pl.BlockSpec(memory_space=pltpu.SMEM)
 VMEM = pl.BlockSpec(memory_space=pltpu.VMEM)
 HBM = pl.BlockSpec(memory_space=pl.ANY)
-UNROLL = 4
+UNROLL = 8
 TAIL = 16
 VMEM_BYTES = 60 * 1024 * 1024
 FIELDS = dict(closes=1, opens=1, result=10, left_row=5, left_buf=5, right_row=5, right_buf=4)
@@ -141,8 +141,7 @@
     numbers[wanted_at : wanted_at + rows, :results] = jnp.where(c_keep[...] > 0, c_cols[...], -2)
     for copy in copies:
         copy.wait()
-    for n in range(len(sources)):
-        numbers[n : n + 1] = tails[n].astype(jnp.float32)[:1].astype(jnp.int32)
+    numbers[: len(sources)] = tails[...].astype(jnp.float32)[:, 0].astype(jnp.int32)
     numbers[lookup_at : lookup_at + 1] = table[:1]
     to_scalars = pltpu.make_async_copy(numbers, scalars, sem.at[0])
     to_scalars.start()

time: 64.1 us -> 63.6 us (level)
  no operation moved by 1% of the time
where the time goes in v6:
time: 63.6 us; the launch traced here: 63.4 us
  waiting for transfers between devices  23.3 us (37%)
  starting transfers between devices  22.7 us (36%)
  Pallas kernels  10.6 us (17%)
  local copies, waits for them, and re-layouts  5.85 us (9%)
  other arithmetic  0.8 us (1%)
    ppermute x6, waiting for transfers between devices, on_device(): step = lambda x: lax.ppermute(x, 'section', pairs)  22.6 us
    ppermute x6, starting transfers between devices, on_device(): step = lambda x: lax.ppermute(x, 'section', pairs)  16.6 us
    pallas_call x1, Pallas kernels, multiply_early(): pl.pallas_call(functools.partial(early_kernel, sizes, len(a_bufs), len(b_...  7.85 us
    ppermute x8, starting transfers between devices, on_device(): lax.ppermute(x, 'rows', [(r, r ^ m) for r in range(n_rows)])  6.02 us
    pallas_call x1, Pallas kernels, multiply_late(): pl.pallas_call(functools.partial(late_kernel, len(a_bufs), len(b_bufs)),...  2.77 us
    unnamed x26, local copies, waits for them, and re-layouts  2.12 us
    slice x2, local copies, waits for them, and re-layouts, on_device(): small, big = ([jnp.concatenate([blocks[:middle], tail])], [blocks[middle:]])  2.04 us
    slice x2, local copies, waits for them, and re-layouts, on_device(): lower, upper = (came[2][:cut], came[2][cut:])  1.67 us
  transfers between devices with their start and end apart: 14, of which 6 were waited for; matrix products, arithmetic and copies ran while one was open for 7% of the time, Pallas kernels for 12%

profile of v6, /device:TPU:0, one launch (start us, length us, event | category | flops | bytes accessed | tf_op | source)
XLA Modules:
  0.0 63.4 jit_solution(5574717684281221356)
XLA Ops:
  0.0 0.7 %convert_bitcast_fusion = bf16[1,12]{1,0:T(2,128)(2,1)S(1)} fusion(s32[12,1]{0,1:T(1,128)} %param.6), kind=kLoop, calls=%fused_computation.2 | loop fusion | flops 12 | bytes 72 | tf_op jit(solution)/shard_map/convert_element_type | solution.py:305
  0.7 1.0 %slice.18 = bf16[4,1,2,128,128]{4,3,2,1,0:T(8,128)(2,1)S(1)} slice(bf16[12,1,2,128,128]{4,3,2,1,0:T(8,128)(2,1)} %param.5), slice={[0:4], [0:1], [0:2], [0:128], [0:128]} | slice | bytes 524288 | tf_op jit(solution)/shard_map/slice | solution.py:315
  1.7 4.1 %collective-permute-start = (bf16[1040,128]{1,0:T(8,128)(2,1)S(1)}, bf16[1040,128]{1,0:T(8,128)(2,1)S(1)}, u32[]{:S(2)}, u32[]{:S(2)}) collective-permute-start(bf16[1040,128]{1,0:T(8,128)(2,1)S(1)} %pad_maximum_fusion.1), channel_id=1, source_target_pairs={{0,2},{2,3},{3,1},{1,0},{4,6},{6,7},{7,5},{5,4},{8,10},{10,11},{11... | collective-permute-start | bytes 798728 | tf_op jit(solution)/shard_map/ppermute | solution.py:312
  5.8 1.1 %slice.21 = bf16[8,1,2,128,128]{4,3,2,1,0:T(8,128)(2,1)S(1)} slice(bf16[12,1,2,128,128]{4,3,2,1,0:T(8,128)(2,1)} %param.5), slice={[4:12], [0:1], [0:2], [0:128], [0:128]} | slice | bytes 1048576 | tf_op jit(solution)/shard_map/slice | solution.py:315
  6.9 1.6 %collective-permute-start.4 = (bf16[2048,128]{1,0:T(8,128)(2,1)S(1)}, bf16[2048,128]{1,0:T(8,128)(2,1)S(1)}, u32[]{:S(2)}, u32[]{:S(2)}) collective-permute-start(bf16[2048,128]{1,0:T(8,128)(2,1)S(1)} %bitcast.7), channel_id=1, source_target_pairs={{0,2},{2,3},{3,1},{1,0},{4,6},{6,7},{7,5},{5,4},{8,10},{10,11},{11... | collective-permute-start | bytes 1572872 | tf_op jit(solution)/shard_map/ppermute | solution.py:312
  8.6 0.1 pad_maximum_fusion.refs_0_.refs_4_.refs_10_.refs_7_
  8.6 1.6 %collective-permute-start.8 = (bf16[3088,128]{1,0:T(8,128)(2,1)S(1)}, bf16[3088,128]{1,0:T(8,128)(2,1)S(1)}, u32[]{:S(2)}, u32[]{:S(2)}) collective-permute-start(bf16[3088,128]{1,0:T(8,128)(2,1)S(1)} %pad_maximum_fusion.refs_0_.refs_4_.refs_10_.refs_7_), channel_id=1, source_target_pairs={{0,16},{4,20},{8,24},{12,28},{16,0},{20,4},{24,8},{28,12},{1,17},{... | collective-permute-start | bytes 2371592 | tf_op jit(solution)/shard_map/ppermute | solution.py:309
  10.2 1.5 %collective-permute-start.7 = (bf16[3088,128]{1,0:T(8,128)(2,1)S(1)}, bf16[3088,128]{1,0:T(8,128)(2,1)S(1)}, u32[]{:S(2)}, u32[]{:S(2)}) collective-permute-start(bf16[3088,128]{1,0:T(8,128)(2,1)S(1)} %pad_maximum_fusion.refs_0_.refs_4_.refs_10_.refs_7_), channel_id=1, source_target_pairs={{0,8},{4,12},{8,0},{12,4},{16,24},{20,28},{24,16},{28,20},{1,9},{5... | collective-permute-start | bytes 2371592 | tf_op jit(solution)/shard_map/ppermute | solution.py:309
  11.7 0.0 collective-permute-start.6
  11.7 0.9 %collective-permute-done.refs_1_.refs_5_ = bf16[1040,128]{1,0:T(8,128)(2,1)S(1)} collective-permute-done((bf16[1040,128]{1,0:T(8,128)(2,1)S(1)}, bf16[1040,128]{1,0:T(8,128)(2,1)S(1)}, u32[]{:S(2)}, u32[]{:S(2)}) %collective-permute-start) | collective-permute-done | bytes 266272 | tf_op jit(solution)/shard_map/ppermute | solution.py:312
  12.6 3.4 %collective-permute-start.1 = (bf16[1040,128]{1,0:T(8,128)(2,1)S(1)}, bf16[1040,128]{1,0:T(8,128)(2,1)S(1)}, u32[]{:S(2)}, u32[]{:S(2)}) collective-permute-start(bf16[1040,128]{1,0:T(8,128)(2,1)S(1)} %collective-permute-done.refs_1_.refs_5_), channel_id=1, source_target_pairs={{0,2},{2,3},{3,1},{1,0},{4,6},{6,7},{7,5},{5,4},{8,10},{10,11},{11... | collective-permute-start | bytes 798728 | tf_op jit(solution)/shard_map/ppermute | solution.py:312
  16.0 7.9 %collective-permute-done.4.refs_8_.refs_4_ = bf16[2048,128]{1,0:T(8,128)(2,1)S(1)} collective-permute-done((bf16[2048,128]{1,0:T(8,128)(2,1)S(1)}, bf16[2048,128]{1,0:T(8,128)(2,1)S(1)}, u32[]{:S(2)}, u32[]{:S(2)}) %collective-permute-start.4) | collective-permute-done | bytes 524320 | tf_op jit(solution)/shard_map/ppermute | solution.py:312
  23.9 2.4 %collective-permute-start.2 = (bf16[3088,128]{1,0:T(8,128)(2,1)S(1)}, bf16[3088,128]{1,0:T(8,128)(2,1)S(1)}, u32[]{:S(2)}, u32[]{:S(2)}) collective-permute-start(bf16[3088,128]{1,0:T(8,128)(2,1)S(1)} %pad_maximum_fusion.refs_0_.refs_4_.refs_10_.refs_7_), channel_id=1, source_target_pairs={{0,24},{4,28},{8,16},{12,20},{16,8},{20,12},{24,0},{28,4},{1,25},{... | collective-permute-start | bytes 2371592 | tf_op jit(solution)/shard_map/ppermute | solution.py:309
  26.3 2.1 %collective-permute-done.1.refs_2_.refs_6_ = bf16[1040,128]{1,0:T(8,128)(2,1)S(1)} collective-permute-done((bf16[1040,128]{1,0:T(8,128)(2,1)S(1)}, bf16[1040,128]{1,0:T(8,128)(2,1)S(1)}, u32[]{:S(2)}, u32[]{:S(2)}) %collective-permute-start.1) | collective-permute-done | bytes 266272 | tf_op jit(solution)/shard_map/ppermute | solution.py:312
  28.4 3.4 %collective-permute-start.5 = (bf16[2048,128]{1,0:T(8,128)(2,1)S(1)}, bf16[2048,128]{1,0:T(8,128)(2,1)}, u32[]{:S(2)}, u32[]{:S(2)}) collective-permute-start(bf16[2048,128]{1,0:T(8,128)(2,1)S(1)} %collective-permute-done.4.refs_8_.refs_4_), channel_id=1, source_target_pairs={{0,2},{2,3},{3,1},{1,0},{4,6},{6,7},{7,5},{5,4},{8,10},{10,11},{11... | collective-permute-start | bytes 1572872 | tf_op jit(solution)/shard_map/ppermute | solution.py:312
  31.8 0.0 collective-permute-done.8.refs_13_.refs_10_
  31.8 0.0 collective-permute-start.10
  31.8 0.0 collective-permute-done.7.refs_12_.refs_9_
  31.8 0.5 collective-permute-start.9
  32.3 0.7 %collective-permute-start.3 = (bf16[1040,128]{1,0:T(8,128)(2,1)S(1)}, bf16[1040,128]{1,0:T(8,128)(2,1)S(1)}, u32[]{:S(2)}, u32[]{:S(2)}) collective-permute-start(bf16[1040,128]{1,0:T(8,128)(2,1)S(1)} %collective-permute-done.1.refs_2_.refs_6_), channel_id=1, source_target_pairs={{0,2},{2,3},{3,1},{1,0},{4,6},{6,7},{7,5},{5,4},{8,10},{10,11},{11... | collective-permute-start | bytes 798728 | tf_op jit(solution)/shard_map/ppermute | solution.py:312
  33.0 11.2 %collective-permute-done.5.refs_9_.refs_5_ = bf16[2048,128]{1,0:T(8,128)(2,1)} collective-permute-done((bf16[2048,128]{1,0:T(8,128)(2,1)S(1)}, bf16[2048,128]{1,0:T(8,128)(2,1)}, u32[]{:S(2)}, u32[]{:S(2)}) %collective-permute-start.5) | collective-permute-done | bytes 524320 | tf_op jit(solution)/shard_map/ppermute | solution.py:312
  44.2 3.5 %collective-permute-start.13 = (bf16[2048,128]{1,0:T(8,128)(2,1)}, bf16[2048,128]{1,0:T(8,128)(2,1)}, u32[]{:S(2)}, u32[]{:S(2)}) collective-permute-start(bf16[2048,128]{1,0:T(8,128)(2,1)} %collective-permute-done.5.refs_9_.refs_5_), channel_id=1, source_target_pairs={{0,2},{2,3},{3,1},{1,0},{4,6},{6,7},{7,5},{5,4},{8,10},{10,11},{11... | collective-permute-start | bytes 1572872 | tf_op jit(solution)/shard_map/ppermute | solution.py:312
  47.7 0.0 collective-permute-done.2.refs_14_.refs_11_
  47.7 0.8 %slice.25 = bf16[1552,128]{1,0:T(8,128)(2,1)} slice(bf16[3088,128]{1,0:T(8,128)(2,1)S(1)} %collective-permute-done.2.refs_14_.refs_11_), slice={[1536:3088], [0:128]} | slice | bytes 794624 | tf_op jit(solution)/shard_map/slice | solution.py:330
  48.5 0.8 %slice.24 = bf16[1536,128]{1,0:T(8,128)(2,1)} slice(bf16[3088,128]{1,0:T(8,128)(2,1)S(1)} %collective-permute-done.2.refs_14_.refs_11_), slice={[0:1536], [0:128]} | slice | bytes 786432 | tf_op jit(solution)/shard_map/slice | solution.py:330
  49.4 0.5 collective-permute-done.3.refs_3_.refs_7_
  49.9 0.7 %copy-done.8 = bf16[1040,128]{1,0:T(8,128)(2,1)} copy-done((bf16[1040,128]{1,0:T(8,128)(2,1)}, bf16[1040,128]{1,0:T(8,128)(2,1)S(1)}, u32[]{:S(2)}) %copy-start.8) | copy-done | bytes 266264
  50.6 0.7 %copy.7.c_cols = s32[12,3]{1,0:T(8,128)} copy(s32[12,3]{0,1:T(4,128)S(1)} %copy-done.10) | data formatting | bytes 288 | tf_op args[2]
  51.3 0.7 %copy.8.c_keep = s32[12,3]{1,0:T(8,128)} copy(s32[12,3]{0,1:T(4,128)S(1)} %copy-done.11) | data formatting | bytes 288 | tf_op args[3]
  52.0 0.7 %collective-permute-done.11.refs_17_.refs_14_ = bf16[1536,128]{1,0:T(8,128)(2,1)} collective-permute-done((bf16[1536,128]{1,0:T(8,128)(2,1)}, bf16[1536,128]{1,0:T(8,128)(2,1)}, u32[]{:S(2)}, u32[]{:S(2)}) %collective-permute-start.11) | collective-permute-done | bytes 393248 | tf_op jit(solution)/shard_map/ppermute | solution.py:309
  52.8 7.9 %shard_map.55 = (bf16[12,3,2,128,128]{4,3,2,1,0:T(8,128)(2,1)}, s32[49]{0:T(128)}) custom-call(s32[32,8,128]{2,1,0:T(8,128)} %constant.5.clone.tables, s32[12,3]{1,0:T(8,128)} %copy.7.c_cols, s32[12,3]{1,0:T(8,128)} %copy.8.c_keep, bf16[3088,128]{1,0:T(8,128)(2,1)} %copy-done, bf16[1040,128]{1,0:T(8,128)(2,1)} %copy-done.6, bf16[1040,128]{1,0:T(8,128)(2,1)} %copy-done.7, ...), custom_call_target="tpu_custom_call" | custom-call | flops 1000 | bytes 1000 | tf_op jit(solution)/shard_map/pallas_call | solution.py:260
  60.6 2.8 %shard_map.56 = bf16[12,3,2,128,128]{4,3,2,1,0:T(8,128)(2,1)} custom-call(s32[49]{0:T(128)} %get-tuple-element.19.codes, bf16[3088,128]{1,0:T(8,128)(2,1)} %copy-done, bf16[1040,128]{1,0:T(8,128)(2,1)} %copy-done.6, bf16[1040,128]{1,0:T(8,128)(2,1)} %copy-done.7, bf16[1040,128]{1,0:T(8,128)(2,1)} %copy-done.8, ...), custom_call_target="tpu_custom_call", output_to_operand_aliasing={{}: (17, {})} | custom-call | tf_op jit(solution)/shard_map/pallas_call | solution.py:286
  (32 shorter events, 0.1 us)
Async XLA Ops:
  0.0 8.5 %copy-start.5 = (bf16[12,1,2,128,128]{4,3,2,1,0:T(8,128)(2,1)S(1)}, bf16[12,1,2,128,128]{4,3,2,1,0:T(8,128)(2,1)}, u32[]{:S(2)}) copy-start(bf16[12,1,2,128,128]{4,3,2,1,0:T(8,128)(2,1)} %param.5) | copy-start | bytes 2359300
  1.7 10.9 %collective-permute-start = (bf16[1040,128]{1,0:T(8,128)(2,1)S(1)}, bf16[1040,128]{1,0:T(8,128)(2,1)S(1)}, u32[]{:S(2)}, u32[]{:S(2)}) collective-permute-start(bf16[1040,128]{1,0:T(8,128)(2,1)S(1)} %pad_maximum_fusion.1), channel_id=1, source_target_pairs={{0,2},{2,3},{3,1},{1,0},{4,6},{6,7},{7,5},{5,4},{8,10},{10,11},{11... | collective-permute-start | bytes 798728 | tf_op jit(solution)/shard_map/ppermute | solution.py:312
  6.9 17.0 %collective-permute-start.4 = (bf16[2048,128]{1,0:T(8,128)(2,1)S(1)}, bf16[2048,128]{1,0:T(8,128)(2,1)S(1)}, u32[]{:S(2)}, u32[]{:S(2)}) collective-permute-start(bf16[2048,128]{1,0:T(8,128)(2,1)S(1)} %bitcast.7), channel_id=1, source_target_pairs={{0,2},{2,3},{3,1},{1,0},{4,6},{6,7},{7,5},{5,4},{8,10},{10,11},{11... | collective-permute-start | bytes 1572872 | tf_op jit(solution)/shard_map/ppermute | solution.py:312
  8.5 42.1 %copy-start.10 = (s32[12,3]{0,1:T(4,128)S(1)}, s32[12,3]{0,1:T(4,128)}, u32[]{:S(2)}) copy-start(s32[12,3]{0,1:T(4,128)} %param.7) | copy-start | bytes 436
  8.6 42.8 %copy-start.11 = (s32[12,3]{0,1:T(4,128)S(1)}, s32[12,3]{0,1:T(4,128)}, u32[]{:S(2)}) copy-start(s32[12,3]{0,1:T(4,128)} %param.8) | copy-start | bytes 436
  8.6 44.1 %copy-start = (bf16[3088,128]{1,0:T(8,128)(2,1)}, bf16[3088,128]{1,0:T(8,128)(2,1)S(1)}, u32[]{:S(2)}) copy-start(bf16[3088,128]{1,0:T(8,128)(2,1)S(1)} %pad_maximum_fusion.refs_0_.refs_4_.refs_10_.refs_7_) | copy-start | bytes 2371588
  8.6 23.2 %collective-permute-start.8 = (bf16[3088,128]{1,0:T(8,128)(2,1)S(1)}, bf16[3088,128]{1,0:T(8,128)(2,1)S(1)}, u32[]{:S(2)}, u32[]{:S(2)}) collective-permute-start(bf16[3088,128]{1,0:T(8,128)(2,1)S(1)} %pad_maximum_fusion.refs_0_.refs_4_.refs_10_.refs_7_), channel_id=1, source_target_pairs={{0,16},{4,20},{8,24},{12,28},{16,0},{20,4},{24,8},{28,12},{1,17},{... | collective-permute-start | bytes 2371592 | tf_op jit(solution)/shard_map/ppermute | solution.py:309
  10.2 21.6 %collective-permute-start.7 = (bf16[3088,128]{1,0:T(8,128)(2,1)S(1)}, bf16[3088,128]{1,0:T(8,128)(2,1)S(1)}, u32[]{:S(2)}, u32[]{:S(2)}) collective-permute-start(bf16[3088,128]{1,0:T(8,128)(2,1)S(1)} %pad_maximum_fusion.refs_0_.refs_4_.refs_10_.refs_7_), channel_id=1, source_target_pairs={{0,8},{4,12},{8,0},{12,4},{16,24},{20,28},{24,16},{28,20},{1,9},{5... | collective-permute-start | bytes 2371592 | tf_op jit(solution)/shard_map/ppermute | solution.py:309
  11.7 20.6 %collective-permute-start.6 = (bf16[3088,128]{1,0:T(8,128)(2,1)S(1)}, bf16[3088,128]{1,0:T(8,128)(2,1)S(1)}, u32[]{:S(2)}, u32[]{:S(2)}) collective-permute-start(bf16[3088,128]{1,0:T(8,128)(2,1)S(1)} %pad_maximum_fusion.refs_0_.refs_4_.refs_10_.refs_7_), channel_id=1, source_target_pairs={{0,4},{4,0},{8,12},{12,8},{16,20},{20,16},{24,28},{28,24},{1,5},{5... | collective-permute-start | bytes 2371592 | tf_op jit(solution)/shard_map/ppermute | solution.py:309
  12.6 40.1 %copy-start.6 = (bf16[1040,128]{1,0:T(8,128)(2,1)}, bf16[1040,128]{1,0:T(8,128)(2,1)S(1)}, u32[]{:S(2)}) copy-start(bf16[1040,128]{1,0:T(8,128)(2,1)S(1)} %collective-permute-done.refs_1_.refs_5_) | copy-start | bytes 798724
  12.6 15.8 %collective-permute-start.1 = (bf16[1040,128]{1,0:T(8,128)(2,1)S(1)}, bf16[1040,128]{1,0:T(8,128)(2,1)S(1)}, u32[]{:S(2)}, u32[]{:S(2)}) collective-permute-start(bf16[1040,128]{1,0:T(8,128)(2,1)S(1)} %collective-permute-done.refs_1_.refs_5_), channel_id=1, source_target_pairs={{0,2},{2,3},{3,1},{1,0},{4,6},{6,7},{7,5},{5,4},{8,10},{10,11},{11... | collective-permute-start | bytes 798728 | tf_op jit(solution)/shard_map/ppermute | solution.py:312
  23.9 26.0 %copy-start.9 = (bf16[2048,128]{1,0:T(8,128)(2,1)}, bf16[2048,128]{1,0:T(8,128)(2,1)S(1)}, u32[]{:S(2)}) copy-start(bf16[2048,128]{1,0:T(8,128)(2,1)S(1)} %collective-permute-done.4.refs_8_.refs_4_) | copy-start | bytes 1572868
  23.9 23.8 %collective-permute-start.2 = (bf16[3088,128]{1,0:T(8,128)(2,1)S(1)}, bf16[3088,128]{1,0:T(8,128)(2,1)S(1)}, u32[]{:S(2)}, u32[]{:S(2)}) collective-permute-start(bf16[3088,128]{1,0:T(8,128)(2,1)S(1)} %pad_maximum_fusion.refs_0_.refs_4_.refs_10_.refs_7_), channel_id=1, source_target_pairs={{0,24},{4,28},{8,16},{12,20},{16,8},{20,12},{24,0},{28,4},{1,25},{... | collective-permute-start | bytes 2371592 | tf_op jit(solution)/shard_map/ppermute | solution.py:309
  28.4 19.3 %copy-start.7 = (bf16[1040,128]{1,0:T(8,128)(2,1)}, bf16[1040,128]{1,0:T(8,128)(2,1)S(1)}, u32[]{:S(2)}) copy-start(bf16[1040,128]{1,0:T(8,128)(2,1)S(1)} %collective-permute-done.1.refs_2_.refs_6_) | copy-start | bytes 798724
  28.4 15.8 %collective-permute-start.5 = (bf16[2048,128]{1,0:T(8,128)(2,1)S(1)}, bf16[2048,128]{1,0:T(8,128)(2,1)}, u32[]{:S(2)}, u32[]{:S(2)}) collective-permute-start(bf16[2048,128]{1,0:T(8,128)(2,1)S(1)} %collective-permute-done.4.refs_8_.refs_4_), channel_id=1, source_target_pairs={{0,2},{2,3},{3,1},{1,0},{4,6},{6,7},{7,5},{5,4},{8,10},{10,11},{11... | collective-permute-start | bytes 1572872 | tf_op jit(solution)/shard_map/ppermute | solution.py:312
  31.8 20.9 %copy-start.2 = (bf16[3088,128]{1,0:T(8,128)(2,1)}, bf16[3088,128]{1,0:T(8,128)(2,1)S(1)}, u32[]{:S(2)}) copy-start(bf16[3088,128]{1,0:T(8,128)(2,1)S(1)} %collective-permute-done.8.refs_13_.refs_10_) | copy-start | bytes 2371588
  31.8 20.9 %collective-permute-start.10 = (bf16[3088,128]{1,0:T(8,128)(2,1)S(1)}, bf16[3088,128]{1,0:T(8,128)(2,1)}, u32[]{:S(2)}, u32[]{:S(2)}) collective-permute-start(bf16[3088,128]{1,0:T(8,128)(2,1)S(1)} %collective-permute-done.8.refs_13_.refs_10_), channel_id=1, source_target_pairs={{0,4},{4,0},{8,12},{12,8},{16,20},{20,16},{24,28},{28,24},{1,5},{5... | collective-permute-start | bytes 2371592 | tf_op jit(solution)/shard_map/ppermute | solution.py:309
  31.8 20.9 %copy-start.3 = (bf16[3088,128]{1,0:T(8,128)(2,1)}, bf16[3088,128]{1,0:T(8,128)(2,1)S(1)}, u32[]{:S(2)}) copy-start(bf16[3088,128]{1,0:T(8,128)(2,1)S(1)} %collective-permute-done.7.refs_12_.refs_9_) | copy-start | bytes 2371588
  31.8 20.9 %collective-permute-start.9 = (bf16[3088,128]{1,0:T(8,128)(2,1)S(1)}, bf16[3088,128]{1,0:T(8,128)(2,1)}, u32[]{:S(2)}, u32[]{:S(2)}) collective-permute-start(bf16[3088,128]{1,0:T(8,128)(2,1)S(1)} %collective-permute-done.7.refs_12_.refs_9_), channel_id=1, source_target_pairs={{0,4},{4,0},{8,12},{12,8},{16,20},{20,16},{24,28},{28,24},{1,5},{5... | collective-permute-start | bytes 2371592 | tf_op jit(solution)/shard_map/ppermute | solution.py:309
  32.3 11.9 %copy-start.4 = (bf16[3088,128]{1,0:T(8,128)(2,1)}, bf16[3088,128]{1,0:T(8,128)(2,1)S(1)}, u32[]{:S(2)}) copy-start(bf16[3088,128]{1,0:T(8,128)(2,1)S(1)} %collective-permute-done.6.refs_11_.refs_8_) | copy-start | bytes 2371588
  32.3 17.6 %collective-permute-start.3 = (bf16[1040,128]{1,0:T(8,128)(2,1)S(1)}, bf16[1040,128]{1,0:T(8,128)(2,1)S(1)}, u32[]{:S(2)}, u32[]{:S(2)}) collective-permute-start(bf16[1040,128]{1,0:T(8,128)(2,1)S(1)} %collective-permute-done.1.refs_2_.refs_6_), channel_id=1, source_target_pairs={{0,2},{2,3},{3,1},{1,0},{4,6},{6,7},{7,5},{5,4},{8,10},{10,11},{11... | collective-permute-start | bytes 798728 | tf_op jit(solution)/shard_map/ppermute | solution.py:312
  44.2 16.4 %collective-permute-start.13 = (bf16[2048,128]{1,0:T(8,128)(2,1)}, bf16[2048,128]{1,0:T(8,128)(2,1)}, u32[]{:S(2)}, u32[]{:S(2)}) collective-permute-start(bf16[2048,128]{1,0:T(8,128)(2,1)} %collective-permute-done.5.refs_9_.refs_5_), channel_id=1, source_target_pairs={{0,2},{2,3},{3,1},{1,0},{4,6},{6,7},{7,5},{5,4},{8,10},{10,11},{11... | collective-permute-start | bytes 1572872 | tf_op jit(solution)/shard_map/ppermute | solution.py:312
  47.7 5.1 %copy-start.1 = (bf16[3088,128]{1,0:T(8,128)(2,1)}, bf16[3088,128]{1,0:T(8,128)(2,1)S(1)}, u32[]{:S(2)}) copy-start(bf16[3088,128]{1,0:T(8,128)(2,1)S(1)} %collective-permute-done.2.refs_14_.refs_11_) | copy-start | bytes 2371588
  48.5 4.2 %collective-permute-start.12 = (bf16[1552,128]{1,0:T(8,128)(2,1)}, bf16[1552,128]{1,0:T(8,128)(2,1)}, u32[]{:S(2)}, u32[]{:S(2)}) collective-permute-start(bf16[1552,128]{1,0:T(8,128)(2,1)} %slice.25), channel_id=1, source_target_pairs={{0,4},{4,0},{8,12},{12,8},{16,20},{20,16},{24,28},{28,24},{1,5},{5... | collective-permute-start | bytes 1191944 | tf_op jit(solution)/shard_map/ppermute | solution.py:309
  49.9 0.7 %copy-start.8 = (bf16[1040,128]{1,0:T(8,128)(2,1)}, bf16[1040,128]{1,0:T(8,128)(2,1)S(1)}, u32[]{:S(2)}) copy-start(bf16[1040,128]{1,0:T(8,128)(2,1)S(1)} %collective-permute-done.3.refs_3_.refs_7_) | copy-start | bytes 798724
  50.6 2.1 %collective-permute-start.11 = (bf16[1536,128]{1,0:T(8,128)(2,1)}, bf16[1536,128]{1,0:T(8,128)(2,1)}, u32[]{:S(2)}, u32[]{:S(2)}) collective-permute-start(bf16[1536,128]{1,0:T(8,128)(2,1)} %slice.24), channel_id=1, source_target_pairs={{0,4},{4,0},{8,12},{12,8},{16,20},{20,16},{24,28},{28,24},{1,5},{5... | collective-permute-start | bytes 1179656 | tf_op jit(solution)/shard_map/ppermute | solution.py:309
